TPU v7x, 256 devices: a whole 4x4x8 slice. The times are simulated.
256 devices in a mesh: grp: 32 (over x, y, core), sp: 8 (over z).
Axes of the slice: x: 4, y: 4, z: 8, core: 2. Of those that a mesh axis runs over, the one named last changes fastest.
Arguments:
- queries: bfloat16 [32768, 2048], P(('grp', 'sp')), may hold values from -170 to 170
- key_rows: bfloat16 [32768, 2048], P(('grp', 'sp')), may hold values from -7 to 7
- value_rows: bfloat16 [32768, 2048], P(('grp', 'sp')), may hold values from -6 to 6
- upstream: bfloat16 [32768, 2048], P(('grp', 'sp')), may hold values from -6 to 6
- neighbours: int32 [256, 8], P('grp'), may hold values from 0 to 255, as said below
- counts: int32 [256], P('grp'), may hold values from 1 to 8, as said below
Outputs:
- attended: bfloat16 [32768, 2048], P(('grp', 'sp'))
- query_grad: bfloat16 [32768, 2048], P(('grp', 'sp'))
- key_grad: bfloat16 [32768, 2048], P(('grp', 'sp'))
- value_grad: bfloat16 [32768, 2048], P(('grp', 'sp'))
Inputs may be any that keep to these rules, and one draw needn't show every extreme that they name: `neighbours`: row b names block b in slot 0 and then distinct blocks of b's group of 8 blocks or of the two groups beside it; slots past counts[b] hold such blocks too and are not used. `counts`: every group of 8 blocks has a block with all 8 slots used.
All inputs are finite; a program needn't handle non-finite values.
Results may differ from a plain program's by a relative error of at most 0.034.
Values may be sent and summed in bfloat16 or wider, within the bound.
No kernel may reach another device: no remote copies, remote signals or barrier semaphores. Data moves between devices by JAX's collectives and lax.ppermute only.
A program may use at most 128 MiB of HBM per device.

v0:
```python
import jax
import jax.numpy as jnp
from jax import lax
from jax.sharding import PartitionSpec as P

H = 16
HD = 128
BLK = 128
NNB = 8


def extended_2(value, sides, width):
    for axis, dim in sides:
        devices, length = (lax.axis_size(axis), value.shape[dim])
        up = [(i, (i + 1) % devices) for i in range(devices - 1)]
        down = [(j, i) for i, j in up]
        last = lax.slice_in_dim(value, length - width, length, axis=dim)
        initial = lax.slice_in_dim(value, 0, width, axis=dim)
        before = lax.ppermute(last, axis, up)
        after = lax.ppermute(initial, axis, down)
        value = jnp.concatenate([before, value, after], axis=dim)
    return value


def passed_along(value, axis, steps):
    count = lax.axis_size(axis)
    initial, last = (max(0, -steps), min(count, count - steps))
    return lax.ppermute(value, axis, [(source, source + steps) for source in range(initial, last)])


def split_tiles(kv_table, slot_ids, heads_dev):
    block_count, slot_count = slot_ids.shape
    block_len = kv_table.shape[1]
    picked = kv_table[slot_ids].reshape(block_count, slot_count * block_len, 2, heads_dev, HD)
    return (picked[:, :, 0], picked[:, :, 1])


def probability_of(query_tile, key_tiles, usable, scaling):
    block_len = query_tile.shape[1]
    scores = (
        jnp.einsum("bqhd,bkhd->bhqk", query_tile, key_tiles, preferred_element_type=jnp.float32)
        * scaling
    )
    allowed = jnp.repeat(usable, block_len, axis=1)
    scores = jnp.where(allowed[:, None, None, :], scores, -1e30)
    highest = jnp.max(scores, axis=-1, keepdims=True)
    raised = jnp.exp(scores - highest)
    return raised / jnp.sum(raised, axis=-1, keepdims=True)


def local(queries, key_rows, value_rows, upstream, neighbours, counts):
    sp_size = lax.axis_size("sp")
    shard_rows = queries.shape[0]
    heads_dev = H // sp_size
    group_tok = shard_rows * sp_size
    group_blocks = group_tok // BLK
    scaling = HD ** (-0.5)
    query_h, key_h, value_h, grad_h = (
        lax.all_to_all(queries, "sp", split_axis=1, concat_axis=0, tiled=True),
        lax.all_to_all(key_rows, "sp", split_axis=1, concat_axis=0, tiled=True),
        lax.all_to_all(value_rows, "sp", split_axis=1, concat_axis=0, tiled=True),
        lax.all_to_all(upstream, "sp", split_axis=1, concat_axis=0, tiled=True),
    )
    joined = jnp.concatenate([key_h, value_h], axis=1)
    extended = extended_2(joined, (("grp", 0),), group_tok)
    kv_table = extended.reshape(3 * group_blocks, BLK, 2 * heads_dev * HD)
    anchor = (lax.axis_index("grp") - 1) * group_blocks
    local_ids = neighbours - anchor
    usable_all = jnp.arange(NNB)[None, :] < counts[:, None]
    per_round = min(group_blocks, max(1, 512 // BLK))
    rounds = group_blocks // per_round
    query_blocks = query_h.reshape(rounds, per_round, BLK, heads_dev, HD)
    slot_table = local_ids.reshape(rounds, per_round, NNB)
    usable_table = usable_all.reshape(rounds, per_round, NNB)

    def forward_round(pieces):
        query_tile, slot_ids, usable = pieces
        key_tiles, value_tiles = split_tiles(kv_table, slot_ids, heads_dev)
        probability = probability_of(query_tile, key_tiles, usable, scaling)
        return jnp.einsum(
            "bhqk,bkhd->bqhd",
            probability.astype(jnp.bfloat16),
            value_tiles,
            preferred_element_type=jnp.float32,
        ).astype(jnp.bfloat16)

    out_blocks = lax.map(forward_round, (query_blocks, slot_table, usable_table))
    out_h = out_blocks.reshape(group_tok, heads_dev * HD)
    row_delta = jnp.sum(
        grad_h.reshape(group_tok, heads_dev, HD).astype(jnp.float32)
        * out_h.reshape(group_tok, heads_dev, HD).astype(jnp.float32),
        axis=-1,
    )
    delta_table = row_delta.reshape(rounds, per_round, BLK, heads_dev)
    grad_blocks = grad_h.reshape(rounds, per_round, BLK, heads_dev, HD)

    def backward_round(grad_table, pieces):
        query_tile, grad_tile, delta_tile, slot_ids, usable = pieces
        key_tiles, value_tiles = split_tiles(kv_table, slot_ids, heads_dev)
        probability = probability_of(query_tile, key_tiles, usable, scaling)
        weights = probability.astype(jnp.bfloat16)
        grad_prob = jnp.einsum(
            "bqhd,bkhd->bhqk", grad_tile, value_tiles, preferred_element_type=jnp.float32
        )
        delta_cols = jnp.transpose(delta_tile, (0, 2, 1))[..., None]
        grad_score = (probability * (grad_prob - delta_cols)).astype(jnp.bfloat16)
        query_part = (
            jnp.einsum("bhqk,bkhd->bqhd", grad_score, key_tiles, preferred_element_type=jnp.float32)
            * scaling
        ).astype(jnp.bfloat16)
        key_part = (
            jnp.einsum(
                "bhqk,bqhd->bkhd", grad_score, query_tile, preferred_element_type=jnp.float32
            )
            * scaling
        )
        value_part = jnp.einsum(
            "bhqk,bqhd->bkhd", weights, grad_tile, preferred_element_type=jnp.float32
        )
        block_count, slot_count = slot_ids.shape
        combined = jnp.concatenate(
            [
                key_part.reshape(block_count, slot_count, BLK, heads_dev * HD),
                value_part.reshape(block_count, slot_count, BLK, heads_dev * HD),
            ],
            axis=-1,
        )
        return (grad_table.at[slot_ids].add(combined), query_part)

    start_table = jnp.zeros((3 * group_blocks, BLK, 2 * heads_dev * HD), jnp.float32)
    grad_table, query_parts = lax.scan(
        backward_round,
        start_table,
        (query_blocks, grad_blocks, delta_table, slot_table, usable_table),
    )
    returned = grad_table.reshape(3, group_tok, 2 * heads_dev * HD)
    from_above = passed_along(returned[0].astype(jnp.bfloat16), "grp", -1)
    from_below = passed_along(returned[2].astype(jnp.bfloat16), "grp", 1)
    summed = (returned[1] + from_above.astype(jnp.float32) + from_below.astype(jnp.float32)).astype(
        jnp.bfloat16
    )
    key_grad_h = summed[:, : heads_dev * HD]
    value_grad_h = summed[:, heads_dev * HD :]
    query_grad_h = query_parts.reshape(group_tok, heads_dev * HD)
    attended, query_grad, key_grad, value_grad = (
        lax.all_to_all(out_h, "sp", split_axis=0, concat_axis=1, tiled=True),
        lax.all_to_all(query_grad_h, "sp", split_axis=0, concat_axis=1, tiled=True),
        lax.all_to_all(key_grad_h, "sp", split_axis=0, concat_axis=1, tiled=True),
        lax.all_to_all(value_grad_h, "sp", split_axis=0, concat_axis=1, tiled=True),
    )
    return (attended, query_grad, key_grad, value_grad)


def solution(mesh):
    return jax.shard_map(
        local,
        mesh=mesh,
        in_specs=(
            P(("grp", "sp"), None),
            P(("grp", "sp"), None),
            P(("grp", "sp"), None),
            P(("grp", "sp"), None),
            P("grp", None),
            P("grp"),
        ),
        out_specs=(
            P(("grp", "sp"), None),
            P(("grp", "sp"), None),
            P(("grp", "sp"), None),
            P(("grp", "sp"), None),
        ),
        check_vma=False,
    )
```

profile of v0, /device:TPU:29, one launch (start us, length us, event | category | flops | bytes accessed | tf_op | source)
XLA Modules:
  0.0 370.2 jit_solution(6007652497970016872)
XLA Ops:
  0.7 2.1 copy.100
  2.8 8.2 %all-to-all-start.2 = ((bf16[128,8,256]{0,2,1:T(8,128)(2,1)}), bf16[128,8,256]{0,2,1:T(8,128)(2,1)S(1)}, u32[]{:S(2)}, u32[]{:S(2)}) async-start(bf16[128,8,256]{0,2,1:T(8,128)(2,1)} %bitcast.28), calls=%async_computation.2 | async-start | bytes 1048576 | tf_op jit(solution)/shard_map/all_to_all | solution.py:59
  11.0 1.3 copy.96
  13.3 15.6 %all-to-all-done.2 = bf16[128,8,256]{0,2,1:T(8,128)(2,1)S(1)} async-done(((bf16[128,8,256]{0,2,1:T(8,128)(2,1)}), bf16[128,8,256]{0,2,1:T(8,128)(2,1)S(1)}, u32[]{:S(2)}, u32[]{:S(2)}) %all-to-all-start.2) | async-done | bytes 524320 | tf_op jit(solution)/shard_map/all_to_all | solution.py:59
  28.9 3.5 all-to-all-start
  32.7 1.0 copy.99
  33.7 16.6 %all-to-all-done = bf16[128,8,256]{2,0,1:T(8,128)(2,1)S(1)} async-done(((bf16[128,8,256]{2,0,1:T(8,128)(2,1)}), bf16[128,8,256]{2,0,1:T(8,128)(2,1)S(1)}, u32[]{:S(2)}, u32[]{:S(2)}) %all-to-all-start) | async-done | bytes 524320 | tf_op jit(solution)/shard_map/all_to_all | solution.py:60
  50.3 3.5 all-to-all-start.1
  54.8 16.9 %all-to-all-done.1 = bf16[128,8,256]{2,0,1:T(8,128)(2,1)S(1)} async-done(((bf16[128,8,256]{2,0,1:T(8,128)(2,1)}), bf16[128,8,256]{2,0,1:T(8,128)(2,1)S(1)}, u32[]{:S(2)}, u32[]{:S(2)}) %all-to-all-start.1) | async-done | bytes 524320 | tf_op jit(solution)/shard_map/all_to_all | solution.py:61
  71.7 3.5 all-to-all-start.4
  75.3 2.4 collective-permute-start.1
  77.7 5.3 %collective-permute-start = (bf16[1024,512]{1,0:T(8,128)(2,1)S(1)}, bf16[1024,512]{1,0:T(8,128)(2,1)}, u32[]{:S(2)}, u32[]{:S(2)}) collective-permute-start(bf16[1024,512]{1,0:T(8,128)(2,1)S(1)} %pad_maximum_fusion.2), channel_id=1, source_target_pairs={{0,8},{8,16},{16,24},{24,32},{32,40},{40,48},{48,56},{56,64},{64,7... | collective-permute-start | bytes 3145736 | tf_op jit(solution)/shard_map/ppermute | solution.py:19
  84.1 8.9 %all-to-all-done.4 = bf16[128,8,256]{0,2,1:T(8,128)(2,1)S(1)} async-done(((bf16[128,8,256]{0,2,1:T(8,128)(2,1)}), bf16[128,8,256]{0,2,1:T(8,128)(2,1)S(1)}, u32[]{:S(2)}, u32[]{:S(2)}) %all-to-all-start.4) | async-done | bytes 524320 | tf_op jit(solution)/shard_map/all_to_all | solution.py:62
  94.6 1.2 reshape.160
  95.8 2.1 pad_maximum_fusion.1
  98.8 60.4 %while.22 = (s32[]{:T(128)}, bf16[2,4,128,2,128]{2,4,3,1,0:T(8,128)(2,1)}, s32[2,4,8]{2,1,0:T(4,128)S(1)}, bf16[24,128,512]{2,1,0:T(8,128)(2,1)S(1)}, pred[2,4,8...) while((s32[]{:T(128)}, bf16[2,4,128,2,128]{2,4,3,1,0:T(8,128)(2,1)}, ...), condition=%wide.region_3.4_spmd, body=%wide.region_0.3_spmd.sunk | while | flops 545392768 | bytes 52982752 | solution.py:87
  99.0 2.8 gather_fusion
  101.8 6.9 %reshape.204 = bf16[4,1024,2,2,128]{4,3,2,1,0:T(2,128)(2,1)} reshape(bf16[32,128,512]{2,1,0:T(8,128)(2,1)} %gather_fusion) | data formatting | bytes 8388608 | tf_op jit(solution)/shard_map/while/body/eval_jaxpr/reshape | solution.py:34
  108.7 5.7 %fusion.79 = (bf16[4,1024,1,2,128]{4,3,2,1,0:T(2,128)(2,1)}, bf16[4,1024,1,2,128]{4,3,2,1,0:T(2,128)(2,1)S(1)}) fusion(bf16[4,1024,2,2,128]{4,3,2,1,0:T(2,128)(2,1)} %reshape.204), kind=kLoop, calls=%fused_computation.79.clone.1 | loop fusion | bytes 8388608 | tf_op jit(solution)/shard_map/while/body/eval_jaxpr/slice | solution.py:35
  115.2 3.4 fusion.81
  118.5 6.2 %copy.164 = bf16[4,1024,1,2,128]{1,4,3,0,2:T(8,128)(2,1)} copy(bf16[4,1024,1,2,128]{4,3,2,1,0:T(2,128)(2,1)} %get-tuple-element.295) | data formatting | bytes 4194304 | tf_op jit(solution)/shard_map/while
  124.7 4.3 %fusion.82 = bf16[2,4,128,2,128]{2,4,3,1,0:T(8,128)(2,1)} fusion(bf16[2,4,128,2,128]{2,4,3,1,0:T(8,128)(2,1)} %get-tuple-element.317, s32[]{:T(128)S(6)} %copy.177, f32[4,2,128,1024]{3,2,1,0:T(8,128)} %get-tuple-element.293, f32[4,2,128]{2,1,0:T(2,128)S(1)} %get-tuple-element.294, bf16[4,1024,1,2,128]{1,4,3,0,2:T(8,128)(2,1)} %copy.164), kind=kOutput, calls=%fused_computation.17.clone.1 | convolution fusion | flops 270663680 | bytes 6557700 | tf_op jit(solution)/shard_map/while/body/eval_jaxpr/bhqk,bkhd->bqhd/dot_general | solution.py:80
  129.2 2.8 gather_fusion
  132.0 6.9 %reshape.204 = bf16[4,1024,2,2,128]{4,3,2,1,0:T(2,128)(2,1)} reshape(bf16[32,128,512]{2,1,0:T(8,128)(2,1)} %gather_fusion) | data formatting | bytes 8388608 | tf_op jit(solution)/shard_map/while/body/eval_jaxpr/reshape | solution.py:34
  138.9 5.7 %fusion.79 = (bf16[4,1024,1,2,128]{4,3,2,1,0:T(2,128)(2,1)}, bf16[4,1024,1,2,128]{4,3,2,1,0:T(2,128)(2,1)S(1)}) fusion(bf16[4,1024,2,2,128]{4,3,2,1,0:T(2,128)(2,1)} %reshape.204), kind=kLoop, calls=%fused_computation.79.clone.1 | loop fusion | bytes 8388608 | tf_op jit(solution)/shard_map/while/body/eval_jaxpr/slice | solution.py:35
  145.4 3.4 fusion.81
  148.7 6.2 %copy.164 = bf16[4,1024,1,2,128]{1,4,3,0,2:T(8,128)(2,1)} copy(bf16[4,1024,1,2,128]{4,3,2,1,0:T(2,128)(2,1)} %get-tuple-element.295) | data formatting | bytes 4194304 | tf_op jit(solution)/shard_map/while
  154.9 4.3 %fusion.82 = bf16[2,4,128,2,128]{2,4,3,1,0:T(8,128)(2,1)} fusion(bf16[2,4,128,2,128]{2,4,3,1,0:T(8,128)(2,1)} %get-tuple-element.317, s32[]{:T(128)S(6)} %copy.177, f32[4,2,128,1024]{3,2,1,0:T(8,128)} %get-tuple-element.293, f32[4,2,128]{2,1,0:T(2,128)S(1)} %get-tuple-element.294, bf16[4,1024,1,2,128]{1,4,3,0,2:T(8,128)(2,1)} %copy.164), kind=kOutput, calls=%fused_computation.17.clone.1 | convolution fusion | flops 270663680 | bytes 6557700 | tf_op jit(solution)/shard_map/while/body/eval_jaxpr/bhqk,bkhd->bqhd/dot_general | solution.py:80
  159.3 2.0 copy.106
  161.3 2.0 copy.122
  163.3 5.4 %all-to-all-start.3 = ((bf16[8,128,256]{2,1,0:T(8,128)(2,1)}), bf16[8,128,256]{2,1,0:T(8,128)(2,1)}, u32[]{:S(2)}, u32[]{:S(2)}) async-start(bf16[8,128,256]{2,1,0:T(8,128)(2,1)} %copy.122), calls=%async_computation.3 | async-start | bytes 1048576 | tf_op jit(solution)/shard_map/all_to_all | solution.py:146
  168.8 2.1 bitcast_convert_fusion
  170.9 2.5 copy.107
  173.4 1.7 multiply_reduce_fusion
  176.0 3.5 broadcast_in_dim.50
  179.4 111.0 %while.23 = (s32[]{:T(128)}, f32[24,128,512]{2,1,0:T(8,128)}, bf16[2,4,128,2,128]{2,4,3,1,0:T(8,128)(2,1)}, s32[2,4,8]{2,1,0:T(4,128)S(1)}, bf16[2,4,128,2,128]{...) while((s32[]{:T(128)}, f32[24,128,512]{2,1,0:T(8,128)}, ...), condition=%wide.region_9.10_spmd, body=%wide.region_5.9_spmd.sunk | while | flops 1360267392 | bytes 152351968 | solution.py:131
  179.7 2.8 gather_fusion.1
  182.4 7.0 %reshape.210 = bf16[4,1024,2,2,128]{4,3,2,1,0:T(2,128)(2,1)} reshape(bf16[32,128,512]{2,1,0:T(8,128)(2,1)} %gather_fusion.1) | data formatting | bytes 8388608 | tf_op jit(solution)/shard_map/while/body/eval_jaxpr/reshape | solution.py:34
  189.4 4.7 %fusion.90 = (bf16[4,1024,1,2,128]{4,3,2,1,0:T(2,128)(2,1)S(1)}, bf16[4,1024,1,2,128]{4,3,2,1,0:T(2,128)(2,1)S(1)}) fusion(bf16[4,1024,2,2,128]{4,3,2,1,0:T(2,128)(2,1)} %reshape.210), kind=kLoop, calls=%fused_computation.81.clone.1 | loop fusion | bytes 8388608 | tf_op jit(solution)/shard_map/while/body/eval_jaxpr/slice | solution.py:35
  194.9 1.7 fusion.92
  196.6 1.1 multiply_convert_fusion.2
  202.3 3.8 %pad_maximum_fusion.4 = f32[4,8,128,512]{2,1,3,0:T(8,128)} fusion(f32[4,8,128,256]{2,1,3,0:T(8,128)S(1)} %bitcast.205, f32[4,8,128,256]{2,1,3,0:T(8,128)S(1)} %bitcast.206), kind=kLoop, calls=%fused_computation.29.clone.1 | loop fusion | flops 2097152 | bytes 16777216 | tf_op jit(solution)/shard_map/while/body/eval_jaxpr/concatenate | solution.py:121
  206.1 10.0 %copy.171 = f32[4,8,128,512]{3,2,1,0:T(8,128)} copy(f32[4,8,128,512]{2,1,3,0:T(8,128)} %pad_maximum_fusion.4) | data formatting | bytes 16777216 | tf_op jit(solution)/shard_map/while/body/eval_jaxpr/concatenate | solution.py:121
  216.1 18.7 %scatter_fusion = f32[24,128,512]{2,1,0:T(8,128)} fusion(f32[24,128,512]{2,1,0:T(8,128)} %get-tuple-element.341, s32[32]{0:T(128)S(1)} %reshape.209, f32[32,128,512]{2,1,0:T(8,128)} %bitcast.202), kind=kCustom, calls=%fused_computation.2.clone.1 | custom fusion | flops 2097152 | bytes 25165952 | tf_op jit(solution)/shard_map/while/body/eval_jaxpr/scatter-add | solution.py:128
  235.1 2.8 gather_fusion.1
  237.8 7.0 %reshape.210 = bf16[4,1024,2,2,128]{4,3,2,1,0:T(2,128)(2,1)} reshape(bf16[32,128,512]{2,1,0:T(8,128)(2,1)} %gather_fusion.1) | data formatting | bytes 8388608 | tf_op jit(solution)/shard_map/while/body/eval_jaxpr/reshape | solution.py:34
  244.8 4.7 %fusion.90 = (bf16[4,1024,1,2,128]{4,3,2,1,0:T(2,128)(2,1)S(1)}, bf16[4,1024,1,2,128]{4,3,2,1,0:T(2,128)(2,1)S(1)}) fusion(bf16[4,1024,2,2,128]{4,3,2,1,0:T(2,128)(2,1)} %reshape.210), kind=kLoop, calls=%fused_computation.81.clone.1 | loop fusion | bytes 8388608 | tf_op jit(solution)/shard_map/while/body/eval_jaxpr/slice | solution.py:35
  250.3 1.7 fusion.92
  252.0 1.1 multiply_convert_fusion.2
  257.8 3.8 %pad_maximum_fusion.4 = f32[4,8,128,512]{2,1,3,0:T(8,128)} fusion(f32[4,8,128,256]{2,1,3,0:T(8,128)S(1)} %bitcast.205, f32[4,8,128,256]{2,1,3,0:T(8,128)S(1)} %bitcast.206), kind=kLoop, calls=%fused_computation.29.clone.1 | loop fusion | flops 2097152 | bytes 16777216 | tf_op jit(solution)/shard_map/while/body/eval_jaxpr/concatenate | solution.py:121
  261.5 10.0 %copy.171 = f32[4,8,128,512]{3,2,1,0:T(8,128)} copy(f32[4,8,128,512]{2,1,3,0:T(8,128)} %pad_maximum_fusion.4) | data formatting | bytes 16777216 | tf_op jit(solution)/shard_map/while/body/eval_jaxpr/concatenate | solution.py:121
  271.5 18.9 %scatter_fusion = f32[24,128,512]{2,1,0:T(8,128)} fusion(f32[24,128,512]{2,1,0:T(8,128)} %get-tuple-element.341, s32[32]{0:T(128)S(1)} %reshape.209, f32[32,128,512]{2,1,0:T(8,128)} %bitcast.202), kind=kCustom, calls=%fused_computation.2.clone.1 | custom fusion | flops 2097152 | bytes 25165952 | tf_op jit(solution)/shard_map/while/body/eval_jaxpr/scatter-add | solution.py:128
  290.4 3.2 convert.6
  293.7 1.5 fusion.55
  295.2 7.0 %collective-permute-start.3 = (bf16[1024,512]{1,0:T(8,128)(2,1)}, bf16[1024,512]{1,0:T(8,128)(2,1)S(1)}, u32[]{:S(2)}, u32[]{:S(2)}) collective-permute-start(bf16[1024,512]{1,0:T(8,128)(2,1)} %bitcast.45), channel_id=1, source_target_pairs={{0,8},{8,16},{16,24},{24,32},{32,40},{40,48},{48,56},{56,64},{64,7... | collective-permute-start | bytes 3145736 | tf_op jit(solution)/shard_map/ppermute | solution.py:28
  302.3 1.9 collective-permute-start.2
  305.2 6.9 %all-to-all-start.5 = ((bf16[8,128,256]{2,1,0:T(8,128)(2,1)}), bf16[8,128,256]{2,1,0:T(8,128)(2,1)S(1)}, u32[]{:S(2)}, u32[]{:S(2)}) async-start(bf16[8,128,256]{2,1,0:T(8,128)(2,1)} %copy.123), calls=%async_computation.5 | async-start | bytes 1048576 | tf_op jit(solution)/shard_map/all_to_all | solution.py:147
  312.1 1.8 slice.32
  314.3 6.7 %collective-permute-done.2 = bf16[1024,512]{1,0:T(8,128)(2,1)S(1)} collective-permute-done((bf16[1024,512]{1,0:T(8,128)(2,1)}, bf16[1024,512]{1,0:T(8,128)(2,1)S(1)}, u32[]{:S(2)}, u32[]{:S(2)}) %collective-permute-start.2) | collective-permute-done | bytes 1048608 | tf_op jit(solution)/shard_map/ppermute | solution.py:28
  322.3 4.8 %all-to-all-done.5 = bf16[8,128,256]{2,1,0:T(8,128)(2,1)S(1)} async-done(((bf16[8,128,256]{2,1,0:T(8,128)(2,1)}), bf16[8,128,256]{2,1,0:T(8,128)(2,1)S(1)}, u32[]{:S(2)}, u32[]{:S(2)}) %all-to-all-start.5) | async-done | bytes 524320 | tf_op jit(solution)/shard_map/all_to_all | solution.py:147
  327.1 20.4 %all_to_all.146 = bf16[8,128,256]{2,1,0:T(8,128)(2,1)S(1)} all-to-all(bf16[8,128,256]{2,1,0:T(8,128)(2,1)S(1)} %bitcast.224), channel_id=1, replica_groups=mesh['grp'=32,'sp'=8] {'sp'}, dimensions={0} | all-to-all | bytes 1048576 | tf_op jit(solution)/shard_map/all_to_all | solution.py:148
  347.6 3.5 all-to-all-start.7
  351.1 1.3 copy.103
  356.0 13.0 %all-to-all-done.7 = bf16[8,128,256]{2,1,0:T(8,128)(2,1)S(1)} async-done(((bf16[8,128,256]{2,1,0:T(8,128)(2,1)}), bf16[8,128,256]{2,1,0:T(8,128)(2,1)S(1)}, u32[]{:S(2)}, u32[]{:S(2)}) %all-to-all-start.7) | async-done | bytes 524320 | tf_op jit(solution)/shard_map/all_to_all | solution.py:149
  (102 shorter events, 27.2 us)
Async XLA Ops:
  0.6 31.8 %copy-start.9 = (bf16[128,2048]{1,0:T(8,128)(2,1)S(1)}, bf16[128,2048]{1,0:T(8,128)(2,1)}, u32[]{:S(2)}) copy-start(bf16[128,2048]{1,0:T(8,128)(2,1)} %param.12) | copy-start | bytes 1572868
  0.6 53.2 %copy-start.10 = (bf16[128,2048]{1,0:T(8,128)(2,1)S(1)}, bf16[128,2048]{1,0:T(8,128)(2,1)}, u32[]{:S(2)}) copy-start(bf16[128,2048]{1,0:T(8,128)(2,1)} %param.13) | copy-start | bytes 1572868
  2.8 26.1 %all-to-all-start.2 = ((bf16[128,8,256]{0,2,1:T(8,128)(2,1)}), bf16[128,8,256]{0,2,1:T(8,128)(2,1)S(1)}, u32[]{:S(2)}, u32[]{:S(2)}) async-start(bf16[128,8,256]{0,2,1:T(8,128)(2,1)} %bitcast.28), calls=%async_computation.2 | async-start | bytes 1048576 | tf_op jit(solution)/shard_map/all_to_all | solution.py:59
  13.3 69.7 %copy-start.12 = (s32[8]{0:T(128)S(1)}, s32[8]{0:T(128)}, u32[]{:S(2)}) copy-start(s32[8]{0:T(128)} %param.15) | copy-start | bytes 100
  13.3 69.8 %copy-start.11 = (s32[8,8]{1,0:T(8,128)S(1)}, s32[8,8]{1,0:T(8,128)}, u32[]{:S(2)}) copy-start(s32[8,8]{1,0:T(8,128)} %param.14) | copy-start | bytes 772
  28.9 21.4 %all-to-all-start = ((bf16[128,8,256]{2,0,1:T(8,128)(2,1)}), bf16[128,8,256]{2,0,1:T(8,128)(2,1)S(1)}, u32[]{:S(2)}, u32[]{:S(2)}) async-start(bf16[128,8,256]{2,0,1:T(8,128)(2,1)} %copy.97), calls=%async_computation | async-start | bytes 1048576 | tf_op jit(solution)/shard_map/all_to_all | solution.py:60
  50.3 44.2 %copy-start.2 = (bf16[128,8,256]{2,0,1:T(8,128)(2,1)}, bf16[128,8,256]{2,0,1:T(8,128)(2,1)S(1)}, u32[]{:S(2)}) copy-start(bf16[128,8,256]{2,0,1:T(8,128)(2,1)S(1)} %all-to-all-done) | copy-start | bytes 1572868
  50.3 21.4 %all-to-all-start.1 = ((bf16[128,8,256]{2,0,1:T(8,128)(2,1)}), bf16[128,8,256]{2,0,1:T(8,128)(2,1)S(1)}, u32[]{:S(2)}, u32[]{:S(2)}) async-start(bf16[128,8,256]{2,0,1:T(8,128)(2,1)} %copy.99), calls=%async_computation.1 | async-start | bytes 1048576 | tf_op jit(solution)/shard_map/all_to_all | solution.py:61
  71.7 24.1 %copy-start.3 = (bf16[128,8,256]{2,0,1:T(8,128)(2,1)}, bf16[128,8,256]{2,0,1:T(8,128)(2,1)S(1)}, u32[]{:S(2)}) copy-start(bf16[128,8,256]{2,0,1:T(8,128)(2,1)S(1)} %all-to-all-done.1) | copy-start | bytes 1572868
  71.7 21.4 %all-to-all-start.4 = ((bf16[128,8,256]{0,2,1:T(8,128)(2,1)}), bf16[128,8,256]{0,2,1:T(8,128)(2,1)S(1)}, u32[]{:S(2)}, u32[]{:S(2)}) async-start(bf16[128,8,256]{0,2,1:T(8,128)(2,1)} %bitcast.35), calls=%async_computation.4 | async-start | bytes 1048576 | tf_op jit(solution)/shard_map/all_to_all | solution.py:62
  75.3 20.5 %collective-permute-start.1 = (bf16[1024,512]{1,0:T(8,128)(2,1)S(1)}, bf16[1024,512]{1,0:T(8,128)(2,1)}, u32[]{:S(2)}, u32[]{:S(2)}) collective-permute-start(bf16[1024,512]{1,0:T(8,128)(2,1)S(1)} %pad_maximum_fusion.2), channel_id=1, source_target_pairs={{8,0},{16,8},{24,16},{32,24},{40,32},{48,40},{56,48},{64,56},{72,6... | collective-permute-start | bytes 3145736 | tf_op jit(solution)/shard_map/ppermute | solution.py:20
  77.7 18.1 %collective-permute-start = (bf16[1024,512]{1,0:T(8,128)(2,1)S(1)}, bf16[1024,512]{1,0:T(8,128)(2,1)}, u32[]{:S(2)}, u32[]{:S(2)}) collective-permute-start(bf16[1024,512]{1,0:T(8,128)(2,1)S(1)} %pad_maximum_fusion.2), channel_id=1, source_target_pairs={{0,8},{8,16},{16,24},{24,32},{32,40},{40,48},{48,56},{56,64},{64,7... | collective-permute-start | bytes 3145736 | tf_op jit(solution)/shard_map/ppermute | solution.py:19
  93.1 0.8 copy-start.4
  108.7 5.7 %copy-start = (bf16[2,4,128,2,128]{4,2,3,1,0:T(8,128)(2,1)S(1)}, bf16[2,4,128,2,128]{4,2,3,1,0:T(8,128)(2,1)}, u32[]{:S(2)}) copy-start(bf16[2,4,128,2,128]{4,2,3,1,0:T(8,128)(2,1)} %get-tuple-element.328) | copy-start | bytes 1572868 | tf_op jit(solution)/shard_map/while
  138.9 5.7 %copy-start = (bf16[2,4,128,2,128]{4,2,3,1,0:T(8,128)(2,1)S(1)}, bf16[2,4,128,2,128]{4,2,3,1,0:T(8,128)(2,1)}, u32[]{:S(2)}) copy-start(bf16[2,4,128,2,128]{4,2,3,1,0:T(8,128)(2,1)} %get-tuple-element.328) | copy-start | bytes 1572868 | tf_op jit(solution)/shard_map/while
  163.3 141.9 %all-to-all-start.3 = ((bf16[8,128,256]{2,1,0:T(8,128)(2,1)}), bf16[8,128,256]{2,1,0:T(8,128)(2,1)}, u32[]{:S(2)}, u32[]{:S(2)}) async-start(bf16[8,128,256]{2,1,0:T(8,128)(2,1)} %copy.122), calls=%async_computation.3 | async-start | bytes 1048576 | tf_op jit(solution)/shard_map/all_to_all | solution.py:146
  189.4 4.7 %copy-start.1 = (bf16[2,4,128,2,128]{4,2,3,1,0:T(8,128)(2,1)S(1)}, bf16[2,4,128,2,128]{4,2,3,1,0:T(8,128)(2,1)}, u32[]{:S(2)}) copy-start(bf16[2,4,128,2,128]{4,2,3,1,0:T(8,128)(2,1)} %get-tuple-element.354) | copy-start | bytes 1572868 | tf_op jit(solution)/shard_map/while
  194.8 1.7 copy-start.5
  196.6 1.2 copy-start.6
  198.7 0.8 copy-start.7
  244.8 4.7 %copy-start.1 = (bf16[2,4,128,2,128]{4,2,3,1,0:T(8,128)(2,1)S(1)}, bf16[2,4,128,2,128]{4,2,3,1,0:T(8,128)(2,1)}, u32[]{:S(2)}) copy-start(bf16[2,4,128,2,128]{4,2,3,1,0:T(8,128)(2,1)} %get-tuple-element.354) | copy-start | bytes 1572868 | tf_op jit(solution)/shard_map/while
  250.3 1.7 copy-start.5
  252.0 1.2 copy-start.6
  254.1 0.8 copy-start.7
  293.7 10.5 %copy-start.8 = (bf16[2,4,128,2,128]{2,4,3,1,0:T(8,128)(2,1)S(1)}, bf16[2,4,128,2,128]{2,4,3,1,0:T(8,128)(2,1)}, u32[]{:S(2)}) copy-start(bf16[2,4,128,2,128]{2,4,3,1,0:T(8,128)(2,1)} %get-tuple-element.85) | copy-start | bytes 1572868
  295.2 19.1 %collective-permute-start.3 = (bf16[1024,512]{1,0:T(8,128)(2,1)}, bf16[1024,512]{1,0:T(8,128)(2,1)S(1)}, u32[]{:S(2)}, u32[]{:S(2)}) collective-permute-start(bf16[1024,512]{1,0:T(8,128)(2,1)} %bitcast.45), channel_id=1, source_target_pairs={{0,8},{8,16},{16,24},{24,32},{32,40},{40,48},{48,56},{56,64},{64,7... | collective-permute-start | bytes 3145736 | tf_op jit(solution)/shard_map/ppermute | solution.py:28
  302.3 18.7 %collective-permute-start.2 = (bf16[1024,512]{1,0:T(8,128)(2,1)}, bf16[1024,512]{1,0:T(8,128)(2,1)S(1)}, u32[]{:S(2)}, u32[]{:S(2)}) collective-permute-start(bf16[1024,512]{1,0:T(8,128)(2,1)} %bitcast.44), channel_id=1, source_target_pairs={{8,0},{16,8},{24,16},{32,24},{40,32},{48,40},{56,48},{64,56},{72,6... | collective-permute-start | bytes 3145736 | tf_op jit(solution)/shard_map/ppermute | solution.py:28
  305.2 21.9 %all-to-all-start.5 = ((bf16[8,128,256]{2,1,0:T(8,128)(2,1)}), bf16[8,128,256]{2,1,0:T(8,128)(2,1)S(1)}, u32[]{:S(2)}, u32[]{:S(2)}) async-start(bf16[8,128,256]{2,1,0:T(8,128)(2,1)} %copy.123), calls=%async_computation.5 | async-start | bytes 1048576 | tf_op jit(solution)/shard_map/all_to_all | solution.py:147
  347.6 21.4 %all-to-all-start.7 = ((bf16[8,128,256]{2,1,0:T(8,128)(2,1)}), bf16[8,128,256]{2,1,0:T(8,128)(2,1)S(1)}, u32[]{:S(2)}, u32[]{:S(2)}) async-start(bf16[8,128,256]{2,1,0:T(8,128)(2,1)} %bitcast.49), calls=%async_computation.7 | async-start | bytes 1048576 | tf_op jit(solution)/shard_map/all_to_all | solution.py:149
where the time goes:
time: 373 us; the launch traced here: 370 us
  local copies, waits for them, and re-layouts  131 us (35%)
  waiting for transfers between devices  82.8 us (22%)
  other arithmetic  65.1 us (17%)
  starting transfers between devices  51.1 us (14%)
  blocking collectives  20.4 us (5%)
  matrix products  18.9 us (5%)
    scatter-add x2, other arithmetic, backward_round(): return (grad_table.at[slot_ids].add(combined), query_part)  37.6 us
    reshape x4, local copies, waits for them, and re-layouts, split_tiles(): kv_table[slot_ids]  27.7 us
    slice x4, local copies, waits for them, and re-layouts, split_tiles(): return (picked[:, :, 0], picked[:, :, 1])  20.9 us
    all_to_all x1, blocking collectives, local(): lax.all_to_all(key_grad_h, 'sp', split_axis=0, concat_axis=1, tiled=True)  20.4 us
    concatenate x2, local copies, waits for them, and re-layouts, backward_round(): jnp.concatenate([key_part.reshape(block_count, slot_count, BLK, heads_dev...  20 us
    all_to_all x1, waiting for transfers between devices, local(): lax.all_to_all(value_rows, 'sp', split_axis=1, concat_axis=0, tiled=True)  16.9 us
    while x34, local copies, waits for them, and re-layouts  16.8 us
    all_to_all x1, waiting for transfers between devices, local(): lax.all_to_all(key_rows, 'sp', split_axis=1, concat_axis=0, tiled=True)  16.6 us
  transfers between devices with their start and end apart: 11, of which 8 were waited for; matrix products, arithmetic and copies ran while one was open for 39% of the time, Pallas kernels for 0%

commit v1 on v0

v1 whole, which is shorter than its diff:
```python
import functools

import jax
import jax.numpy as jnp
from jax import lax
from jax.experimental import pallas as pl
from jax.experimental.pallas import tpu as pltpu
from jax.sharding import PartitionSpec as P

H = 16
HD = 128
BLK = 128
NNB = 8
SCALE = HD ** (-0.5)
LOG2E = 1.4426950408889634
NT = (((1,), (1,)), ((), ()))
NN = (((1,), (0,)), ((), ()))
TN = (((0,), (0,)), ((), ()))
F32 = jnp.float32
BF16 = jnp.bfloat16
ANY = pl.BlockSpec(memory_space=pl.ANY)
SMEM = pl.BlockSpec(memory_space=pltpu.SMEM)
VMEM = pl.BlockSpec(memory_space=pltpu.VMEM)
LIMIT = 48 * 1024 * 1024


def dot(a, b, dims):
    return lax.dot_general(a, b, dims, preferred_element_type=F32)


def run_copies(copies):
    for copy in copies:
        copy.start()
    for copy in copies:
        copy.wait()


def pack_kernel(phase, heads_dev, sp, *refs):
    sources, out, sems = refs[:4], refs[4], refs[5]
    copies = []
    for i, source in enumerate(sources):
        for j in range(sp):
            head = j * heads_dev + phase
            copies.append(
                pltpu.make_async_copy(
                    source.at[:, pl.ds(head * HD, HD)], out.at[j, i], sems.at[i, j]
                )
            )
    run_copies(copies)


def pack(arrays, phase, heads_dev, sp):
    rows = arrays[0].shape[0]
    return pl.pallas_call(
        functools.partial(pack_kernel, phase, heads_dev, sp),
        out_shape=jax.ShapeDtypeStruct((sp, 4, rows, HD), BF16),
        in_specs=[ANY] * 4,
        out_specs=ANY,
        scratch_shapes=[pltpu.SemaphoreType.DMA((4, sp))],
        name="pack",
    )(*arrays)


def unpack_kernel(phase, heads_dev, sp, received, *refs):
    outs, sems = refs[-5:-1], refs[-1]
    copies = []
    for i, out in enumerate(outs):
        for j in range(sp):
            head = j * heads_dev + phase
            copies.append(
                pltpu.make_async_copy(
                    received.at[j, i], out.at[:, pl.ds(head * HD, HD)], sems.at[i, j]
                )
            )
    run_copies(copies)


def unpack(received, held, phase, heads_dev, sp):
    rows = received.shape[2]
    shape = jax.ShapeDtypeStruct((rows, sp * heads_dev * HD), BF16)
    return pl.pallas_call(
        functools.partial(unpack_kernel, phase, heads_dev, sp),
        out_shape=[shape] * 4,
        in_specs=[ANY] * (1 + len(held)),
        out_specs=[ANY] * 4,
        input_output_aliases={1 + i: i for i in range(len(held))},
        scratch_shapes=[pltpu.SemaphoreType.DMA((4, sp))],
        name="unpack",
    )(received, *held)


def attn_kernel(
    nb, ids, counts, own, before, after, main, grad_own, grad_before, grad_after,
    keys, values, key_acc, value_acc, sems,
):
    copies = []
    for i, table in enumerate((keys, values)):
        for g, source in enumerate((before.at[:, i], own.at[:, i], after.at[:, i])):
            copies.append(
                pltpu.make_async_copy(source, table.at[pl.ds(g * nb, nb)], sems.at[i, g])
            )
    for copy in copies:
        copy.start()
    key_acc[...] = jnp.zeros_like(key_acc)
    value_acc[...] = jnp.zeros_like(value_acc)
    for copy in copies:
        copy.wait()

    def block(b, carry):
        count = counts[b]
        query = own[b, 2]
        grad = own[b, 3]
        slots = [ids[b, j] for j in range(NNB)]
        key_cat = jnp.concatenate([keys[s] for s in slots], axis=0)
        value_cat = jnp.concatenate([values[s] for s in slots], axis=0)
        raw = dot(query, key_cat, NT)
        slot_of = lax.broadcasted_iota(jnp.int32, (1, NNB * BLK), 1) // BLK
        raw = jnp.where(slot_of < count, raw, -1e30)
        highest = jnp.max(raw, axis=1, keepdims=True)
        raised = jnp.exp2((raw - highest) * (SCALE * LOG2E))
        total = jnp.sum(raised, axis=1, keepdims=True)
        prob = raised * (1.0 / total)
        weights = prob.astype(BF16)
        attended = dot(weights, value_cat, NN).astype(BF16)
        delta = jnp.sum(grad.astype(F32) * attended.astype(F32), axis=1, keepdims=True)
        grad_prob = dot(grad, value_cat, NT)
        score = (prob * (grad_prob - delta)).astype(BF16)
        main[b, 0] = attended
        main[b, 1] = (dot(score, key_cat, NN) * SCALE).astype(BF16)
        key_part = dot(score, query, TN)
        value_part = dot(weights, grad, TN)
        for j, s in enumerate(slots):
            key_acc[s] += key_part[j * BLK:(j + 1) * BLK]
            value_acc[s] += value_part[j * BLK:(j + 1) * BLK]
        return carry

    lax.fori_loop(0, nb, block, 0)
    for g, (out, kind) in enumerate(((grad_before, BF16), (grad_own, F32), (grad_after, BF16))):
        out[:, 0] = (key_acc[g * nb:(g + 1) * nb] * SCALE).astype(kind)
        out[:, 1] = value_acc[g * nb:(g + 1) * nb].astype(kind)


def attention(ids, counts, own, before, after):
    nb = own.shape[0]
    pair = (nb, 2, BLK, HD)
    return pl.pallas_call(
        functools.partial(attn_kernel, nb),
        out_shape=[
            jax.ShapeDtypeStruct(pair, BF16),
            jax.ShapeDtypeStruct(pair, F32),
            jax.ShapeDtypeStruct(pair, BF16),
            jax.ShapeDtypeStruct(pair, BF16),
        ],
        in_specs=[SMEM, SMEM, VMEM, ANY, ANY],
        out_specs=[VMEM] * 4,
        scratch_shapes=[
            pltpu.VMEM((3 * nb, BLK, HD), BF16),
            pltpu.VMEM((3 * nb, BLK, HD), BF16),
            pltpu.VMEM((3 * nb, BLK, HD), F32),
            pltpu.VMEM((3 * nb, BLK, HD), F32),
            pltpu.SemaphoreType.DMA((2, 3)),
        ],
        compiler_params=pltpu.CompilerParams(vmem_limit_bytes=LIMIT),
        cost_estimate=pl.CostEstimate(
            flops=12 * nb * NNB * BLK * BLK * HD,
            bytes_accessed=6 * 1024 * 1024,
            transcendentals=nb * NNB * BLK * BLK,
        ),
        name="attention",
    )(ids, counts, own, before, after)


def settle_kernel(main, grad_own, from_above, from_below, out):
    out[:, :2] = main[...]
    out[:, 2:] = (
        grad_own[...] + from_above[...].astype(F32) + from_below[...].astype(F32)
    ).astype(BF16)


def settle(main, grad_own, from_above, from_below):
    nb = main.shape[0]
    return pl.pallas_call(
        settle_kernel,
        out_shape=jax.ShapeDtypeStruct((nb, 4, BLK, HD), BF16),
        in_specs=[VMEM] * 4,
        out_specs=VMEM,
        compiler_params=pltpu.CompilerParams(vmem_limit_bytes=LIMIT),
        name="settle",
    )(main, grad_own, from_above, from_below)


def passed_along(value, axis, steps):
    count = lax.axis_size(axis)
    initial, last = (max(0, -steps), min(count, count - steps))
    return lax.ppermute(value, axis, [(source, source + steps) for source in range(initial, last)])


def exchange(value):
    return lax.all_to_all(value, "sp", split_axis=0, concat_axis=0, tiled=True)


def local(queries, key_rows, value_rows, upstream, neighbours, counts):
    sp = lax.axis_size("sp")
    heads_dev = H // sp
    nb = queries.shape[0] * sp // BLK
    ids = neighbours - (lax.axis_index("grp") - 1) * nb
    arrays = (key_rows, value_rows, queries, upstream)
    owned = [exchange(pack(arrays, phase, heads_dev, sp)) for phase in range(heads_dev)]
    outs = ()
    for phase, own in enumerate(owned):
        tables = own[:, :2]
        before = passed_along(tables, "grp", 1)
        after = passed_along(tables, "grp", -1)
        main, grad_own, grad_before, grad_after = attention(ids, counts, own, before, after)
        from_above = passed_along(grad_before, "grp", -1)
        from_below = passed_along(grad_after, "grp", 1)
        sent = exchange(settle(main, grad_own, from_above, from_below))
        outs = unpack(sent, outs, phase, heads_dev, sp)
    return tuple(outs)


def solution(mesh):
    rows = P(("grp", "sp"), None)
    return jax.shard_map(
        local,
        mesh=mesh,
        in_specs=(rows, rows, rows, rows, P("grp", None), P("grp")),
        out_specs=(rows, rows, rows, rows),
        check_vma=False,
    )
```

time: 373 us -> 248 us (0.66)
  Pallas kernels: 0 us -> 154 us
  local copies, waits for them, and re-layouts: 131 us -> 3.51 us
  other arithmetic: 65.1 us -> 0.01 us
  waiting for transfers between devices: 82.8 us -> 24 us
  blocking collectives: 20.4 us -> 0 us
  matrix products: 18.9 us -> 0 us
  starting transfers between devices: 51.1 us -> 61.5 us
    pallas_call x0 -> x8, Pallas kernels: none -> 154 us  [the longest x2 66.3 us: pack(): pl.pallas_call(functools.partial(pack_kernel, phase, heads_dev, sp), out_...]
    all_to_all x7 -> x4, waiting for transfers between devices: 75.7 us -> 0.01 us  [exchange(): return lax.all_to_all(value, 'sp', split_axis=0, concat_axis=0, tiled=True)]
    scatter-add x2 -> x0, other arithmetic: 37.6 us -> none  [backward_round(): return (grad_table.at[slot_ids].add(combined), query_part)]
    reshape x4 -> x0, local copies, waits for them, and re-layouts: 27.7 us -> none  [split_tiles(): kv_table[slot_ids]]
    slice x7 -> x2, local copies, waits for them, and re-layouts: 25.1 us -> 0.86 us  [local(): tables = own[:, :2]]
    ppermute x2 -> x8, starting transfers between devices: 8.95 us -> 33.1 us  [passed_along(): lax.ppermute(value, axis, [(source, source + steps) for source in range(i...]
    all_to_all x1 -> x0, blocking collectives: 20.4 us -> none  [local(): lax.all_to_all(key_grad_h, 'sp', split_axis=0, concat_axis=1, tiled=True)]
    concatenate x2 -> x0, local copies, waits for them, and re-layouts: 20 us -> none  [backward_round(): jnp.concatenate([key_part.reshape(block_count, slot_count, BLK, heads_dev...]
  transfers between devices with their start and end apart: 11 -> 12, of which waited for: 8 -> 8; matrix products, arithmetic and copies ran while one was open for 39% -> 0% of each run, Pallas kernels for 0% -> 36%
where the time goes in v1:
time: 248 us; the launch traced here: 243 us
  Pallas kernels  154 us (62%)
  starting transfers between devices  61.5 us (25%)
  waiting for transfers between devices  24 us (10%)
  local copies, waits for them, and re-layouts  3.51 us (1%)
    pallas_call x2, Pallas kernels, pack(): pl.pallas_call(functools.partial(pack_kernel, phase, heads_dev, sp), out_...  66.3 us
    pallas_call x2, Pallas kernels, unpack(): pl.pallas_call(functools.partial(unpack_kernel, phase, heads_dev, sp), ou...  66.3 us
    ppermute x8, starting transfers between devices, passed_along(): lax.ppermute(value, axis, [(source, source + steps) for source in range(i...  33.1 us
    all_to_all x4, starting transfers between devices, exchange(): return lax.all_to_all(value, 'sp', split_axis=0, concat_axis=0, tiled=True)  28.4 us
    ppermute x8, waiting for transfers between devices, passed_along(): lax.ppermute(value, axis, [(source, source + steps) for source in range(i...  24 us
    pallas_call x2, Pallas kernels, attention(): pl.pallas_call(functools.partial(attn_kernel, nb), out_shape=[jax.ShapeDt...  18.6 us
  transfers between devices with their start and end apart: 12, of which 8 were waited for; matrix products, arithmetic and copies ran while one was open for 0% of the time, Pallas kernels for 36%

profile of v1, /device:TPU:29, one launch (start us, length us, event | category | flops | bytes accessed | tf_op | source)
XLA Modules:
  0.0 243.4 jit_solution(8125960102067921750)
XLA Ops:
  0.6 33.2 %pack.3 = bf16[8,4,128,128]{3,2,1,0:T(8,128)(2,1)} custom-call(bf16[128,2048]{1,0:T(8,128)(2,1)} %refs_0_.3, bf16[128,2048]{1,0:T(8,128)(2,1)} %refs_1_.3, bf16[128,2048]{1,0:T(8,128)(2,1)} %refs_2_.3, bf16[128,2048]{1,0:T(8,128)(2,1)} %refs_3_.3), custom_call_target="tpu_custom_call" | custom-call | tf_op jit(solution)/shard_map/pack/pallas_call | solution.py:54
  33.8 8.2 %all-to-all-start.2 = ((bf16[8,4,128,128]{3,2,1,0:T(8,128)(2,1)}), bf16[8,4,128,128]{3,2,1,0:T(8,128)(2,1)S(1)}, u32[]{:S(2)}, u32[]{:S(2)}) async-start(bf16[8,4,128,128]{3,2,1,0:T(8,128)(2,1)} %pack.3), calls=%async_computation.2 | async-start | bytes 2097152 | tf_op jit(solution)/shard_map/all_to_all | solution.py:199
  42.0 33.1 %pack.2 = bf16[8,4,128,128]{3,2,1,0:T(8,128)(2,1)} custom-call(bf16[128,2048]{1,0:T(8,128)(2,1)} %refs_0_.3, bf16[128,2048]{1,0:T(8,128)(2,1)} %refs_1_.3, bf16[128,2048]{1,0:T(8,128)(2,1)} %refs_2_.3, bf16[128,2048]{1,0:T(8,128)(2,1)} %refs_3_.3), custom_call_target="tpu_custom_call" | custom-call | tf_op jit(solution)/shard_map/pack/pallas_call | solution.py:54
  75.1 0.0 all-to-all-done.2.own
  75.2 6.7 %all-to-all-start = ((bf16[8,4,128,128]{3,2,1,0:T(8,128)(2,1)}), bf16[8,4,128,128]{3,2,1,0:T(8,128)(2,1)S(1)}, u32[]{:S(2)}, u32[]{:S(2)}) async-start(bf16[8,4,128,128]{3,2,1,0:T(8,128)(2,1)} %pack.2), calls=%async_computation | async-start | bytes 2097152 | tf_op jit(solution)/shard_map/all_to_all | solution.py:199
  81.8 0.8 slice.9
  82.6 3.4 %collective-permute-start.5 = (bf16[8,2,128,128]{3,2,1,0:T(8,128)(2,1)}, bf16[8,2,128,128]{3,2,1,0:T(8,128)(2,1)S(1)}, u32[]{:S(2)}, u32[]{:S(2)}) collective-permute-start(bf16[8,2,128,128]{3,2,1,0:T(8,128)(2,1)} %slice.9), channel_id=1, source_target_pairs={{8,0},{16,8},{24,16},{32,24},{40,32},{48,40},{56,48},{64,56},{72,6... | collective-permute-start | bytes 1572872 | tf_op jit(solution)/shard_map/ppermute | solution.py:195
  86.1 4.2 %collective-permute-start.4 = (bf16[8,2,128,128]{3,2,1,0:T(8,128)(2,1)}, bf16[8,2,128,128]{3,2,1,0:T(8,128)(2,1)S(1)}, u32[]{:S(2)}, u32[]{:S(2)}) collective-permute-start(bf16[8,2,128,128]{3,2,1,0:T(8,128)(2,1)} %slice.9), channel_id=1, source_target_pairs={{0,8},{8,16},{16,24},{24,32},{32,40},{40,48},{48,56},{56,64},{64,7... | collective-permute-start | bytes 1572872 | tf_op jit(solution)/shard_map/ppermute | solution.py:195
  90.3 0.0 copy-start.3
  90.3 0.7 copy-done.3
  91.0 0.0 copy-start
  91.0 4.7 %collective-permute-done.5.after = bf16[8,2,128,128]{3,2,1,0:T(8,128)(2,1)S(1)} collective-permute-done((bf16[8,2,128,128]{3,2,1,0:T(8,128)(2,1)}, bf16[8,2,128,128]{3,2,1,0:T(8,128)(2,1)S(1)}, u32[]{:S(2)}, u32[]{:S(2)}) %collective-permute-start.5) | collective-permute-done | bytes 524320 | tf_op jit(solution)/shard_map/ppermute | solution.py:195
  95.7 1.0 collective-permute-done.4.before
  96.7 0.0 copy-done
  96.7 9.3 %attention.3 = (bf16[8,2,128,128]{3,2,1,0:T(8,128)(2,1)S(1)}, f32[8,2,128,128]{3,2,1,0:T(8,128)S(1)}, bf16[8,2,128,128]{3,2,1,0:T(8,128)(2,1)S(1)}, bf16[8,2,128,128]{3,2,1,0:T(8,128)(2,1)S(1)}) custom-call(s32[8,8]{1,0:T(8,128)S(1)} %broadcast_subtract_fusion.ids, s32[8]{0:T(128)S(1)} %copy-done, bf16[8,4,128,128]{3,2,1,0:T(8,128)(2,1)S(1)} %all-to-all-done.2.own, ...), custom_call_target="tpu_custom_call" | custom-call | flops 1610612736 | bytes 6291456 | tf_op jit(solution)/shard_map/attention/pallas_call | solution.py:146
  106.1 2.0 collective-permute-start.6
  108.0 6.4 %collective-permute-start.7 = (bf16[8,2,128,128]{3,2,1,0:T(8,128)(2,1)S(1)}, bf16[8,2,128,128]{3,2,1,0:T(8,128)(2,1)S(1)}, u32[]{:S(2)}, u32[]{:S(2)}) collective-permute-start(bf16[8,2,128,128]{3,2,1,0:T(8,128)(2,1)S(1)} %get-tuple-element.23), channel_id=1, source_target_pairs={{0,8},{8,16},{16,24},{24,32},{32,40},{40,48},{48,56},{56,64},{64,7... | collective-permute-start | bytes 1572872 | tf_op jit(solution)/shard_map/ppermute | solution.py:195
  114.4 4.9 %collective-permute-done.6.from_above = bf16[8,2,128,128]{3,2,1,0:T(8,128)(2,1)S(1)} collective-permute-done((bf16[8,2,128,128]{3,2,1,0:T(8,128)(2,1)S(1)}, bf16[8,2,128,128]{3,2,1,0:T(8,128)(2,1)S(1)}, u32[]{:S(2)}, u32[]{:S(2)}) %collective-permute-start.6) | collective-permute-done | bytes 524320 | tf_op jit(solution)/shard_map/ppermute | solution.py:195
  119.3 1.2 collective-permute-done.7.from_below
  120.5 1.2 settle.3
  121.7 0.0 all-to-all-done.own
  121.7 6.7 %all-to-all-start.3 = ((bf16[8,4,128,128]{3,2,1,0:T(8,128)(2,1)}), bf16[8,4,128,128]{3,2,1,0:T(8,128)(2,1)S(1)}, u32[]{:S(2)}, u32[]{:S(2)}) async-start(bf16[8,4,128,128]{3,2,1,0:T(8,128)(2,1)} %settle.3), calls=%async_computation.3 | async-start | bytes 2097152 | tf_op jit(solution)/shard_map/all_to_all | solution.py:199
  128.4 1.9 collective-permute-start.1
  130.3 6.8 %collective-permute-start = (bf16[8,2,128,128]{3,2,1,0:T(8,128)(2,1)S(1)}, bf16[8,2,128,128]{3,2,1,0:T(8,128)(2,1)S(1)}, u32[]{:S(2)}, u32[]{:S(2)}) collective-permute-start(bf16[8,2,128,128]{3,2,1,0:T(8,128)(2,1)S(1)} %slice.8), channel_id=1, source_target_pairs={{0,8},{8,16},{16,24},{24,32},{32,40},{40,48},{48,56},{56,64},{64,7... | collective-permute-start | bytes 1572872 | tf_op jit(solution)/shard_map/ppermute | solution.py:195
  137.1 5.2 %collective-permute-done.1.after = bf16[8,2,128,128]{3,2,1,0:T(8,128)(2,1)S(1)} collective-permute-done((bf16[8,2,128,128]{3,2,1,0:T(8,128)(2,1)S(1)}, bf16[8,2,128,128]{3,2,1,0:T(8,128)(2,1)S(1)}, u32[]{:S(2)}, u32[]{:S(2)}) %collective-permute-start.1) | collective-permute-done | bytes 524320 | tf_op jit(solution)/shard_map/ppermute | solution.py:195
  142.3 0.9 collective-permute-done.before
  143.2 9.3 %attention.2 = (bf16[8,2,128,128]{3,2,1,0:T(8,128)(2,1)S(1)}, f32[8,2,128,128]{3,2,1,0:T(8,128)S(1)}, bf16[8,2,128,128]{3,2,1,0:T(8,128)(2,1)S(1)}, bf16[8,2,128,128]{3,2,1,0:T(8,128)(2,1)S(1)}) custom-call(s32[8,8]{1,0:T(8,128)S(1)} %broadcast_subtract_fusion.ids, s32[8]{0:T(128)S(1)} %copy-done, bf16[8,4,128,128]{3,2,1,0:T(8,128)(2,1)S(1)} %all-to-all-done.own, ...), custom_call_target="tpu_custom_call" | custom-call | flops 1610612736 | bytes 6291456 | tf_op jit(solution)/shard_map/attention/pallas_call | solution.py:146
  152.5 1.9 collective-permute-start.2
  154.4 6.5 %collective-permute-start.3 = (bf16[8,2,128,128]{3,2,1,0:T(8,128)(2,1)S(1)}, bf16[8,2,128,128]{3,2,1,0:T(8,128)(2,1)S(1)}, u32[]{:S(2)}, u32[]{:S(2)}) collective-permute-start(bf16[8,2,128,128]{3,2,1,0:T(8,128)(2,1)S(1)} %get-tuple-element.19), channel_id=1, source_target_pairs={{0,8},{8,16},{16,24},{24,32},{32,40},{40,48},{48,56},{56,64},{64,7... | collective-permute-start | bytes 1572872 | tf_op jit(solution)/shard_map/ppermute | solution.py:195
  160.9 4.9 %collective-permute-done.2.from_above = bf16[8,2,128,128]{3,2,1,0:T(8,128)(2,1)S(1)} collective-permute-done((bf16[8,2,128,128]{3,2,1,0:T(8,128)(2,1)S(1)}, bf16[8,2,128,128]{3,2,1,0:T(8,128)(2,1)S(1)}, u32[]{:S(2)}, u32[]{:S(2)}) %collective-permute-start.2) | collective-permute-done | bytes 524320 | tf_op jit(solution)/shard_map/ppermute | solution.py:195
  165.8 1.2 collective-permute-done.3.from_below
  167.0 1.2 settle.2
  168.2 0.0 all-to-all-done.3.received
  168.2 0.0 copy-start.2
  168.2 1.0 copy-done.2
  169.2 6.9 %all-to-all-start.1 = ((bf16[8,4,128,128]{3,2,1,0:T(8,128)(2,1)}), bf16[8,4,128,128]{3,2,1,0:T(8,128)(2,1)S(1)}, u32[]{:S(2)}, u32[]{:S(2)}) async-start(bf16[8,4,128,128]{3,2,1,0:T(8,128)(2,1)} %settle.2), calls=%async_computation.1 | async-start | bytes 2097152 | tf_op jit(solution)/shard_map/all_to_all | solution.py:199
  176.1 33.1 %unpack.2 = (bf16[128,2048]{1,0:T(8,128)(2,1)}, bf16[128,2048]{1,0:T(8,128)(2,1)}, bf16[128,2048]{1,0:T(8,128)(2,1)}, bf16[128,2048]{1,0:T(8,128)(2,1)}) custom-call(bf16[8,4,128,128]{3,2,1,0:T(8,128)(2,1)} %copy-done.2), custom_call_target="tpu_custom_call" | custom-call | tf_op jit(solution)/shard_map/unpack/pallas_call | solution.py:81
  209.3 0.0 all-to-all-done.1.received
  209.3 0.0 copy-start.1
  209.3 1.0 copy-done.1
  210.3 33.1 %unpack.3 = (bf16[128,2048]{1,0:T(8,128)(2,1)}, bf16[128,2048]{1,0:T(8,128)(2,1)}, bf16[128,2048]{1,0:T(8,128)(2,1)}, bf16[128,2048]{1,0:T(8,128)(2,1)}) custom-call(bf16[8,4,128,128]{3,2,1,0:T(8,128)(2,1)} %copy-done.1, bf16[128,2048]{1,0:T(8,128)(2,1)} %get-tuple-element.24.refs_0_, ...), custom_call_target="tpu_custom_call", output_to_operand_aliasing={{0}: (1, {}), {1}: (2, {}), {2}: (3, {}), {3}: (4, {})} | custom-call | tf_op jit(solution)/shard_map/unpack/pallas_call | solution.py:81
  (2 shorter events, 0.0 us)
Async XLA Ops:
  33.8 41.4 %all-to-all-start.2 = ((bf16[8,4,128,128]{3,2,1,0:T(8,128)(2,1)}), bf16[8,4,128,128]{3,2,1,0:T(8,128)(2,1)S(1)}, u32[]{:S(2)}, u32[]{:S(2)}) async-start(bf16[8,4,128,128]{3,2,1,0:T(8,128)(2,1)} %pack.3), calls=%async_computation.2 | async-start | bytes 2097152 | tf_op jit(solution)/shard_map/all_to_all | solution.py:199
  75.2 46.5 %all-to-all-start = ((bf16[8,4,128,128]{3,2,1,0:T(8,128)(2,1)}), bf16[8,4,128,128]{3,2,1,0:T(8,128)(2,1)S(1)}, u32[]{:S(2)}, u32[]{:S(2)}) async-start(bf16[8,4,128,128]{3,2,1,0:T(8,128)(2,1)} %pack.2), calls=%async_computation | async-start | bytes 2097152 | tf_op jit(solution)/shard_map/all_to_all | solution.py:199
  82.6 13.1 %collective-permute-start.5 = (bf16[8,2,128,128]{3,2,1,0:T(8,128)(2,1)}, bf16[8,2,128,128]{3,2,1,0:T(8,128)(2,1)S(1)}, u32[]{:S(2)}, u32[]{:S(2)}) collective-permute-start(bf16[8,2,128,128]{3,2,1,0:T(8,128)(2,1)} %slice.9), channel_id=1, source_target_pairs={{8,0},{16,8},{24,16},{32,24},{40,32},{48,40},{56,48},{64,56},{72,6... | collective-permute-start | bytes 1572872 | tf_op jit(solution)/shard_map/ppermute | solution.py:195
  86.1 10.7 %collective-permute-start.4 = (bf16[8,2,128,128]{3,2,1,0:T(8,128)(2,1)}, bf16[8,2,128,128]{3,2,1,0:T(8,128)(2,1)S(1)}, u32[]{:S(2)}, u32[]{:S(2)}) collective-permute-start(bf16[8,2,128,128]{3,2,1,0:T(8,128)(2,1)} %slice.9), channel_id=1, source_target_pairs={{0,8},{8,16},{16,24},{24,32},{32,40},{40,48},{48,56},{56,64},{64,7... | collective-permute-start | bytes 1572872 | tf_op jit(solution)/shard_map/ppermute | solution.py:195
  90.3 0.7 copy-start.3
  91.0 5.7 %copy-start = (s32[8]{0:T(128)S(1)}, s32[8]{0:T(128)}, u32[]{:S(2)}) copy-start(s32[8]{0:T(128)} %counts.3) | copy-start | bytes 100
  106.1 13.2 %collective-permute-start.6 = (bf16[8,2,128,128]{3,2,1,0:T(8,128)(2,1)S(1)}, bf16[8,2,128,128]{3,2,1,0:T(8,128)(2,1)S(1)}, u32[]{:S(2)}, u32[]{:S(2)}) collective-permute-start(bf16[8,2,128,128]{3,2,1,0:T(8,128)(2,1)S(1)} %get-tuple-element.22), channel_id=1, source_target_pairs={{8,0},{16,8},{24,16},{32,24},{40,32},{48,40},{56,48},{64,56},{72,6... | collective-permute-start | bytes 1572872 | tf_op jit(solution)/shard_map/ppermute | solution.py:195
  108.0 12.5 %collective-permute-start.7 = (bf16[8,2,128,128]{3,2,1,0:T(8,128)(2,1)S(1)}, bf16[8,2,128,128]{3,2,1,0:T(8,128)(2,1)S(1)}, u32[]{:S(2)}, u32[]{:S(2)}) collective-permute-start(bf16[8,2,128,128]{3,2,1,0:T(8,128)(2,1)S(1)} %get-tuple-element.23), channel_id=1, source_target_pairs={{0,8},{8,16},{16,24},{24,32},{32,40},{40,48},{48,56},{56,64},{64,7... | collective-permute-start | bytes 1572872 | tf_op jit(solution)/shard_map/ppermute | solution.py:195
  121.7 46.5 %all-to-all-start.3 = ((bf16[8,4,128,128]{3,2,1,0:T(8,128)(2,1)}), bf16[8,4,128,128]{3,2,1,0:T(8,128)(2,1)S(1)}, u32[]{:S(2)}, u32[]{:S(2)}) async-start(bf16[8,4,128,128]{3,2,1,0:T(8,128)(2,1)} %settle.3), calls=%async_computation.3 | async-start | bytes 2097152 | tf_op jit(solution)/shard_map/all_to_all | solution.py:199
  128.4 13.9 %collective-permute-start.1 = (bf16[8,2,128,128]{3,2,1,0:T(8,128)(2,1)S(1)}, bf16[8,2,128,128]{3,2,1,0:T(8,128)(2,1)S(1)}, u32[]{:S(2)}, u32[]{:S(2)}) collective-permute-start(bf16[8,2,128,128]{3,2,1,0:T(8,128)(2,1)S(1)} %slice.8), channel_id=1, source_target_pairs={{8,0},{16,8},{24,16},{32,24},{40,32},{48,40},{56,48},{64,56},{72,6... | collective-permute-start | bytes 1572872 | tf_op jit(solution)/shard_map/ppermute | solution.py:195
  130.3 12.9 %collective-permute-start = (bf16[8,2,128,128]{3,2,1,0:T(8,128)(2,1)S(1)}, bf16[8,2,128,128]{3,2,1,0:T(8,128)(2,1)S(1)}, u32[]{:S(2)}, u32[]{:S(2)}) collective-permute-start(bf16[8,2,128,128]{3,2,1,0:T(8,128)(2,1)S(1)} %slice.8), channel_id=1, source_target_pairs={{0,8},{8,16},{16,24},{24,32},{32,40},{40,48},{48,56},{56,64},{64,7... | collective-permute-start | bytes 1572872 | tf_op jit(solution)/shard_map/ppermute | solution.py:195
  152.5 13.4 %collective-permute-start.2 = (bf16[8,2,128,128]{3,2,1,0:T(8,128)(2,1)S(1)}, bf16[8,2,128,128]{3,2,1,0:T(8,128)(2,1)S(1)}, u32[]{:S(2)}, u32[]{:S(2)}) collective-permute-start(bf16[8,2,128,128]{3,2,1,0:T(8,128)(2,1)S(1)} %get-tuple-element.18), channel_id=1, source_target_pairs={{8,0},{16,8},{24,16},{32,24},{40,32},{48,40},{56,48},{64,56},{72,6... | collective-permute-start | bytes 1572872 | tf_op jit(solution)/shard_map/ppermute | solution.py:195
  154.4 12.6 %collective-permute-start.3 = (bf16[8,2,128,128]{3,2,1,0:T(8,128)(2,1)S(1)}, bf16[8,2,128,128]{3,2,1,0:T(8,128)(2,1)S(1)}, u32[]{:S(2)}, u32[]{:S(2)}) collective-permute-start(bf16[8,2,128,128]{3,2,1,0:T(8,128)(2,1)S(1)} %get-tuple-element.19), channel_id=1, source_target_pairs={{0,8},{8,16},{16,24},{24,32},{32,40},{40,48},{48,56},{56,64},{64,7... | collective-permute-start | bytes 1572872 | tf_op jit(solution)/shard_map/ppermute | solution.py:195
  168.2 1.0 copy-start.2
  169.2 40.1 %all-to-all-start.1 = ((bf16[8,4,128,128]{3,2,1,0:T(8,128)(2,1)}), bf16[8,4,128,128]{3,2,1,0:T(8,128)(2,1)S(1)}, u32[]{:S(2)}, u32[]{:S(2)}) async-start(bf16[8,4,128,128]{3,2,1,0:T(8,128)(2,1)} %settle.2), calls=%async_computation.1 | async-start | bytes 2097152 | tf_op jit(solution)/shard_map/all_to_all | solution.py:199
  209.3 1.0 copy-start.1

commit v2 on v1

v2 whole, which is shorter than its diff:
```python
import functools

import jax
import jax.numpy as jnp
from jax import lax
from jax.experimental import pallas as pl
from jax.experimental.pallas import tpu as pltpu
from jax.sharding import PartitionSpec as P

H = 16
HD = 128
BLK = 128
NNB = 8
PAIR = 8
SCALE = HD ** (-0.5)
LOG2E = 1.4426950408889634
NT = (((1,), (1,)), ((), ()))
NN = (((1,), (0,)), ((), ()))
TN = (((0,), (0,)), ((), ()))
F32 = jnp.float32
BF16 = jnp.bfloat16
ANY = pl.BlockSpec(memory_space=pltpu.HBM)
SMEM = pl.BlockSpec(memory_space=pltpu.SMEM)
VMEM = pl.BlockSpec(memory_space=pltpu.VMEM)
LIMIT = 28 * 1024 * 1024


def dot(a, b, dims):
    return lax.dot_general(a, b, dims, preferred_element_type=F32)


def run_copies(copies):
    for copy in copies:
        copy.start()
    for copy in copies:
        copy.wait()


def pack_kernel(spots, *refs):
    place, sources = refs[0], refs[1:3]
    outs, sems = refs[3:-1], refs[-1]
    n = len(outs)
    copies = []
    for d, out in enumerate(outs):
        owner = lax.rem(place[0] + d, n)
        for i, source in enumerate(sources):
            for h in range(spots):
                column = pl.multiple_of((owner * spots + h) * HD, HD)
                copies.append(
                    pltpu.make_async_copy(
                        source.at[:, pl.ds(column, HD)], out.at[h, i], sems.at[d, i, h]
                    )
                )
    run_copies(copies)


def pack(place, first, second, spots):
    rows, width = first.shape
    n = width // (spots * HD)
    return pl.pallas_call(
        functools.partial(pack_kernel, spots),
        out_shape=[jax.ShapeDtypeStruct((spots, 2, rows, HD), BF16)] * n,
        in_specs=[SMEM, ANY, ANY],
        out_specs=[VMEM] * n,
        scratch_shapes=[pltpu.SemaphoreType.DMA((n, 2, spots))],
        name="pack",
    )(place, first, second)


def unpack_kernel(spots, n, place, *refs):
    received, outs, sems = refs[:n], refs[n:n + 2], refs[-1]
    copies = []
    for r, value in enumerate(received):
        source = lax.rem(place[0] + r, n)
        for i, out in enumerate(outs):
            for h in range(spots):
                column = pl.multiple_of((source * spots + h) * HD, HD)
                copies.append(
                    pltpu.make_async_copy(
                        value.at[h, i], out.at[:, pl.ds(column, HD)], sems.at[r, i, h]
                    )
                )
    run_copies(copies)


def unpack(place, received):
    n = len(received)
    spots, _, rows, _ = received[0].shape
    return pl.pallas_call(
        functools.partial(unpack_kernel, spots, n),
        out_shape=[jax.ShapeDtypeStruct((rows, n * spots * HD), BF16)] * 2,
        in_specs=[SMEM] + [VMEM] * n,
        out_specs=[ANY] * 2,
        scratch_shapes=[pltpu.SemaphoreType.DMA((n, 2, spots))],
        name="unpack",
    )(place, *received)


def join_kernel(*refs):
    out, sems = refs[-2], refs[-1]
    run_copies(
        [pltpu.make_async_copy(x, out.at[r], sems.at[r]) for r, x in enumerate(refs[:-2])]
    )


def join(parts):
    n = len(parts)
    return pl.pallas_call(
        join_kernel,
        out_shape=jax.ShapeDtypeStruct((n, *parts[0].shape), BF16),
        in_specs=[ANY] * n,
        out_specs=VMEM,
        scratch_shapes=[pltpu.SemaphoreType.DMA((n,))],
        name="join",
    )(*parts)


def stack_kernel(spots, *refs):
    sources, out, sems = refs[:2], refs[2], refs[3]
    copies = []
    for j in range(out.shape[0]):
        for i, source in enumerate(sources):
            for h in range(spots):
                copies.append(
                    pltpu.make_async_copy(
                        source.at[:, pl.ds((j * spots + h) * HD, HD)],
                        out.at[j, h, i],
                        sems.at[j, i, h],
                    )
                )
    run_copies(copies)


def stack(first, second, spots):
    rows, width = first.shape
    n = width // (spots * HD)
    return pl.pallas_call(
        functools.partial(stack_kernel, spots),
        out_shape=jax.ShapeDtypeStruct((n, spots, 2, rows, HD), BF16),
        in_specs=[ANY] * 2,
        out_specs=VMEM,
        scratch_shapes=[pltpu.SemaphoreType.DMA((n, 2, spots))],
        name="stack",
    )(first, second)


def unstack_kernel(spots, value, first, second, sems):
    copies = []
    for j in range(value.shape[0]):
        for i, out in enumerate((first, second)):
            for h in range(spots):
                copies.append(
                    pltpu.make_async_copy(
                        value.at[j, h, i],
                        out.at[:, pl.ds((j * spots + h) * HD, HD)],
                        sems.at[j, i, h],
                    )
                )
    run_copies(copies)


def unstack(value):
    n, spots, _, rows, _ = value.shape
    return pl.pallas_call(
        functools.partial(unstack_kernel, spots),
        out_shape=[jax.ShapeDtypeStruct((rows, n * spots * HD), BF16)] * 2,
        in_specs=[VMEM],
        out_specs=[ANY] * 2,
        scratch_shapes=[pltpu.SemaphoreType.DMA((n, 2, spots))],
        name="unstack",
    )(value)


def join_kernel(*refs):
    out, sems = refs[-2], refs[-1]
    run_copies(
        [pltpu.make_async_copy(x, out.at[r], sems.at[r]) for r, x in enumerate(refs[:-2])]
    )


def join(parts):
    n = len(parts)
    return pl.pallas_call(
        join_kernel,
        out_shape=jax.ShapeDtypeStruct((n, *parts[0].shape), BF16),
        in_specs=[ANY] * n,
        out_specs=VMEM,
        scratch_shapes=[pltpu.SemaphoreType.DMA((n,))],
        name="join",
    )(*parts)


def attn_kernel(
    spots, nb, place, ids, counts, chip, own, link, rows,
    main_out, grad_chip, grad_own, grad_link, cache, acc, main, edge, soft, sems,
):
    here, offset, odd = place[0], place[1], place[2]
    chip_at = 2 * nb * (1 - odd)
    link_at = 2 * nb * odd
    copies = []
    for g, (x, at) in enumerate(((chip, chip_at), (own, nb), (link, link_at))):
        copies.append(pltpu.make_async_copy(x, cache.at[pl.ds(at, nb)], sems.at[g]))
    for copy in copies:
        copy.start()
    acc[...] = jnp.zeros_like(acc)
    for copy in copies:
        copy.wait()

    wide = PAIR * BLK

    def block(b, carry):
        used = counts[b]
        slots = []
        for j in range(NNB):
            local_id = ids[b, j] - offset
            side = local_id // nb
            slots.append(side * nb + lax.rem(here - (local_id - side * nb) + nb, nb))
        heads = range(spots)
        chunks = range(NNB // PAIR)
        lane_slot = lax.broadcasted_iota(jnp.int32, (1, wide), 1) // BLK

        def tile(h, i, c):
            return jnp.concatenate(
                [cache[s, h, i] for s in slots[c * PAIR:(c + 1) * PAIR]], axis=0
            )

        def span(c):
            return slice(c * wide, (c + 1) * wide)

        def add(h, i, c, part):
            for j, s in enumerate(slots[c * PAIR:(c + 1) * PAIR]):
                acc[s, h, i] += part[j * BLK:(j + 1) * BLK]

        queries = [rows[b, h, 0] for h in heads]
        grads = [rows[b, h, 1] for h in heads]
        highest, inverse, delta = [], [], []
        for h in heads:
            top = None
            for c in chunks:
                raw = dot(queries[h], tile(h, 0, c), NT)
                raw = jnp.where(lane_slot + c * PAIR < used, raw, -1e30)
                soft[h, :, span(c)] = raw
                top = raw if top is None else jnp.maximum(top, raw)
            highest.append(jnp.max(top, axis=1, keepdims=True))
        for h in heads:
            total = None
            for c in chunks:
                raised = jnp.exp2((soft[h, :, span(c)] - highest[h]) * (SCALE * LOG2E))
                soft[h, :, span(c)] = raised
                total = raised if total is None else total + raised
            inverse.append(1.0 / jnp.sum(total, axis=1, keepdims=True))
        for h in heads:
            out = None
            for c in chunks:
                weights = (soft[h, :, span(c)] * inverse[h]).astype(BF16)
                part = dot(weights, tile(h, 1, c), NN)
                out = part if out is None else out + part
                add(h, 1, c, dot(weights, grads[h], TN))
            attended = out.astype(BF16)
            main[b, h, 0] = attended
            delta.append(
                jnp.sum(grads[h].astype(F32) * attended.astype(F32), axis=1, keepdims=True)
            )
        for h in heads:
            out = None
            for c in chunks:
                grad_prob = dot(grads[h], tile(h, 1, c), NT)
                prob = soft[h, :, span(c)] * inverse[h]
                score = (prob * (grad_prob - delta[h])).astype(BF16)
                part = dot(score, tile(h, 0, c), NN)
                out = part if out is None else out + part
                add(h, 0, c, dot(score, queries[h], TN))
            main[b, h, 1] = (out * SCALE).astype(BF16)
        pltpu.make_async_copy(main.at[b], main_out.at[b], sems.at[3 + b]).start()
        return carry

    lax.fori_loop(0, nb, block, 0)
    copies = [
        pltpu.make_async_copy(main.at[b], main_out.at[b], sems.at[3 + b]) for b in range(nb)
    ]
    for i, (at, out) in enumerate(((link_at, grad_link), (chip_at, grad_chip))):
        part = pl.ds(at, nb)
        edge[i, :, :, 0] = (acc[part, :, 0] * SCALE).astype(BF16)
        edge[i, :, :, 1] = acc[part, :, 1].astype(BF16)
        copies.append(pltpu.make_async_copy(edge.at[i], out, sems.at[i]))
        copies[-1].start()
    copies.append(pltpu.make_async_copy(acc.at[pl.ds(nb, nb)], grad_own, sems.at[2]))
    copies[-1].start()
    for copy in copies:
        copy.wait()


def attention(place, ids, counts, rows, tables):
    shape = tables[0].shape
    nb, spots = shape[:2]
    whole = (3 * nb, *shape[1:])
    return pl.pallas_call(
        functools.partial(attn_kernel, spots, nb),
        out_shape=[jax.ShapeDtypeStruct(shape, kind) for kind in (BF16, BF16, F32, BF16)],
        in_specs=[SMEM] * 3 + [VMEM] * 4,
        out_specs=[ANY] * 4,
        scratch_shapes=[
            pltpu.VMEM(whole, BF16),
            pltpu.VMEM(whole, F32),
            pltpu.VMEM(shape, BF16),
            pltpu.VMEM((2, *shape), BF16),
            pltpu.VMEM((spots, BLK, NNB * BLK), F32),
            pltpu.SemaphoreType.DMA((3 + nb,)),
        ],
        compiler_params=pltpu.CompilerParams(vmem_limit_bytes=59 * 1024 * 1024),
        cost_estimate=pl.CostEstimate(
            flops=12 * spots * nb * NNB * BLK * BLK * HD,
            bytes_accessed=10 * 1024 * 1024,
            transcendentals=spots * nb * NNB * BLK * BLK,
        ),
        name="attention",
    )(place, ids, counts, *tables, rows)


def settle_kernel(grad_own, first, second, *outs):
    for r, out in enumerate(outs):
        for i, scale in enumerate((SCALE, 1.0)):
            total = grad_own[r, :, i] * scale
            total = total + first[r, :, i].astype(F32) + second[r, :, i].astype(F32)
            out[:, i] = total.astype(BF16)


def settle(grad_own, first, second):
    n = grad_own.shape[0]
    return pl.pallas_call(
        settle_kernel,
        out_shape=[jax.ShapeDtypeStruct(grad_own.shape[1:], BF16)] * n,
        in_specs=[VMEM] * 3,
        out_specs=[VMEM] * n,
        compiler_params=pltpu.CompilerParams(vmem_limit_bytes=LIMIT),
        name="settle",
    )(grad_own, first, second)


def swapped(value, start):
    pairs = [(i, i + 1) for i in range(start, lax.axis_size("grp") - 1, 2)]
    return lax.ppermute(value, "grp", pairs + [(j, i) for i, j in pairs])


def turned(value, steps):
    n = lax.axis_size("sp")
    if steps % n == 0:
        return value
    return lax.ppermute(value, "sp", [(i, (i + steps) % n) for i in range(n)])


def exchange(value):
    return lax.all_to_all(value, "sp", split_axis=0, concat_axis=0, tiled=True)


def follow(values, earlier):
    return lax.optimization_barrier((values, earlier))[0]


def local(queries, key_rows, value_rows, upstream, neighbours, counts):
    n = lax.axis_size("sp")
    spots = H // n
    nb = queries.shape[0] * n // BLK
    group = lax.axis_index("grp")
    place = jnp.stack([lax.axis_index("sp"), (group - 1) * nb, group % 2]).astype(jnp.int32)
    order = sorted(range(n), key=lambda d: -min(d, n - d))

    key_parts = pack(place, key_rows, value_rows, spots)
    row_parts = stack(*follow((queries, upstream), key_parts), spots)
    moved = [turned(key_parts[d], d) for d in order]
    moved, row_parts = lax.optimization_barrier((moved, row_parts))
    rows = exchange(row_parts)
    own = join([moved[order.index(d)] for d in range(n)])
    chip, link = swapped(own, 0), swapped(own, 1)
    main, grad_chip, grad_own, grad_link = attention(
        place, neighbours, counts, rows, (chip, own, link)
    )
    from_chip, from_link = swapped(grad_chip, 0), swapped(grad_link, 1)
    attended, query_grad = unstack(exchange(main))
    grads = settle(grad_own, from_chip, from_link)
    returned = [turned(grads[r], -r) for r in order]
    returned = follow(returned, (attended, query_grad))
    key_grad, value_grad = unpack(place, [returned[order.index(r)] for r in range(n)])
    return attended, query_grad, key_grad, value_grad


def solution(mesh):
    rows = P(("grp", "sp"), None)
    return jax.shard_map(
        local,
        mesh=mesh,
        in_specs=(rows, rows, rows, rows, P("grp", None), P("grp")),
        out_specs=(rows, rows, rows, rows),
        check_vma=False,
    )
```

time: 248 us -> 147 us (0.59); the launches traced: 243 us -> 145 us
  Pallas kernels: 154 us -> 30.9 us
  waiting for transfers between devices: 24 us -> 62.5 us
  starting transfers between devices: 61.5 us -> 47.9 us
    pallas_call x8 -> x7, Pallas kernels: 154 us -> 30.9 us  [the longest x1 17.6 us: attention(): pl.pallas_call(functools.partial(attn_kernel, spots, nb), out_shape=[jax....]
    ppermute x8 -> x18, waiting for transfers between devices: 24 us -> 54.3 us  [the longest x4 31.3 us: swapped(): return lax.ppermute(value, 'grp', pairs + [(j, i) for i, j in pairs])]
    all_to_all x4 -> x2, starting transfers between devices: 28.4 us -> 8.94 us  [exchange(): return lax.all_to_all(value, 'sp', split_axis=0, concat_axis=0, tiled=True)]
    all_to_all x4 -> x2, waiting for transfers between devices: 0.01 us -> 8.22 us  [exchange(): return lax.all_to_all(value, 'sp', split_axis=0, concat_axis=0, tiled=True)]
    ppermute x8 -> x18, starting transfers between devices: 33.1 us -> 39 us  [the longest x14 32.3 us: turned(): return lax.ppermute(value, 'sp', [(i, (i + steps) % n) for i in range(n)])]
  transfers between devices with their start and end apart: 12 -> 20, of which waited for: 8 -> 13; matrix products, arithmetic and copies ran while one was open for 0% -> 0% of each run, Pallas kernels for 36% -> 5%
where the time goes in v2:
time: 147 us; the launch traced here: 145 us
  waiting for transfers between devices  62.5 us (43%)
  starting transfers between devices  47.9 us (33%)
  Pallas kernels  30.9 us (21%)
  local copies, waits for them, and re-layouts  2.3 us (2%)
    ppermute x14, starting transfers between devices, turned(): return lax.ppermute(value, 'sp', [(i, (i + steps) % n) for i in range(n)])  32.3 us
    ppermute x4, waiting for transfers between devices, swapped(): return lax.ppermute(value, 'grp', pairs + [(j, i) for i, j in pairs])  31.3 us
    ppermute x14, waiting for transfers between devices, turned(): return lax.ppermute(value, 'sp', [(i, (i + steps) % n) for i in range(n)])  23 us
    pallas_call x1, Pallas kernels, attention(): pl.pallas_call(functools.partial(attn_kernel, spots, nb), out_shape=[jax....  17.6 us
    all_to_all x2, starting transfers between devices, exchange(): return lax.all_to_all(value, 'sp', split_axis=0, concat_axis=0, tiled=True)  8.94 us
    all_to_all x2, waiting for transfers between devices, exchange(): return lax.all_to_all(value, 'sp', split_axis=0, concat_axis=0, tiled=True)  8.22 us
    ppermute x4, starting transfers between devices, swapped(): return lax.ppermute(value, 'grp', pairs + [(j, i) for i, j in pairs])  6.66 us
    pallas_call x1, Pallas kernels, pack(): pl.pallas_call(functools.partial(pack_kernel, spots), out_shape=[jax.Shap...  3.11 us
  transfers between devices with their start and end apart: 20, of which 13 were waited for; matrix products, arithmetic and copies ran while one was open for 0% of the time, Pallas kernels for 5%

profile of v2, /device:TPU:29, one launch (start us, length us, event | category | flops | bytes accessed | tf_op | source)
XLA Modules:
  0.0 145.3 jit_solution(7908296698534198044)
XLA Ops:
  0.6 0.6 pad_add_fusion.refs_0_.place
  1.3 3.1 %pack.1 = (bf16[2,2,128,128]{3,2,1,0:T(8,128)(2,1)}, bf16[2,2,128,128]{3,2,1,0:T(8,128)(2,1)}, bf16[2,2,128,128]{3,2,1,0:T(8,128)(2,1)}, bf16[2,2,128,128]{3,2,1...) custom-call(s32[3]{0:T(128)} %pad_add_fusion.refs_0_.place, ...), custom_call_target="tpu_custom_call" | custom-call | tf_op jit(solution)/shard_map/pack/pallas_call | solution.py:60
  4.4 7.0 %collective-permute-start = (bf16[2,2,128,128]{3,2,1,0:T(8,128)(2,1)}, bf16[2,2,128,128]{3,2,1,0:T(8,128)(2,1)S(1)}, u32[]{:S(2)}, u32[]{:S(2)}) collective-permute-start(bf16[2,2,128,128]{3,2,1,0:T(8,128)(2,1)} %get-tuple-element.47), channel_id=1, source_target_pairs={{0,4},{1,5},{2,6},{3,7},{4,0},{5,1},{6,2},{7,3},{8,12},{9,13},{10,... | collective-permute-start | bytes 393224 | tf_op jit(solution)/shard_map/ppermute | solution.py:349
  11.4 1.6 %collective-permute-start.1 = (bf16[2,2,128,128]{3,2,1,0:T(8,128)(2,1)}, bf16[2,2,128,128]{3,2,1,0:T(8,128)(2,1)S(1)}, u32[]{:S(2)}, u32[]{:S(2)}) collective-permute-start(bf16[2,2,128,128]{3,2,1,0:T(8,128)(2,1)} %get-tuple-element.48), channel_id=1, source_target_pairs={{0,3},{1,4},{2,5},{3,6},{4,7},{5,0},{6,1},{7,2},{8,11},{9,12},{10,... | collective-permute-start | bytes 393224 | tf_op jit(solution)/shard_map/ppermute | solution.py:349
  13.1 2.8 %collective-permute-start.2 = (bf16[2,2,128,128]{3,2,1,0:T(8,128)(2,1)}, bf16[2,2,128,128]{3,2,1,0:T(8,128)(2,1)S(1)}, u32[]{:S(2)}, u32[]{:S(2)}) collective-permute-start(bf16[2,2,128,128]{3,2,1,0:T(8,128)(2,1)} %get-tuple-element.49), channel_id=1, source_target_pairs={{0,5},{1,6},{2,7},{3,0},{4,1},{5,2},{6,3},{7,4},{8,13},{9,14},{10,... | collective-permute-start | bytes 393224 | tf_op jit(solution)/shard_map/ppermute | solution.py:349
  15.9 1.2 collective-permute-start.3
  17.1 2.4 %collective-permute-start.4 = (bf16[2,2,128,128]{3,2,1,0:T(8,128)(2,1)}, bf16[2,2,128,128]{3,2,1,0:T(8,128)(2,1)S(1)}, u32[]{:S(2)}, u32[]{:S(2)}) collective-permute-start(bf16[2,2,128,128]{3,2,1,0:T(8,128)(2,1)} %get-tuple-element.51), channel_id=1, source_target_pairs={{0,6},{1,7},{2,0},{3,1},{4,2},{5,3},{6,4},{7,5},{8,14},{9,15},{10,... | collective-permute-start | bytes 393224 | tf_op jit(solution)/shard_map/ppermute | solution.py:349
  19.5 0.0 collective-permute-done.refs_4_
  19.5 0.7 collective-permute-start.5
  20.2 7.8 %collective-permute-done.1.refs_3_ = bf16[2,2,128,128]{3,2,1,0:T(8,128)(2,1)S(1)} collective-permute-done((bf16[2,2,128,128]{3,2,1,0:T(8,128)(2,1)}, bf16[2,2,128,128]{3,2,1,0:T(8,128)(2,1)S(1)}, u32[]{:S(2)}, u32[]{:S(2)}) %collective-permute-start.1) | collective-permute-done | bytes 131104 | tf_op jit(solution)/shard_map/ppermute | solution.py:349
  28.0 0.0 collective-permute-start.6
  28.0 2.5 %stack.17 = bf16[8,2,2,128,128]{4,3,2,1,0:T(8,128)(2,1)} custom-call(bf16[128,2048]{1,0:T(8,128)(2,1)} %refs_0_, bf16[128,2048]{1,0:T(8,128)(2,1)} %refs_1_.2), custom_call_target="tpu_custom_call" | custom-call | tf_op jit(solution)/shard_map/stack/pallas_call | solution.py:137
  30.5 0.0 collective-permute-done.2.refs_5_
  30.6 0.0 copy-start.5
  30.6 0.0 collective-permute-done.3.refs_2_
  30.6 0.0 copy-start.6
  30.6 1.1 collective-permute-done.4.refs_6_
  31.7 3.2 %collective-permute-done.5.refs_1_ = bf16[2,2,128,128]{3,2,1,0:T(8,128)(2,1)S(1)} collective-permute-done((bf16[2,2,128,128]{3,2,1,0:T(8,128)(2,1)}, bf16[2,2,128,128]{3,2,1,0:T(8,128)(2,1)S(1)}, u32[]{:S(2)}, u32[]{:S(2)}) %collective-permute-start.5) | collective-permute-done | bytes 131104 | tf_op jit(solution)/shard_map/ppermute | solution.py:349
  34.8 0.7 collective-permute-done.6.refs_7_
  35.6 0.0 copy-done.3
  35.6 0.0 copy-done.4
  35.6 4.6 %all-to-all-start = ((bf16[8,2,2,128,128]{4,3,2,1,0:T(8,128)(2,1)}), bf16[8,2,2,128,128]{4,3,2,1,0:T(8,128)(2,1)S(1)}, u32[]{:S(2)}, u32[]{:S(2)}) async-start(bf16[8,2,2,128,128]{4,3,2,1,0:T(8,128)(2,1)} %stack.17), calls=%async_computation | async-start | bytes 2097152 | tf_op jit(solution)/shard_map/all_to_all | solution.py:353
  40.1 0.0 copy-done.5
  40.1 0.0 copy-done.6
  40.1 0.0 copy-done.7
  40.1 0.0 copy-done.8
  40.2 0.0 copy-done.9
  40.2 2.3 %join.1.own = bf16[8,2,2,128,128]{4,3,2,1,0:T(8,128)(2,1)} custom-call(bf16[2,2,128,128]{3,2,1,0:T(8,128)(2,1)} %get-tuple-element.57.refs_0_, bf16[2,2,128,128]{3,2,1,0:T(8,128)(2,1)} %copy-done.8, bf16[2,2,128,128]{3,2,1,0:T(8,128)(2,1)} %copy-done.6, bf16[2,2,128,128]{3,2,1,0:T(8,128)(2,1)} %copy-done.4, bf16[2,2,128,128]{3,2,1,0:T(8,128)(2,1)} %copy-done.3, ...), custom_call_target="tpu_custom_call" | custom-call | tf_op jit(solution)/shard_map/join/pallas_call | solution.py:183
  42.5 3.6 %collective-permute-start.8 = (bf16[8,2,2,128,128]{4,3,2,1,0:T(8,128)(2,1)}, bf16[8,2,2,128,128]{4,3,2,1,0:T(8,128)(2,1)S(1)}, u32[]{:S(2)}, u32[]{:S(2)}) collective-permute-start(bf16[8,2,2,128,128]{4,3,2,1,0:T(8,128)(2,1)} %join.1.own), channel_id=1, source_target_pairs={{8,16},{24,32},{40,48},{56,64},{72,80},{88,96},{104,112},{120,128}... | collective-permute-start | bytes 3145736 | tf_op jit(solution)/shard_map/ppermute | solution.py:342
  46.1 0.1 collective-permute-start.7
  46.2 14.9 %collective-permute-done.8.link = bf16[8,2,2,128,128]{4,3,2,1,0:T(8,128)(2,1)S(1)} collective-permute-done((bf16[8,2,2,128,128]{4,3,2,1,0:T(8,128)(2,1)}, bf16[8,2,2,128,128]{4,3,2,1,0:T(8,128)(2,1)S(1)}, u32[]{:S(2)}, u32[]{:S(2)}) %collective-permute-start.8) | collective-permute-done | bytes 1048608 | tf_op jit(solution)/shard_map/ppermute | solution.py:342
  61.1 0.0 collective-permute-done.7.chip
  61.1 8.2 %all-to-all-done.rows = bf16[8,2,2,128,128]{4,3,2,1,0:T(8,128)(2,1)S(1)} async-done(((bf16[8,2,2,128,128]{4,3,2,1,0:T(8,128)(2,1)}), bf16[8,2,2,128,128]{4,3,2,1,0:T(8,128)(2,1)S(1)}, u32[]{:S(2)}, u32[]{:S(2)}) %all-to-all-start) | async-done | bytes 1048608 | tf_op jit(solution)/shard_map/all_to_all | solution.py:353
  69.3 1.0 copy-done.2
  70.3 17.6 %attention.1 = (bf16[8,2,2,128,128]{4,3,2,1,0:T(8,128)(2,1)}, bf16[8,2,2,128,128]{4,3,2,1,0:T(8,128)(2,1)}, f32[8,2,2,128,128]{4,3,2,1,0:T(8,128)}, bf16[8,2,2,128,128]{4,3,2,1,0:T(8,128)(2,1)}) custom-call(s32[3]{0:T(128)} %pad_add_fusion.refs_0_.place, s32[8,8]{1,0:T(8,128)} %ids.1, s32[8]{0:T(128)} %counts.1, ...), custom_call_target="tpu_custom_call" | custom-call | flops 3221225472 | bytes 10485760 | tf_op jit(solution)/shard_map/attention/pallas_call | solution.py:297
  87.9 4.4 %all-to-all-start.1 = ((bf16[8,2,2,128,128]{4,3,2,1,0:T(8,128)(2,1)}), bf16[8,2,2,128,128]{4,3,2,1,0:T(8,128)(2,1)}, u32[]{:S(2)}, u32[]{:S(2)}) async-start(bf16[8,2,2,128,128]{4,3,2,1,0:T(8,128)(2,1)} %get-tuple-element.66), calls=%async_computation.1 | async-start | bytes 2097152 | tf_op jit(solution)/shard_map/all_to_all | solution.py:353
  92.3 0.6 collective-permute-start.9
  92.9 2.4 %collective-permute-start.10 = (bf16[8,2,2,128,128]{4,3,2,1,0:T(8,128)(2,1)}, bf16[8,2,2,128,128]{4,3,2,1,0:T(8,128)(2,1)S(1)}, u32[]{:S(2)}, u32[]{:S(2)}) collective-permute-start(bf16[8,2,2,128,128]{4,3,2,1,0:T(8,128)(2,1)} %get-tuple-element.71), channel_id=1, source_target_pairs={{8,16},{24,32},{40,48},{56,64},{72,80},{88,96},{104,112},{120,128}... | collective-permute-start | bytes 3145736 | tf_op jit(solution)/shard_map/ppermute | solution.py:342
  95.3 0.1 collective-permute-done.9.first
  95.4 16.3 %collective-permute-done.10.second = bf16[8,2,2,128,128]{4,3,2,1,0:T(8,128)(2,1)S(1)} collective-permute-done((bf16[8,2,2,128,128]{4,3,2,1,0:T(8,128)(2,1)}, bf16[8,2,2,128,128]{4,3,2,1,0:T(8,128)(2,1)S(1)}, u32[]{:S(2)}, u32[]{:S(2)}) %collective-permute-start.10) | collective-permute-done | bytes 1048608 | tf_op jit(solution)/shard_map/ppermute | solution.py:342
  111.7 0.3 settle.1
  112.1 0.6 copy-done.1
  112.7 5.5 %collective-permute-start.11 = (bf16[2,2,128,128]{3,2,1,0:T(8,128)(2,1)S(1)}, bf16[2,2,128,128]{3,2,1,0:T(8,128)(2,1)S(1)}, u32[]{:S(2)}, u32[]{:S(2)}) collective-permute-start(bf16[2,2,128,128]{3,2,1,0:T(8,128)(2,1)S(1)} %get-tuple-element.72), channel_id=1, source_target_pairs={{0,4},{1,5},{2,6},{3,7},{4,0},{5,1},{6,2},{7,3},{8,12},{9,13},{10,... | collective-permute-start | bytes 393224 | tf_op jit(solution)/shard_map/ppermute | solution.py:349
  118.2 0.3 collective-permute-start.12
  118.4 3.0 %collective-permute-start.13 = (bf16[2,2,128,128]{3,2,1,0:T(8,128)(2,1)S(1)}, bf16[2,2,128,128]{3,2,1,0:T(8,128)(2,1)S(1)}, u32[]{:S(2)}, u32[]{:S(2)}) collective-permute-start(bf16[2,2,128,128]{3,2,1,0:T(8,128)(2,1)S(1)} %get-tuple-element.74), channel_id=1, source_target_pairs={{0,3},{1,4},{2,5},{3,6},{4,7},{5,0},{6,1},{7,2},{8,11},{9,12},{10,... | collective-permute-start | bytes 393224 | tf_op jit(solution)/shard_map/ppermute | solution.py:349
  121.4 1.5 %collective-permute-start.14 = (bf16[2,2,128,128]{3,2,1,0:T(8,128)(2,1)S(1)}, bf16[2,2,128,128]{3,2,1,0:T(8,128)(2,1)S(1)}, u32[]{:S(2)}, u32[]{:S(2)}) collective-permute-start(bf16[2,2,128,128]{3,2,1,0:T(8,128)(2,1)S(1)} %get-tuple-element.75), channel_id=1, source_target_pairs={{0,6},{1,7},{2,0},{3,1},{4,2},{5,3},{6,4},{7,5},{8,14},{9,15},{10,... | collective-permute-start | bytes 393224 | tf_op jit(solution)/shard_map/ppermute | solution.py:349
  122.9 0.9 collective-permute-start.15
  123.8 5.7 %collective-permute-done.11.refs_4_ = bf16[2,2,128,128]{3,2,1,0:T(8,128)(2,1)S(1)} collective-permute-done((bf16[2,2,128,128]{3,2,1,0:T(8,128)(2,1)S(1)}, bf16[2,2,128,128]{3,2,1,0:T(8,128)(2,1)S(1)}, u32[]{:S(2)}, u32[]{:S(2)}) %collective-permute-start.11) | collective-permute-done | bytes 131104 | tf_op jit(solution)/shard_map/ppermute | solution.py:349
  129.5 0.0 collective-permute-start.16
  129.5 1.9 %collective-permute-done.12.refs_3_ = bf16[2,2,128,128]{3,2,1,0:T(8,128)(2,1)S(1)} collective-permute-done((bf16[2,2,128,128]{3,2,1,0:T(8,128)(2,1)S(1)}, bf16[2,2,128,128]{3,2,1,0:T(8,128)(2,1)S(1)}, u32[]{:S(2)}, u32[]{:S(2)}) %collective-permute-start.12) | collective-permute-done | bytes 131104 | tf_op jit(solution)/shard_map/ppermute | solution.py:349
  131.4 5.4 %collective-permute-start.17 = (bf16[2,2,128,128]{3,2,1,0:T(8,128)(2,1)S(1)}, bf16[2,2,128,128]{3,2,1,0:T(8,128)(2,1)S(1)}, u32[]{:S(2)}, u32[]{:S(2)}) collective-permute-start(bf16[2,2,128,128]{3,2,1,0:T(8,128)(2,1)S(1)} %get-tuple-element.78), channel_id=1, source_target_pairs={{0,1},{1,2},{2,3},{3,4},{4,5},{5,6},{6,7},{7,0},{8,9},{9,10},{10,1... | collective-permute-start | bytes 393224 | tf_op jit(solution)/shard_map/ppermute | solution.py:349
  136.9 0.0 all-to-all-done.1.value
  136.9 2.5 %unstack.1 = (bf16[128,2048]{1,0:T(8,128)(2,1)}, bf16[128,2048]{1,0:T(8,128)(2,1)}) custom-call(bf16[8,2,2,128,128]{4,3,2,1,0:T(8,128)(2,1)} %all-to-all-done.1.value), custom_call_target="tpu_custom_call" | custom-call | tf_op jit(solution)/shard_map/unstack/pallas_call | solution.py:164
  139.3 0.0 collective-permute-done.13.refs_5_
  139.3 0.2 collective-permute-done.14.refs_2_
  139.6 0.0 collective-permute-done.15.refs_6_
  139.6 0.3 collective-permute-done.16.refs_1_
  139.8 2.1 %collective-permute-done.17.refs_7_ = bf16[2,2,128,128]{3,2,1,0:T(8,128)(2,1)S(1)} collective-permute-done((bf16[2,2,128,128]{3,2,1,0:T(8,128)(2,1)S(1)}, bf16[2,2,128,128]{3,2,1,0:T(8,128)(2,1)S(1)}, u32[]{:S(2)}, u32[]{:S(2)}) %collective-permute-start.17) | collective-permute-done | bytes 131104 | tf_op jit(solution)/shard_map/ppermute | solution.py:349
  141.9 0.0 copy-done.11
  142.0 0.0 copy-done.13
  142.0 0.0 copy-done.14
  142.0 0.0 copy-done.15
  142.0 0.6 copy-done.16
  142.6 2.5 %unpack.1 = (bf16[128,2048]{1,0:T(8,128)(2,1)}, bf16[128,2048]{1,0:T(8,128)(2,1)}) custom-call(s32[3]{0:T(128)} %pad_add_fusion.refs_0_.place, bf16[2,2,128,128]{3,2,1,0:T(8,128)(2,1)} %copy-done.1, bf16[2,2,128,128]{3,2,1,0:T(8,128)(2,1)} %copy-done.15, bf16[2,2,128,128]{3,2,1,0:T(8,128)(2,1)} %copy-done.13, bf16[2,2,128,128]{3,2,1,0:T(8,128)(2,1)} %copy-done.11, ...), custom_call_target="tpu_custom_call" | custom-call | tf_op jit(solution)/shard_map/unpack/pallas_call | solution.py:89
  (20 shorter events, 0.0 us)
Async XLA Ops:
  4.4 15.1 %collective-permute-start = (bf16[2,2,128,128]{3,2,1,0:T(8,128)(2,1)}, bf16[2,2,128,128]{3,2,1,0:T(8,128)(2,1)S(1)}, u32[]{:S(2)}, u32[]{:S(2)}) collective-permute-start(bf16[2,2,128,128]{3,2,1,0:T(8,128)(2,1)} %get-tuple-element.47), channel_id=1, source_target_pairs={{0,4},{1,5},{2,6},{3,7},{4,0},{5,1},{6,2},{7,3},{8,12},{9,13},{10,... | collective-permute-start | bytes 393224 | tf_op jit(solution)/shard_map/ppermute | solution.py:349
  11.4 16.6 %collective-permute-start.1 = (bf16[2,2,128,128]{3,2,1,0:T(8,128)(2,1)}, bf16[2,2,128,128]{3,2,1,0:T(8,128)(2,1)S(1)}, u32[]{:S(2)}, u32[]{:S(2)}) collective-permute-start(bf16[2,2,128,128]{3,2,1,0:T(8,128)(2,1)} %get-tuple-element.48), channel_id=1, source_target_pairs={{0,3},{1,4},{2,5},{3,6},{4,7},{5,0},{6,1},{7,2},{8,11},{9,12},{10,... | collective-permute-start | bytes 393224 | tf_op jit(solution)/shard_map/ppermute | solution.py:349
  13.1 17.5 %collective-permute-start.2 = (bf16[2,2,128,128]{3,2,1,0:T(8,128)(2,1)}, bf16[2,2,128,128]{3,2,1,0:T(8,128)(2,1)S(1)}, u32[]{:S(2)}, u32[]{:S(2)}) collective-permute-start(bf16[2,2,128,128]{3,2,1,0:T(8,128)(2,1)} %get-tuple-element.49), channel_id=1, source_target_pairs={{0,5},{1,6},{2,7},{3,0},{4,1},{5,2},{6,3},{7,4},{8,13},{9,14},{10,... | collective-permute-start | bytes 393224 | tf_op jit(solution)/shard_map/ppermute | solution.py:349
  15.9 14.7 %collective-permute-start.3 = (bf16[2,2,128,128]{3,2,1,0:T(8,128)(2,1)}, bf16[2,2,128,128]{3,2,1,0:T(8,128)(2,1)S(1)}, u32[]{:S(2)}, u32[]{:S(2)}) collective-permute-start(bf16[2,2,128,128]{3,2,1,0:T(8,128)(2,1)} %get-tuple-element.50), channel_id=1, source_target_pairs={{0,2},{1,3},{2,4},{3,5},{4,6},{5,7},{6,0},{7,1},{8,10},{9,11},{10,... | collective-permute-start | bytes 393224 | tf_op jit(solution)/shard_map/ppermute | solution.py:349
  17.1 14.6 %collective-permute-start.4 = (bf16[2,2,128,128]{3,2,1,0:T(8,128)(2,1)}, bf16[2,2,128,128]{3,2,1,0:T(8,128)(2,1)S(1)}, u32[]{:S(2)}, u32[]{:S(2)}) collective-permute-start(bf16[2,2,128,128]{3,2,1,0:T(8,128)(2,1)} %get-tuple-element.51), channel_id=1, source_target_pairs={{0,6},{1,7},{2,0},{3,1},{4,2},{5,3},{6,4},{7,5},{8,14},{9,15},{10,... | collective-permute-start | bytes 393224 | tf_op jit(solution)/shard_map/ppermute | solution.py:349
  19.5 16.1 %copy-start.3 = (bf16[2,2,128,128]{3,2,1,0:T(8,128)(2,1)}, bf16[2,2,128,128]{3,2,1,0:T(8,128)(2,1)S(1)}, u32[]{:S(2)}) copy-start(bf16[2,2,128,128]{3,2,1,0:T(8,128)(2,1)S(1)} %collective-permute-done.refs_4_) | copy-start | bytes 393220
  19.5 15.4 %collective-permute-start.5 = (bf16[2,2,128,128]{3,2,1,0:T(8,128)(2,1)}, bf16[2,2,128,128]{3,2,1,0:T(8,128)(2,1)S(1)}, u32[]{:S(2)}, u32[]{:S(2)}) collective-permute-start(bf16[2,2,128,128]{3,2,1,0:T(8,128)(2,1)} %get-tuple-element.52), channel_id=1, source_target_pairs={{0,1},{1,2},{2,3},{3,4},{4,5},{5,6},{6,7},{7,0},{8,9},{9,10},{10,1... | collective-permute-start | bytes 393224 | tf_op jit(solution)/shard_map/ppermute | solution.py:349
  28.0 7.5 %copy-start.4 = (bf16[2,2,128,128]{3,2,1,0:T(8,128)(2,1)}, bf16[2,2,128,128]{3,2,1,0:T(8,128)(2,1)S(1)}, u32[]{:S(2)}) copy-start(bf16[2,2,128,128]{3,2,1,0:T(8,128)(2,1)S(1)} %collective-permute-done.1.refs_3_) | copy-start | bytes 393220
  28.0 7.5 %collective-permute-start.6 = (bf16[2,2,128,128]{3,2,1,0:T(8,128)(2,1)}, bf16[2,2,128,128]{3,2,1,0:T(8,128)(2,1)S(1)}, u32[]{:S(2)}, u32[]{:S(2)}) collective-permute-start(bf16[2,2,128,128]{3,2,1,0:T(8,128)(2,1)} %get-tuple-element.53), channel_id=1, source_target_pairs={{0,7},{1,0},{2,1},{3,2},{4,3},{5,4},{6,5},{7,6},{8,15},{9,8},{10,9... | collective-permute-start | bytes 393224 | tf_op jit(solution)/shard_map/ppermute | solution.py:349
  30.6 9.6 %copy-start.5 = (bf16[2,2,128,128]{3,2,1,0:T(8,128)(2,1)}, bf16[2,2,128,128]{3,2,1,0:T(8,128)(2,1)S(1)}, u32[]{:S(2)}) copy-start(bf16[2,2,128,128]{3,2,1,0:T(8,128)(2,1)S(1)} %collective-permute-done.2.refs_5_) | copy-start | bytes 393220
  30.6 9.5 %copy-start.6 = (bf16[2,2,128,128]{3,2,1,0:T(8,128)(2,1)}, bf16[2,2,128,128]{3,2,1,0:T(8,128)(2,1)S(1)}, u32[]{:S(2)}) copy-start(bf16[2,2,128,128]{3,2,1,0:T(8,128)(2,1)S(1)} %collective-permute-done.3.refs_2_) | copy-start | bytes 393220
  31.7 8.5 %copy-start.7 = (bf16[2,2,128,128]{3,2,1,0:T(8,128)(2,1)}, bf16[2,2,128,128]{3,2,1,0:T(8,128)(2,1)S(1)}, u32[]{:S(2)}) copy-start(bf16[2,2,128,128]{3,2,1,0:T(8,128)(2,1)S(1)} %collective-permute-done.4.refs_6_) | copy-start | bytes 393220
  34.8 5.3 %copy-start.8 = (bf16[2,2,128,128]{3,2,1,0:T(8,128)(2,1)}, bf16[2,2,128,128]{3,2,1,0:T(8,128)(2,1)S(1)}, u32[]{:S(2)}) copy-start(bf16[2,2,128,128]{3,2,1,0:T(8,128)(2,1)S(1)} %collective-permute-done.5.refs_1_) | copy-start | bytes 393220
  35.6 4.6 %copy-start.9 = (bf16[2,2,128,128]{3,2,1,0:T(8,128)(2,1)}, bf16[2,2,128,128]{3,2,1,0:T(8,128)(2,1)S(1)}, u32[]{:S(2)}) copy-start(bf16[2,2,128,128]{3,2,1,0:T(8,128)(2,1)S(1)} %collective-permute-done.6.refs_7_) | copy-start | bytes 393220
  35.6 33.8 %all-to-all-start = ((bf16[8,2,2,128,128]{4,3,2,1,0:T(8,128)(2,1)}), bf16[8,2,2,128,128]{4,3,2,1,0:T(8,128)(2,1)S(1)}, u32[]{:S(2)}, u32[]{:S(2)}) async-start(bf16[8,2,2,128,128]{4,3,2,1,0:T(8,128)(2,1)} %stack.17), calls=%async_computation | async-start | bytes 2097152 | tf_op jit(solution)/shard_map/all_to_all | solution.py:353
  42.5 18.6 %collective-permute-start.8 = (bf16[8,2,2,128,128]{4,3,2,1,0:T(8,128)(2,1)}, bf16[8,2,2,128,128]{4,3,2,1,0:T(8,128)(2,1)S(1)}, u32[]{:S(2)}, u32[]{:S(2)}) collective-permute-start(bf16[8,2,2,128,128]{4,3,2,1,0:T(8,128)(2,1)} %join.1.own), channel_id=1, source_target_pairs={{8,16},{24,32},{40,48},{56,64},{72,80},{88,96},{104,112},{120,128}... | collective-permute-start | bytes 3145736 | tf_op jit(solution)/shard_map/ppermute | solution.py:342
  46.1 15.0 %collective-permute-start.7 = (bf16[8,2,2,128,128]{4,3,2,1,0:T(8,128)(2,1)}, bf16[8,2,2,128,128]{4,3,2,1,0:T(8,128)(2,1)}, u32[]{:S(2)}, u32[]{:S(2)}) collective-permute-start(bf16[8,2,2,128,128]{4,3,2,1,0:T(8,128)(2,1)} %join.1.own), channel_id=1, source_target_pairs={{0,8},{16,24},{32,40},{48,56},{64,72},{80,88},{96,104},{112,120},{... | collective-permute-start | bytes 3145736 | tf_op jit(solution)/shard_map/ppermute | solution.py:342
  61.1 8.2 %copy-start.17 = (bf16[8,2,2,128,128]{4,3,2,1,0:T(8,128)(2,1)}, bf16[8,2,2,128,128]{4,3,2,1,0:T(8,128)(2,1)S(1)}, u32[]{:S(2)}) copy-start(bf16[8,2,2,128,128]{4,3,2,1,0:T(8,128)(2,1)S(1)} %collective-permute-done.8.link) | copy-start | bytes 3145732
  69.3 1.0 copy-start.2
  87.9 23.8 %copy-start = (f32[8,2,2,128,128]{4,3,2,1,0:T(8,128)S(1)}, f32[8,2,2,128,128]{4,3,2,1,0:T(8,128)}, u32[]{:S(2)}) copy-start(f32[8,2,2,128,128]{4,3,2,1,0:T(8,128)} %get-tuple-element.69.grad_own) | copy-start | bytes 6291460
  87.9 48.9 %all-to-all-start.1 = ((bf16[8,2,2,128,128]{4,3,2,1,0:T(8,128)(2,1)}), bf16[8,2,2,128,128]{4,3,2,1,0:T(8,128)(2,1)}, u32[]{:S(2)}, u32[]{:S(2)}) async-start(bf16[8,2,2,128,128]{4,3,2,1,0:T(8,128)(2,1)} %get-tuple-element.66), calls=%async_computation.1 | async-start | bytes 2097152 | tf_op jit(solution)/shard_map/all_to_all | solution.py:353
  92.3 3.1 %collective-permute-start.9 = (bf16[8,2,2,128,128]{4,3,2,1,0:T(8,128)(2,1)}, bf16[8,2,2,128,128]{4,3,2,1,0:T(8,128)(2,1)S(1)}, u32[]{:S(2)}, u32[]{:S(2)}) collective-permute-start(bf16[8,2,2,128,128]{4,3,2,1,0:T(8,128)(2,1)} %get-tuple-element.70), channel_id=1, source_target_pairs={{0,8},{16,24},{32,40},{48,56},{64,72},{80,88},{96,104},{112,120},{... | collective-permute-start | bytes 3145736 | tf_op jit(solution)/shard_map/ppermute | solution.py:342
  92.9 18.8 %collective-permute-start.10 = (bf16[8,2,2,128,128]{4,3,2,1,0:T(8,128)(2,1)}, bf16[8,2,2,128,128]{4,3,2,1,0:T(8,128)(2,1)S(1)}, u32[]{:S(2)}, u32[]{:S(2)}) collective-permute-start(bf16[8,2,2,128,128]{4,3,2,1,0:T(8,128)(2,1)} %get-tuple-element.71), channel_id=1, source_target_pairs={{8,16},{24,32},{40,48},{56,64},{72,80},{88,96},{104,112},{120,128}... | collective-permute-start | bytes 3145736 | tf_op jit(solution)/shard_map/ppermute | solution.py:342
  112.1 0.7 copy-start.1
  112.7 16.7 %collective-permute-start.11 = (bf16[2,2,128,128]{3,2,1,0:T(8,128)(2,1)S(1)}, bf16[2,2,128,128]{3,2,1,0:T(8,128)(2,1)S(1)}, u32[]{:S(2)}, u32[]{:S(2)}) collective-permute-start(bf16[2,2,128,128]{3,2,1,0:T(8,128)(2,1)S(1)} %get-tuple-element.72), channel_id=1, source_target_pairs={{0,4},{1,5},{2,6},{3,7},{4,0},{5,1},{6,2},{7,3},{8,12},{9,13},{10,... | collective-permute-start | bytes 393224 | tf_op jit(solution)/shard_map/ppermute | solution.py:349
  118.2 13.2 %collective-permute-start.12 = (bf16[2,2,128,128]{3,2,1,0:T(8,128)(2,1)S(1)}, bf16[2,2,128,128]{3,2,1,0:T(8,128)(2,1)S(1)}, u32[]{:S(2)}, u32[]{:S(2)}) collective-permute-start(bf16[2,2,128,128]{3,2,1,0:T(8,128)(2,1)S(1)} %get-tuple-element.73), channel_id=1, source_target_pairs={{0,5},{1,6},{2,7},{3,0},{4,1},{5,2},{6,3},{7,4},{8,13},{9,14},{10,... | collective-permute-start | bytes 393224 | tf_op jit(solution)/shard_map/ppermute | solution.py:349
  118.4 20.9 %collective-permute-start.13 = (bf16[2,2,128,128]{3,2,1,0:T(8,128)(2,1)S(1)}, bf16[2,2,128,128]{3,2,1,0:T(8,128)(2,1)S(1)}, u32[]{:S(2)}, u32[]{:S(2)}) collective-permute-start(bf16[2,2,128,128]{3,2,1,0:T(8,128)(2,1)S(1)} %get-tuple-element.74), channel_id=1, source_target_pairs={{0,3},{1,4},{2,5},{3,6},{4,7},{5,0},{6,1},{7,2},{8,11},{9,12},{10,... | collective-permute-start | bytes 393224 | tf_op jit(solution)/shard_map/ppermute | solution.py:349
  121.4 18.1 %collective-permute-start.14 = (bf16[2,2,128,128]{3,2,1,0:T(8,128)(2,1)S(1)}, bf16[2,2,128,128]{3,2,1,0:T(8,128)(2,1)S(1)}, u32[]{:S(2)}, u32[]{:S(2)}) collective-permute-start(bf16[2,2,128,128]{3,2,1,0:T(8,128)(2,1)S(1)} %get-tuple-element.75), channel_id=1, source_target_pairs={{0,6},{1,7},{2,0},{3,1},{4,2},{5,3},{6,4},{7,5},{8,14},{9,15},{10,... | collective-permute-start | bytes 393224 | tf_op jit(solution)/shard_map/ppermute | solution.py:349
  122.9 16.6 %collective-permute-start.15 = (bf16[2,2,128,128]{3,2,1,0:T(8,128)(2,1)S(1)}, bf16[2,2,128,128]{3,2,1,0:T(8,128)(2,1)S(1)}, u32[]{:S(2)}, u32[]{:S(2)}) collective-permute-start(bf16[2,2,128,128]{3,2,1,0:T(8,128)(2,1)S(1)} %get-tuple-element.76), channel_id=1, source_target_pairs={{0,2},{1,3},{2,4},{3,5},{4,6},{5,7},{6,0},{7,1},{8,10},{9,11},{10,... | collective-permute-start | bytes 393224 | tf_op jit(solution)/shard_map/ppermute | solution.py:349
  129.5 12.5 %copy-start.10 = (bf16[2,2,128,128]{3,2,1,0:T(8,128)(2,1)}, bf16[2,2,128,128]{3,2,1,0:T(8,128)(2,1)S(1)}, u32[]{:S(2)}) copy-start(bf16[2,2,128,128]{3,2,1,0:T(8,128)(2,1)S(1)} %collective-permute-done.11.refs_4_) | copy-start | bytes 393220
  129.5 10.4 %collective-permute-start.16 = (bf16[2,2,128,128]{3,2,1,0:T(8,128)(2,1)S(1)}, bf16[2,2,128,128]{3,2,1,0:T(8,128)(2,1)S(1)}, u32[]{:S(2)}, u32[]{:S(2)}) collective-permute-start(bf16[2,2,128,128]{3,2,1,0:T(8,128)(2,1)S(1)} %get-tuple-element.77), channel_id=1, source_target_pairs={{0,7},{1,0},{2,1},{3,2},{4,3},{5,4},{6,5},{7,6},{8,15},{9,8},{10,9... | collective-permute-start | bytes 393224 | tf_op jit(solution)/shard_map/ppermute | solution.py:349
  131.4 10.5 %copy-start.11 = (bf16[2,2,128,128]{3,2,1,0:T(8,128)(2,1)}, bf16[2,2,128,128]{3,2,1,0:T(8,128)(2,1)S(1)}, u32[]{:S(2)}) copy-start(bf16[2,2,128,128]{3,2,1,0:T(8,128)(2,1)S(1)} %collective-permute-done.12.refs_3_) | copy-start | bytes 393220
  131.4 10.5 %collective-permute-start.17 = (bf16[2,2,128,128]{3,2,1,0:T(8,128)(2,1)S(1)}, bf16[2,2,128,128]{3,2,1,0:T(8,128)(2,1)S(1)}, u32[]{:S(2)}, u32[]{:S(2)}) collective-permute-start(bf16[2,2,128,128]{3,2,1,0:T(8,128)(2,1)S(1)} %get-tuple-element.78), channel_id=1, source_target_pairs={{0,1},{1,2},{2,3},{3,4},{4,5},{5,6},{6,7},{7,0},{8,9},{9,10},{10,1... | collective-permute-start | bytes 393224 | tf_op jit(solution)/shard_map/ppermute | solution.py:349
  139.3 2.6 %copy-start.12 = (bf16[2,2,128,128]{3,2,1,0:T(8,128)(2,1)}, bf16[2,2,128,128]{3,2,1,0:T(8,128)(2,1)S(1)}, u32[]{:S(2)}) copy-start(bf16[2,2,128,128]{3,2,1,0:T(8,128)(2,1)S(1)} %collective-permute-done.13.refs_5_) | copy-start | bytes 393220
  139.6 2.4 %copy-start.13 = (bf16[2,2,128,128]{3,2,1,0:T(8,128)(2,1)}, bf16[2,2,128,128]{3,2,1,0:T(8,128)(2,1)S(1)}, u32[]{:S(2)}) copy-start(bf16[2,2,128,128]{3,2,1,0:T(8,128)(2,1)S(1)} %collective-permute-done.14.refs_2_) | copy-start | bytes 393220
  139.6 2.4 %copy-start.14 = (bf16[2,2,128,128]{3,2,1,0:T(8,128)(2,1)}, bf16[2,2,128,128]{3,2,1,0:T(8,128)(2,1)S(1)}, u32[]{:S(2)}) copy-start(bf16[2,2,128,128]{3,2,1,0:T(8,128)(2,1)S(1)} %collective-permute-done.15.refs_6_) | copy-start | bytes 393220
  139.8 2.1 %copy-start.15 = (bf16[2,2,128,128]{3,2,1,0:T(8,128)(2,1)}, bf16[2,2,128,128]{3,2,1,0:T(8,128)(2,1)S(1)}, u32[]{:S(2)}) copy-start(bf16[2,2,128,128]{3,2,1,0:T(8,128)(2,1)S(1)} %collective-permute-done.16.refs_1_) | copy-start | bytes 393220
  141.9 0.7 copy-start.16

commit v3 on v2

--- a/solution.py
+++ b/solution.py
@@ -37,12 +37,12 @@
 
 
 def pack_kernel(spots, *refs):
-    place, sources = refs[0], refs[1:3]
-    outs, sems = refs[3:-1], refs[-1]
+    sources, outs, sems = refs[:2], refs[2:-1], refs[-1]
     n = len(outs)
+    here = lax.axis_index("sp")
     copies = []
     for d, out in enumerate(outs):
-        owner = lax.rem(place[0] + d, n)
+        owner = lax.rem(here + d, n)
         for i, source in enumerate(sources):
             for h in range(spots):
                 column = pl.multiple_of((owner * spots + h) * HD, HD)
@@ -54,46 +54,48 @@
     run_copies(copies)
 
 
-def pack(place, first, second, spots):
+def pack(first, second, spots):
     rows, width = first.shape
     n = width // (spots * HD)
     return pl.pallas_call(
         functools.partial(pack_kernel, spots),
         out_shape=[jax.ShapeDtypeStruct((spots, 2, rows, HD), BF16)] * n,
-        in_specs=[SMEM, ANY, ANY],
+        in_specs=[ANY, ANY],
         out_specs=[VMEM] * n,
         scratch_shapes=[pltpu.SemaphoreType.DMA((n, 2, spots))],
         name="pack",
-    )(place, first, second)
-
-
-def unpack_kernel(spots, n, place, *refs):
-    received, outs, sems = refs[:n], refs[n:n + 2], refs[-1]
+    )(first, second)
+
+
+def unpack_kernel(spots, n, turns, *refs):
+    received, outs, sems = refs[:len(turns)], refs[-3:-1], refs[-1]
+    here = lax.axis_index("sp")
     copies = []
-    for r, value in enumerate(received):
-        source = lax.rem(place[0] + r, n)
+    for at, (turn, value) in enumerate(zip(turns, received)):
+        source = lax.rem(here + turn, n)
         for i, out in enumerate(outs):
             for h in range(spots):
                 column = pl.multiple_of((source * spots + h) * HD, HD)
                 copies.append(
                     pltpu.make_async_copy(
-                        value.at[h, i], out.at[:, pl.ds(column, HD)], sems.at[r, i, h]
+                        value.at[h, i], out.at[:, pl.ds(column, HD)], sems.at[at, i, h]
                     )
                 )
     run_copies(copies)
 
 
-def unpack(place, received):
-    n = len(received)
+def unpack(turns, received, n, held=()):
     spots, _, rows, _ = received[0].shape
-    return pl.pallas_call(
-        functools.partial(unpack_kernel, spots, n),
+    count = len(turns)
+    return pl.pallas_call(
+        functools.partial(unpack_kernel, spots, n, turns),
         out_shape=[jax.ShapeDtypeStruct((rows, n * spots * HD), BF16)] * 2,
-        in_specs=[SMEM] + [VMEM] * n,
+        in_specs=[VMEM] * count + [ANY] * len(held),
         out_specs=[ANY] * 2,
-        scratch_shapes=[pltpu.SemaphoreType.DMA((n, 2, spots))],
+        input_output_aliases={count + i: i for i in range(len(held))},
+        scratch_shapes=[pltpu.SemaphoreType.DMA((count, 2, spots))],
         name="unpack",
-    )(place, *received)
+    )(*received, *held)
 
 
 def join_kernel(*refs):
@@ -191,13 +193,14 @@
 
 
 def attn_kernel(
-    spots, nb, place, ids, counts, chip, own, link, rows,
-    main_out, grad_chip, grad_own, grad_link, cache, acc, main, edge, soft, sems,
+    spots, nb, ids, counts, chip, own, link, rows_in,
+    main_out, grad_chip, grad_own, grad_link, rows, cache, acc, main, edge, sems,
 ):
-    here, offset, odd = place[0], place[1], place[2]
+    here, group = lax.axis_index("sp"), lax.axis_index("grp")
+    offset, odd = (group - 1) * nb, lax.rem(group, 2)
     chip_at = 2 * nb * (1 - odd)
     link_at = 2 * nb * odd
-    copies = []
+    copies = [pltpu.make_async_copy(rows_in, rows, sems.at[3])]
     for g, (x, at) in enumerate(((chip, chip_at), (own, nb), (link, link_at))):
         copies.append(pltpu.make_async_copy(x, cache.at[pl.ds(at, nb)], sems.at[g]))
     for copy in copies:
@@ -206,106 +209,93 @@
     for copy in copies:
         copy.wait()
 
-    wide = PAIR * BLK
-
-    def block(b, carry):
-        used = counts[b]
+    def visit(b, used, width):
         slots = []
-        for j in range(NNB):
+        for j in range(width):
             local_id = ids[b, j] - offset
             side = local_id // nb
             slots.append(side * nb + lax.rem(here - (local_id - side * nb) + nb, nb))
         heads = range(spots)
-        chunks = range(NNB // PAIR)
-        lane_slot = lax.broadcasted_iota(jnp.int32, (1, wide), 1) // BLK
-
-        def tile(h, i, c):
-            return jnp.concatenate(
-                [cache[s, h, i] for s in slots[c * PAIR:(c + 1) * PAIR]], axis=0
-            )
-
-        def span(c):
-            return slice(c * wide, (c + 1) * wide)
-
-        def add(h, i, c, part):
-            for j, s in enumerate(slots[c * PAIR:(c + 1) * PAIR]):
-                acc[s, h, i] += part[j * BLK:(j + 1) * BLK]
+        lane_slot = lax.broadcasted_iota(jnp.int32, (1, width * BLK), 1) // BLK
+
+        def tiles(h, i):
+            return jnp.concatenate([cache[s, h, i] for s in slots], axis=0)
 
         queries = [rows[b, h, 0] for h in heads]
         grads = [rows[b, h, 1] for h in heads]
-        highest, inverse, delta = [], [], []
+        probs = []
         for h in heads:
-            top = None
-            for c in chunks:
-                raw = dot(queries[h], tile(h, 0, c), NT)
-                raw = jnp.where(lane_slot + c * PAIR < used, raw, -1e30)
-                soft[h, :, span(c)] = raw
-                top = raw if top is None else jnp.maximum(top, raw)
-            highest.append(jnp.max(top, axis=1, keepdims=True))
+            raw = dot(queries[h], tiles(h, 0), NT)
+            raw = jnp.where(lane_slot < used, raw, -1e30)
+            highest = jnp.max(raw, axis=1, keepdims=True)
+            raised = jnp.exp2((raw - highest) * (SCALE * LOG2E))
+            probs.append(raised * (1.0 / jnp.sum(raised, axis=1, keepdims=True)))
+        weights, deltas = [], []
         for h in heads:
-            total = None
-            for c in chunks:
-                raised = jnp.exp2((soft[h, :, span(c)] - highest[h]) * (SCALE * LOG2E))
-                soft[h, :, span(c)] = raised
-                total = raised if total is None else total + raised
-            inverse.append(1.0 / jnp.sum(total, axis=1, keepdims=True))
-        for h in heads:
-            out = None
-            for c in chunks:
-                weights = (soft[h, :, span(c)] * inverse[h]).astype(BF16)
-                part = dot(weights, tile(h, 1, c), NN)
-                out = part if out is None else out + part
-                add(h, 1, c, dot(weights, grads[h], TN))
-            attended = out.astype(BF16)
+            weights.append(probs[h].astype(BF16))
+            attended = dot(weights[h], tiles(h, 1), NN).astype(BF16)
             main[b, h, 0] = attended
-            delta.append(
+            deltas.append(
                 jnp.sum(grads[h].astype(F32) * attended.astype(F32), axis=1, keepdims=True)
             )
         for h in heads:
-            out = None
-            for c in chunks:
-                grad_prob = dot(grads[h], tile(h, 1, c), NT)
-                prob = soft[h, :, span(c)] * inverse[h]
-                score = (prob * (grad_prob - delta[h])).astype(BF16)
-                part = dot(score, tile(h, 0, c), NN)
-                out = part if out is None else out + part
-                add(h, 0, c, dot(score, queries[h], TN))
-            main[b, h, 1] = (out * SCALE).astype(BF16)
-        pltpu.make_async_copy(main.at[b], main_out.at[b], sems.at[3 + b]).start()
+            grad_prob = dot(grads[h], tiles(h, 1), NT)
+            score = (probs[h] * (grad_prob - deltas[h])).astype(BF16)
+            main[b, h, 1] = (dot(score, tiles(h, 0), NN) * SCALE).astype(BF16)
+            key_part = dot(score, queries[h], TN)
+            value_part = dot(weights[h], grads[h], TN)
+            for j, s in enumerate(slots):
+                acc[s, h, 0] += key_part[j * BLK:(j + 1) * BLK]
+                acc[s, h, 1] += value_part[j * BLK:(j + 1) * BLK]
+        pltpu.make_async_copy(main.at[b], main_out.at[b], sems.at[4 + b]).start()
+
+    def block(b, carry):
+        used = counts[b]
+        for width in (2, 4, 6, 8):
+            pl.when((used <= width) & (used > width - 2))(
+                functools.partial(visit, b, used, width)
+            )
         return carry
 
     lax.fori_loop(0, nb, block, 0)
     copies = [
-        pltpu.make_async_copy(main.at[b], main_out.at[b], sems.at[3 + b]) for b in range(nb)
+        pltpu.make_async_copy(main.at[b], main_out.at[b], sems.at[4 + b]) for b in range(nb)
     ]
+    copies.append(pltpu.make_async_copy(acc.at[pl.ds(nb, nb)], grad_own, sems.at[2]))
+    copies[-1].start()
     for i, (at, out) in enumerate(((link_at, grad_link), (chip_at, grad_chip))):
         part = pl.ds(at, nb)
         edge[i, :, :, 0] = (acc[part, :, 0] * SCALE).astype(BF16)
         edge[i, :, :, 1] = acc[part, :, 1].astype(BF16)
         copies.append(pltpu.make_async_copy(edge.at[i], out, sems.at[i]))
         copies[-1].start()
-    copies.append(pltpu.make_async_copy(acc.at[pl.ds(nb, nb)], grad_own, sems.at[2]))
-    copies[-1].start()
     for copy in copies:
         copy.wait()
 
 
-def attention(place, ids, counts, rows, tables):
+def attention(ids, counts, rows, tables):
     shape = tables[0].shape
     nb, spots = shape[:2]
     whole = (3 * nb, *shape[1:])
+    sums = whole
+    mine = shape
     return pl.pallas_call(
         functools.partial(attn_kernel, spots, nb),
-        out_shape=[jax.ShapeDtypeStruct(shape, kind) for kind in (BF16, BF16, F32, BF16)],
-        in_specs=[SMEM] * 3 + [VMEM] * 4,
+        out_shape=[
+            jax.ShapeDtypeStruct(shape, BF16),
+            jax.ShapeDtypeStruct(shape, BF16),
+            jax.ShapeDtypeStruct(mine, F32),
+            jax.ShapeDtypeStruct(shape, BF16),
+        ],
+        in_specs=[SMEM] * 2 + [ANY] * 4,
         out_specs=[ANY] * 4,
         scratch_shapes=[
+            pltpu.VMEM(shape, BF16),
             pltpu.VMEM(whole, BF16),
-            pltpu.VMEM(whole, F32),
+            pltpu.VMEM(sums, F32),
             pltpu.VMEM(shape, BF16),
             pltpu.VMEM((2, *shape), BF16),
-            pltpu.VMEM((spots, BLK, NNB * BLK), F32),
-            pltpu.SemaphoreType.DMA((3 + nb,)),
+            pltpu.SemaphoreType.DMA((4 + nb,)),
         ],
         compiler_params=pltpu.CompilerParams(vmem_limit_bytes=59 * 1024 * 1024),
         cost_estimate=pl.CostEstimate(
@@ -314,7 +304,7 @@
             transcendentals=spots * nb * NNB * BLK * BLK,
         ),
         name="attention",
-    )(place, ids, counts, *tables, rows)
+    )(ids, counts, *tables, rows)
 
 
 def settle_kernel(grad_own, first, second, *outs):
@@ -361,26 +351,24 @@
     n = lax.axis_size("sp")
     spots = H // n
     nb = queries.shape[0] * n // BLK
-    group = lax.axis_index("grp")
-    place = jnp.stack([lax.axis_index("sp"), (group - 1) * nb, group % 2]).astype(jnp.int32)
-    order = sorted(range(n), key=lambda d: -min(d, n - d))
-
-    key_parts = pack(place, key_rows, value_rows, spots)
+    order = tuple(sorted(range(1, n), key=lambda d: -min(d, n - d)))
+
+    key_parts = pack(key_rows, value_rows, spots)
     row_parts = stack(*follow((queries, upstream), key_parts), spots)
     moved = [turned(key_parts[d], d) for d in order]
     moved, row_parts = lax.optimization_barrier((moved, row_parts))
     rows = exchange(row_parts)
-    own = join([moved[order.index(d)] for d in range(n)])
+    own = join([key_parts[0], *(moved[order.index(d)] for d in range(1, n))])
     chip, link = swapped(own, 0), swapped(own, 1)
     main, grad_chip, grad_own, grad_link = attention(
-        place, neighbours, counts, rows, (chip, own, link)
+        neighbours, counts, rows, (chip, own, link)
     )
     from_chip, from_link = swapped(grad_chip, 0), swapped(grad_link, 1)
     attended, query_grad = unstack(exchange(main))
     grads = settle(grad_own, from_chip, from_link)
     returned = [turned(grads[r], -r) for r in order]
     returned = follow(returned, (attended, query_grad))
-    key_grad, value_grad = unpack(place, [returned[order.index(r)] for r in range(n)])
+    key_grad, value_grad = unpack((0, *order), [grads[0], *returned], n)
     return attended, query_grad, key_grad, value_grad
 
 

time: 147 us -> 144 us (0.980)
  Pallas kernels: 30.9 us -> 29.3 us
  transfers between devices with their start and end apart: 20 -> 20, of which waited for: 13 -> 12; matrix products, arithmetic and copies ran while one was open for 0% -> 0% of each run, Pallas kernels for 5% -> 5%
where the time goes in v3:
time: 144 us; the launch traced here: 143 us
  waiting for transfers between devices  61.6 us (43%)
  starting transfers between devices  48.9 us (34%)
  Pallas kernels  29.3 us (20%)
  local copies, waits for them, and re-layouts  2.3 us (2%)
    ppermute x14, starting transfers between devices, turned(): return lax.ppermute(value, 'sp', [(i, (i + steps) % n) for i in range(n)])  33.6 us
    ppermute x4, waiting for transfers between devices, swapped(): return lax.ppermute(value, 'grp', pairs + [(j, i) for i, j in pairs])  30.9 us
    ppermute x14, waiting for transfers between devices, turned(): return lax.ppermute(value, 'sp', [(i, (i + steps) % n) for i in range(n)])  22.4 us
    pallas_call x1, Pallas kernels, attention(): pl.pallas_call(functools.partial(attn_kernel, spots, nb), out_shape=[jax....  16.7 us
    all_to_all x2, starting transfers between devices, exchange(): return lax.all_to_all(value, 'sp', split_axis=0, concat_axis=0, tiled=True)  8.94 us
    all_to_all x2, waiting for transfers between devices, exchange(): return lax.all_to_all(value, 'sp', split_axis=0, concat_axis=0, tiled=True)  8.22 us
    ppermute x4, starting transfers between devices, swapped(): return lax.ppermute(value, 'grp', pairs + [(j, i) for i, j in pairs])  6.38 us
  transfers between devices with their start and end apart: 20, of which 12 were waited for; matrix products, arithmetic and copies ran while one was open for 0% of the time, Pallas kernels for 5%

profile of v3, /device:TPU:29, one launch (start us, length us, event | category | flops | bytes accessed | tf_op | source)
XLA Modules:
  0.0 143.1 jit_solution(11776400394579194915)
XLA Ops:
  0.6 2.5 %pack.1 = (bf16[2,2,128,128]{3,2,1,0:T(8,128)(2,1)}, bf16[2,2,128,128]{3,2,1,0:T(8,128)(2,1)}, bf16[2,2,128,128]{3,2,1,0:T(8,128)(2,1)}, bf16[2,2,128,128]{3,2,1...) custom-call(bf16[128,2048]{1,0:T(8,128)(2,1)} %refs_0_.1, ...), custom_call_target="tpu_custom_call" | custom-call | tf_op jit(solution)/shard_map/pack/pallas_call | solution.py:60
  3.1 7.0 %collective-permute-start = (bf16[2,2,128,128]{3,2,1,0:T(8,128)(2,1)}, bf16[2,2,128,128]{3,2,1,0:T(8,128)(2,1)S(1)}, u32[]{:S(2)}, u32[]{:S(2)}) collective-permute-start(bf16[2,2,128,128]{3,2,1,0:T(8,128)(2,1)} %get-tuple-element.46), channel_id=1, source_target_pairs={{0,4},{1,5},{2,6},{3,7},{4,0},{5,1},{6,2},{7,3},{8,12},{9,13},{10,... | collective-permute-start | bytes 393224 | tf_op jit(solution)/shard_map/ppermute | solution.py:339
  10.1 1.6 %collective-permute-start.1 = (bf16[2,2,128,128]{3,2,1,0:T(8,128)(2,1)}, bf16[2,2,128,128]{3,2,1,0:T(8,128)(2,1)S(1)}, u32[]{:S(2)}, u32[]{:S(2)}) collective-permute-start(bf16[2,2,128,128]{3,2,1,0:T(8,128)(2,1)} %get-tuple-element.47), channel_id=1, source_target_pairs={{0,3},{1,4},{2,5},{3,6},{4,7},{5,0},{6,1},{7,2},{8,11},{9,12},{10,... | collective-permute-start | bytes 393224 | tf_op jit(solution)/shard_map/ppermute | solution.py:339
  11.7 2.8 %collective-permute-start.2 = (bf16[2,2,128,128]{3,2,1,0:T(8,128)(2,1)}, bf16[2,2,128,128]{3,2,1,0:T(8,128)(2,1)S(1)}, u32[]{:S(2)}, u32[]{:S(2)}) collective-permute-start(bf16[2,2,128,128]{3,2,1,0:T(8,128)(2,1)} %get-tuple-element.48), channel_id=1, source_target_pairs={{0,5},{1,6},{2,7},{3,0},{4,1},{5,2},{6,3},{7,4},{8,13},{9,14},{10,... | collective-permute-start | bytes 393224 | tf_op jit(solution)/shard_map/ppermute | solution.py:339
  14.6 1.2 collective-permute-start.3
  15.8 2.4 %collective-permute-start.4 = (bf16[2,2,128,128]{3,2,1,0:T(8,128)(2,1)}, bf16[2,2,128,128]{3,2,1,0:T(8,128)(2,1)S(1)}, u32[]{:S(2)}, u32[]{:S(2)}) collective-permute-start(bf16[2,2,128,128]{3,2,1,0:T(8,128)(2,1)} %get-tuple-element.50), channel_id=1, source_target_pairs={{0,6},{1,7},{2,0},{3,1},{4,2},{5,3},{6,4},{7,5},{8,14},{9,15},{10,... | collective-permute-start | bytes 393224 | tf_op jit(solution)/shard_map/ppermute | solution.py:339
  18.1 0.0 collective-permute-done.refs_4_
  18.2 0.7 collective-permute-start.5
  18.9 7.8 %collective-permute-done.1.refs_3_ = bf16[2,2,128,128]{3,2,1,0:T(8,128)(2,1)S(1)} collective-permute-done((bf16[2,2,128,128]{3,2,1,0:T(8,128)(2,1)}, bf16[2,2,128,128]{3,2,1,0:T(8,128)(2,1)S(1)}, u32[]{:S(2)}, u32[]{:S(2)}) %collective-permute-start.1) | collective-permute-done | bytes 131104 | tf_op jit(solution)/shard_map/ppermute | solution.py:339
  26.7 0.0 collective-permute-start.6
  26.7 2.5 %stack.1 = bf16[8,2,2,128,128]{4,3,2,1,0:T(8,128)(2,1)} custom-call(bf16[128,2048]{1,0:T(8,128)(2,1)} %refs_0_.2, bf16[128,2048]{1,0:T(8,128)(2,1)} %refs_1_.2), custom_call_target="tpu_custom_call" | custom-call | tf_op jit(solution)/shard_map/stack/pallas_call | solution.py:139
  29.2 0.0 collective-permute-done.2.refs_5_
  29.2 0.0 copy-start.5
  29.3 0.0 collective-permute-done.3.refs_2_
  29.3 0.0 copy-start.6
  29.3 1.1 collective-permute-done.4.refs_6_
  30.4 3.2 %collective-permute-done.5.refs_1_ = bf16[2,2,128,128]{3,2,1,0:T(8,128)(2,1)S(1)} collective-permute-done((bf16[2,2,128,128]{3,2,1,0:T(8,128)(2,1)}, bf16[2,2,128,128]{3,2,1,0:T(8,128)(2,1)S(1)}, u32[]{:S(2)}, u32[]{:S(2)}) %collective-permute-start.5) | collective-permute-done | bytes 131104 | tf_op jit(solution)/shard_map/ppermute | solution.py:339
  33.5 0.7 collective-permute-done.6.refs_7_
  34.2 0.0 copy-done.3
  34.2 0.0 copy-done.4
  34.2 4.6 %all-to-all-start = ((bf16[8,2,2,128,128]{4,3,2,1,0:T(8,128)(2,1)}), bf16[8,2,2,128,128]{4,3,2,1,0:T(8,128)(2,1)S(1)}, u32[]{:S(2)}, u32[]{:S(2)}) async-start(bf16[8,2,2,128,128]{4,3,2,1,0:T(8,128)(2,1)} %stack.1), calls=%async_computation | async-start | bytes 2097152 | tf_op jit(solution)/shard_map/all_to_all | solution.py:343
  38.8 0.0 copy-done.5
  38.8 0.0 copy-done.6
  38.8 0.0 copy-done.7
  38.8 0.0 copy-done.8
  38.8 0.0 copy-done.9
  38.8 2.3 %join.1.own = bf16[8,2,2,128,128]{4,3,2,1,0:T(8,128)(2,1)} custom-call(bf16[2,2,128,128]{3,2,1,0:T(8,128)(2,1)} %get-tuple-element.45.refs_0_, bf16[2,2,128,128]{3,2,1,0:T(8,128)(2,1)} %copy-done.8, bf16[2,2,128,128]{3,2,1,0:T(8,128)(2,1)} %copy-done.6, bf16[2,2,128,128]{3,2,1,0:T(8,128)(2,1)} %copy-done.4, bf16[2,2,128,128]{3,2,1,0:T(8,128)(2,1)} %copy-done.3, ...), custom_call_target="tpu_custom_call" | custom-call | tf_op jit(solution)/shard_map/join/pallas_call | solution.py:185
  41.2 3.6 %collective-permute-start.8 = (bf16[8,2,2,128,128]{4,3,2,1,0:T(8,128)(2,1)}, bf16[8,2,2,128,128]{4,3,2,1,0:T(8,128)(2,1)S(1)}, u32[]{:S(2)}, u32[]{:S(2)}) collective-permute-start(bf16[8,2,2,128,128]{4,3,2,1,0:T(8,128)(2,1)} %join.1.own), channel_id=1, source_target_pairs={{8,16},{24,32},{40,48},{56,64},{72,80},{88,96},{104,112},{120,128}... | collective-permute-start | bytes 3145736 | tf_op jit(solution)/shard_map/ppermute | solution.py:332
  44.8 0.1 collective-permute-start.7
  44.9 14.9 %collective-permute-done.8.link = bf16[8,2,2,128,128]{4,3,2,1,0:T(8,128)(2,1)S(1)} collective-permute-done((bf16[8,2,2,128,128]{4,3,2,1,0:T(8,128)(2,1)}, bf16[8,2,2,128,128]{4,3,2,1,0:T(8,128)(2,1)S(1)}, u32[]{:S(2)}, u32[]{:S(2)}) %collective-permute-start.8) | collective-permute-done | bytes 1048608 | tf_op jit(solution)/shard_map/ppermute | solution.py:332
  59.8 0.0 collective-permute-done.7.chip
  59.8 8.2 %all-to-all-done.rows_in = bf16[8,2,2,128,128]{4,3,2,1,0:T(8,128)(2,1)S(1)} async-done(((bf16[8,2,2,128,128]{4,3,2,1,0:T(8,128)(2,1)}), bf16[8,2,2,128,128]{4,3,2,1,0:T(8,128)(2,1)S(1)}, u32[]{:S(2)}, u32[]{:S(2)}) %all-to-all-start) | async-done | bytes 1048608 | tf_op jit(solution)/shard_map/all_to_all | solution.py:343
  68.0 0.0 copy-done.17
  68.0 1.0 copy-done.2
  69.0 16.7 %attention.1 = (bf16[8,2,2,128,128]{4,3,2,1,0:T(8,128)(2,1)}, bf16[8,2,2,128,128]{4,3,2,1,0:T(8,128)(2,1)}, f32[8,2,2,128,128]{4,3,2,1,0:T(8,128)}, bf16[8,2,2,128,128]{4,3,2,1,0:T(8,128)(2,1)}) custom-call(s32[8,8]{1,0:T(8,128)} %ids.1, s32[8]{0:T(128)} %counts.1, bf16[8,2,2,128,128]{4,3,2,1,0:T(8,128)(2,1)} %collective-permute-done.7.chip, ...), custom_call_target="tpu_custom_call" | custom-call | flops 3221225472 | bytes 10485760 | tf_op jit(solution)/shard_map/attention/pallas_call | solution.py:282
  85.7 0.0 copy-start
  85.7 4.4 %all-to-all-start.1 = ((bf16[8,2,2,128,128]{4,3,2,1,0:T(8,128)(2,1)}), bf16[8,2,2,128,128]{4,3,2,1,0:T(8,128)(2,1)}, u32[]{:S(2)}, u32[]{:S(2)}) async-start(bf16[8,2,2,128,128]{4,3,2,1,0:T(8,128)(2,1)} %get-tuple-element.63), calls=%async_computation.1 | async-start | bytes 2097152 | tf_op jit(solution)/shard_map/all_to_all | solution.py:343
  90.1 0.1 collective-permute-start.9
  90.2 2.6 %collective-permute-start.10 = (bf16[8,2,2,128,128]{4,3,2,1,0:T(8,128)(2,1)}, bf16[8,2,2,128,128]{4,3,2,1,0:T(8,128)(2,1)S(1)}, u32[]{:S(2)}, u32[]{:S(2)}) collective-permute-start(bf16[8,2,2,128,128]{4,3,2,1,0:T(8,128)(2,1)} %get-tuple-element.68), channel_id=1, source_target_pairs={{8,16},{24,32},{40,48},{56,64},{72,80},{88,96},{104,112},{120,128}... | collective-permute-start | bytes 3145736 | tf_op jit(solution)/shard_map/ppermute | solution.py:332
  92.8 0.3 collective-permute-done.9.first
  93.1 15.8 %collective-permute-done.10.second = bf16[8,2,2,128,128]{4,3,2,1,0:T(8,128)(2,1)S(1)} collective-permute-done((bf16[8,2,2,128,128]{4,3,2,1,0:T(8,128)(2,1)}, bf16[8,2,2,128,128]{4,3,2,1,0:T(8,128)(2,1)S(1)}, u32[]{:S(2)}, u32[]{:S(2)}) %collective-permute-start.10) | collective-permute-done | bytes 1048608 | tf_op jit(solution)/shard_map/ppermute | solution.py:332
  108.9 0.0 copy-done
  108.9 0.3 settle.1
  109.2 0.0 copy-start.1
  109.2 0.6 copy-done.1
  109.9 5.3 %collective-permute-start.11 = (bf16[2,2,128,128]{3,2,1,0:T(8,128)(2,1)S(1)}, bf16[2,2,128,128]{3,2,1,0:T(8,128)(2,1)S(1)}, u32[]{:S(2)}, u32[]{:S(2)}) collective-permute-start(bf16[2,2,128,128]{3,2,1,0:T(8,128)(2,1)S(1)} %get-tuple-element.70), channel_id=1, source_target_pairs={{0,4},{1,5},{2,6},{3,7},{4,0},{5,1},{6,2},{7,3},{8,12},{9,13},{10,... | collective-permute-start | bytes 393224 | tf_op jit(solution)/shard_map/ppermute | solution.py:339
  115.2 0.3 collective-permute-start.12
  115.5 3.0 %collective-permute-start.13 = (bf16[2,2,128,128]{3,2,1,0:T(8,128)(2,1)S(1)}, bf16[2,2,128,128]{3,2,1,0:T(8,128)(2,1)S(1)}, u32[]{:S(2)}, u32[]{:S(2)}) collective-permute-start(bf16[2,2,128,128]{3,2,1,0:T(8,128)(2,1)S(1)} %get-tuple-element.72), channel_id=1, source_target_pairs={{0,3},{1,4},{2,5},{3,6},{4,7},{5,0},{6,1},{7,2},{8,11},{9,12},{10,... | collective-permute-start | bytes 393224 | tf_op jit(solution)/shard_map/ppermute | solution.py:339
  118.5 1.1 collective-permute-start.14
  119.5 1.3 collective-permute-start.15
  120.8 6.5 %collective-permute-done.11.refs_1_ = bf16[2,2,128,128]{3,2,1,0:T(8,128)(2,1)S(1)} collective-permute-done((bf16[2,2,128,128]{3,2,1,0:T(8,128)(2,1)S(1)}, bf16[2,2,128,128]{3,2,1,0:T(8,128)(2,1)S(1)}, u32[]{:S(2)}, u32[]{:S(2)}) %collective-permute-start.11) | collective-permute-done | bytes 131104 | tf_op jit(solution)/shard_map/ppermute | solution.py:339
  127.3 0.0 collective-permute-start.16
  127.3 0.0 collective-permute-done.12.refs_2_
  127.4 6.9 %collective-permute-start.17 = (bf16[2,2,128,128]{3,2,1,0:T(8,128)(2,1)S(1)}, bf16[2,2,128,128]{3,2,1,0:T(8,128)(2,1)S(1)}, u32[]{:S(2)}, u32[]{:S(2)}) collective-permute-start(bf16[2,2,128,128]{3,2,1,0:T(8,128)(2,1)S(1)} %get-tuple-element.76), channel_id=1, source_target_pairs={{0,1},{1,2},{2,3},{3,4},{4,5},{5,6},{6,7},{7,0},{8,9},{9,10},{10,1... | collective-permute-start | bytes 393224 | tf_op jit(solution)/shard_map/ppermute | solution.py:339
  134.2 0.0 all-to-all-done.1.value
  134.2 2.5 %unstack.1 = (bf16[128,2048]{1,0:T(8,128)(2,1)}, bf16[128,2048]{1,0:T(8,128)(2,1)}) custom-call(bf16[8,2,2,128,128]{4,3,2,1,0:T(8,128)(2,1)} %all-to-all-done.1.value), custom_call_target="tpu_custom_call" | custom-call | tf_op jit(solution)/shard_map/unstack/pallas_call | solution.py:166
  136.7 0.0 collective-permute-done.13.refs_3_
  136.7 0.8 collective-permute-done.14.refs_4_
  137.5 0.0 collective-permute-done.15.refs_5_
  137.5 0.4 collective-permute-done.16.refs_6_
  137.9 1.9 %collective-permute-done.17.refs_7_ = bf16[2,2,128,128]{3,2,1,0:T(8,128)(2,1)S(1)} collective-permute-done((bf16[2,2,128,128]{3,2,1,0:T(8,128)(2,1)S(1)}, bf16[2,2,128,128]{3,2,1,0:T(8,128)(2,1)S(1)}, u32[]{:S(2)}, u32[]{:S(2)}) %collective-permute-start.17) | collective-permute-done | bytes 131104 | tf_op jit(solution)/shard_map/ppermute | solution.py:339
  139.8 0.0 copy-done.10
  139.8 0.6 copy-done.16
  140.5 2.5 %unpack.1 = (bf16[128,2048]{1,0:T(8,128)(2,1)}, bf16[128,2048]{1,0:T(8,128)(2,1)}) custom-call(bf16[2,2,128,128]{3,2,1,0:T(8,128)(2,1)} %copy-done.1, bf16[2,2,128,128]{3,2,1,0:T(8,128)(2,1)} %copy-done.10, bf16[2,2,128,128]{3,2,1,0:T(8,128)(2,1)} %copy-done.11, bf16[2,2,128,128]{3,2,1,0:T(8,128)(2,1)} %copy-done.12, bf16[2,2,128,128]{3,2,1,0:T(8,128)(2,1)} %copy-done.13, ...), custom_call_target="tpu_custom_call" | custom-call | tf_op jit(solution)/shard_map/unpack/pallas_call | solution.py:90
  (19 shorter events, 0.0 us)
Async XLA Ops:
  3.1 15.1 %collective-permute-start = (bf16[2,2,128,128]{3,2,1,0:T(8,128)(2,1)}, bf16[2,2,128,128]{3,2,1,0:T(8,128)(2,1)S(1)}, u32[]{:S(2)}, u32[]{:S(2)}) collective-permute-start(bf16[2,2,128,128]{3,2,1,0:T(8,128)(2,1)} %get-tuple-element.46), channel_id=1, source_target_pairs={{0,4},{1,5},{2,6},{3,7},{4,0},{5,1},{6,2},{7,3},{8,12},{9,13},{10,... | collective-permute-start | bytes 393224 | tf_op jit(solution)/shard_map/ppermute | solution.py:339
  10.1 16.6 %collective-permute-start.1 = (bf16[2,2,128,128]{3,2,1,0:T(8,128)(2,1)}, bf16[2,2,128,128]{3,2,1,0:T(8,128)(2,1)S(1)}, u32[]{:S(2)}, u32[]{:S(2)}) collective-permute-start(bf16[2,2,128,128]{3,2,1,0:T(8,128)(2,1)} %get-tuple-element.47), channel_id=1, source_target_pairs={{0,3},{1,4},{2,5},{3,6},{4,7},{5,0},{6,1},{7,2},{8,11},{9,12},{10,... | collective-permute-start | bytes 393224 | tf_op jit(solution)/shard_map/ppermute | solution.py:339
  11.7 17.5 %collective-permute-start.2 = (bf16[2,2,128,128]{3,2,1,0:T(8,128)(2,1)}, bf16[2,2,128,128]{3,2,1,0:T(8,128)(2,1)S(1)}, u32[]{:S(2)}, u32[]{:S(2)}) collective-permute-start(bf16[2,2,128,128]{3,2,1,0:T(8,128)(2,1)} %get-tuple-element.48), channel_id=1, source_target_pairs={{0,5},{1,6},{2,7},{3,0},{4,1},{5,2},{6,3},{7,4},{8,13},{9,14},{10,... | collective-permute-start | bytes 393224 | tf_op jit(solution)/shard_map/ppermute | solution.py:339
  14.6 14.7 %collective-permute-start.3 = (bf16[2,2,128,128]{3,2,1,0:T(8,128)(2,1)}, bf16[2,2,128,128]{3,2,1,0:T(8,128)(2,1)S(1)}, u32[]{:S(2)}, u32[]{:S(2)}) collective-permute-start(bf16[2,2,128,128]{3,2,1,0:T(8,128)(2,1)} %get-tuple-element.49), channel_id=1, source_target_pairs={{0,2},{1,3},{2,4},{3,5},{4,6},{5,7},{6,0},{7,1},{8,10},{9,11},{10,... | collective-permute-start | bytes 393224 | tf_op jit(solution)/shard_map/ppermute | solution.py:339
  15.8 14.6 %collective-permute-start.4 = (bf16[2,2,128,128]{3,2,1,0:T(8,128)(2,1)}, bf16[2,2,128,128]{3,2,1,0:T(8,128)(2,1)S(1)}, u32[]{:S(2)}, u32[]{:S(2)}) collective-permute-start(bf16[2,2,128,128]{3,2,1,0:T(8,128)(2,1)} %get-tuple-element.50), channel_id=1, source_target_pairs={{0,6},{1,7},{2,0},{3,1},{4,2},{5,3},{6,4},{7,5},{8,14},{9,15},{10,... | collective-permute-start | bytes 393224 | tf_op jit(solution)/shard_map/ppermute | solution.py:339
  18.1 16.1 %copy-start.3 = (bf16[2,2,128,128]{3,2,1,0:T(8,128)(2,1)}, bf16[2,2,128,128]{3,2,1,0:T(8,128)(2,1)S(1)}, u32[]{:S(2)}) copy-start(bf16[2,2,128,128]{3,2,1,0:T(8,128)(2,1)S(1)} %collective-permute-done.refs_4_) | copy-start | bytes 393220
  18.2 15.4 %collective-permute-start.5 = (bf16[2,2,128,128]{3,2,1,0:T(8,128)(2,1)}, bf16[2,2,128,128]{3,2,1,0:T(8,128)(2,1)S(1)}, u32[]{:S(2)}, u32[]{:S(2)}) collective-permute-start(bf16[2,2,128,128]{3,2,1,0:T(8,128)(2,1)} %get-tuple-element.51), channel_id=1, source_target_pairs={{0,1},{1,2},{2,3},{3,4},{4,5},{5,6},{6,7},{7,0},{8,9},{9,10},{10,1... | collective-permute-start | bytes 393224 | tf_op jit(solution)/shard_map/ppermute | solution.py:339
  26.7 7.5 %copy-start.4 = (bf16[2,2,128,128]{3,2,1,0:T(8,128)(2,1)}, bf16[2,2,128,128]{3,2,1,0:T(8,128)(2,1)S(1)}, u32[]{:S(2)}) copy-start(bf16[2,2,128,128]{3,2,1,0:T(8,128)(2,1)S(1)} %collective-permute-done.1.refs_3_) | copy-start | bytes 393220
  26.7 7.5 %collective-permute-start.6 = (bf16[2,2,128,128]{3,2,1,0:T(8,128)(2,1)}, bf16[2,2,128,128]{3,2,1,0:T(8,128)(2,1)S(1)}, u32[]{:S(2)}, u32[]{:S(2)}) collective-permute-start(bf16[2,2,128,128]{3,2,1,0:T(8,128)(2,1)} %get-tuple-element.52), channel_id=1, source_target_pairs={{0,7},{1,0},{2,1},{3,2},{4,3},{5,4},{6,5},{7,6},{8,15},{9,8},{10,9... | collective-permute-start | bytes 393224 | tf_op jit(solution)/shard_map/ppermute | solution.py:339
  29.2 9.6 %copy-start.5 = (bf16[2,2,128,128]{3,2,1,0:T(8,128)(2,1)}, bf16[2,2,128,128]{3,2,1,0:T(8,128)(2,1)S(1)}, u32[]{:S(2)}) copy-start(bf16[2,2,128,128]{3,2,1,0:T(8,128)(2,1)S(1)} %collective-permute-done.2.refs_5_) | copy-start | bytes 393220
  29.3 9.5 %copy-start.6 = (bf16[2,2,128,128]{3,2,1,0:T(8,128)(2,1)}, bf16[2,2,128,128]{3,2,1,0:T(8,128)(2,1)S(1)}, u32[]{:S(2)}) copy-start(bf16[2,2,128,128]{3,2,1,0:T(8,128)(2,1)S(1)} %collective-permute-done.3.refs_2_) | copy-start | bytes 393220
  30.4 8.5 %copy-start.7 = (bf16[2,2,128,128]{3,2,1,0:T(8,128)(2,1)}, bf16[2,2,128,128]{3,2,1,0:T(8,128)(2,1)S(1)}, u32[]{:S(2)}) copy-start(bf16[2,2,128,128]{3,2,1,0:T(8,128)(2,1)S(1)} %collective-permute-done.4.refs_6_) | copy-start | bytes 393220
  33.5 5.3 %copy-start.8 = (bf16[2,2,128,128]{3,2,1,0:T(8,128)(2,1)}, bf16[2,2,128,128]{3,2,1,0:T(8,128)(2,1)S(1)}, u32[]{:S(2)}) copy-start(bf16[2,2,128,128]{3,2,1,0:T(8,128)(2,1)S(1)} %collective-permute-done.5.refs_1_) | copy-start | bytes 393220
  34.2 4.6 %copy-start.9 = (bf16[2,2,128,128]{3,2,1,0:T(8,128)(2,1)}, bf16[2,2,128,128]{3,2,1,0:T(8,128)(2,1)S(1)}, u32[]{:S(2)}) copy-start(bf16[2,2,128,128]{3,2,1,0:T(8,128)(2,1)S(1)} %collective-permute-done.6.refs_7_) | copy-start | bytes 393220
  34.2 33.8 %all-to-all-start = ((bf16[8,2,2,128,128]{4,3,2,1,0:T(8,128)(2,1)}), bf16[8,2,2,128,128]{4,3,2,1,0:T(8,128)(2,1)S(1)}, u32[]{:S(2)}, u32[]{:S(2)}) async-start(bf16[8,2,2,128,128]{4,3,2,1,0:T(8,128)(2,1)} %stack.1), calls=%async_computation | async-start | bytes 2097152 | tf_op jit(solution)/shard_map/all_to_all | solution.py:343
  41.2 18.6 %collective-permute-start.8 = (bf16[8,2,2,128,128]{4,3,2,1,0:T(8,128)(2,1)}, bf16[8,2,2,128,128]{4,3,2,1,0:T(8,128)(2,1)S(1)}, u32[]{:S(2)}, u32[]{:S(2)}) collective-permute-start(bf16[8,2,2,128,128]{4,3,2,1,0:T(8,128)(2,1)} %join.1.own), channel_id=1, source_target_pairs={{8,16},{24,32},{40,48},{56,64},{72,80},{88,96},{104,112},{120,128}... | collective-permute-start | bytes 3145736 | tf_op jit(solution)/shard_map/ppermute | solution.py:332
  44.8 15.0 %collective-permute-start.7 = (bf16[8,2,2,128,128]{4,3,2,1,0:T(8,128)(2,1)}, bf16[8,2,2,128,128]{4,3,2,1,0:T(8,128)(2,1)}, u32[]{:S(2)}, u32[]{:S(2)}) collective-permute-start(bf16[8,2,2,128,128]{4,3,2,1,0:T(8,128)(2,1)} %join.1.own), channel_id=1, source_target_pairs={{0,8},{16,24},{32,40},{48,56},{64,72},{80,88},{96,104},{112,120},{... | collective-permute-start | bytes 3145736 | tf_op jit(solution)/shard_map/ppermute | solution.py:332
  59.8 8.2 %copy-start.17 = (bf16[8,2,2,128,128]{4,3,2,1,0:T(8,128)(2,1)}, bf16[8,2,2,128,128]{4,3,2,1,0:T(8,128)(2,1)S(1)}, u32[]{:S(2)}) copy-start(bf16[8,2,2,128,128]{4,3,2,1,0:T(8,128)(2,1)S(1)} %collective-permute-done.8.link) | copy-start | bytes 3145732
  68.0 1.0 copy-start.2
  85.7 23.2 %copy-start = (f32[8,2,2,128,128]{4,3,2,1,0:T(8,128)S(1)}, f32[8,2,2,128,128]{4,3,2,1,0:T(8,128)}, u32[]{:S(2)}) copy-start(f32[8,2,2,128,128]{4,3,2,1,0:T(8,128)} %get-tuple-element.66.grad_own) | copy-start | bytes 6291460
  85.7 48.5 %all-to-all-start.1 = ((bf16[8,2,2,128,128]{4,3,2,1,0:T(8,128)(2,1)}), bf16[8,2,2,128,128]{4,3,2,1,0:T(8,128)(2,1)}, u32[]{:S(2)}, u32[]{:S(2)}) async-start(bf16[8,2,2,128,128]{4,3,2,1,0:T(8,128)(2,1)} %get-tuple-element.63), calls=%async_computation.1 | async-start | bytes 2097152 | tf_op jit(solution)/shard_map/all_to_all | solution.py:343
  90.1 3.0 %collective-permute-start.9 = (bf16[8,2,2,128,128]{4,3,2,1,0:T(8,128)(2,1)}, bf16[8,2,2,128,128]{4,3,2,1,0:T(8,128)(2,1)S(1)}, u32[]{:S(2)}, u32[]{:S(2)}) collective-permute-start(bf16[8,2,2,128,128]{4,3,2,1,0:T(8,128)(2,1)} %get-tuple-element.67), channel_id=1, source_target_pairs={{0,8},{16,24},{32,40},{48,56},{64,72},{80,88},{96,104},{112,120},{... | collective-permute-start | bytes 3145736 | tf_op jit(solution)/shard_map/ppermute | solution.py:332
  90.2 18.7 %collective-permute-start.10 = (bf16[8,2,2,128,128]{4,3,2,1,0:T(8,128)(2,1)}, bf16[8,2,2,128,128]{4,3,2,1,0:T(8,128)(2,1)S(1)}, u32[]{:S(2)}, u32[]{:S(2)}) collective-permute-start(bf16[8,2,2,128,128]{4,3,2,1,0:T(8,128)(2,1)} %get-tuple-element.68), channel_id=1, source_target_pairs={{8,16},{24,32},{40,48},{56,64},{72,80},{88,96},{104,112},{120,128}... | collective-permute-start | bytes 3145736 | tf_op jit(solution)/shard_map/ppermute | solution.py:332
  109.2 0.7 copy-start.1
  109.9 17.4 %collective-permute-start.11 = (bf16[2,2,128,128]{3,2,1,0:T(8,128)(2,1)S(1)}, bf16[2,2,128,128]{3,2,1,0:T(8,128)(2,1)S(1)}, u32[]{:S(2)}, u32[]{:S(2)}) collective-permute-start(bf16[2,2,128,128]{3,2,1,0:T(8,128)(2,1)S(1)} %get-tuple-element.70), channel_id=1, source_target_pairs={{0,4},{1,5},{2,6},{3,7},{4,0},{5,1},{6,2},{7,3},{8,12},{9,13},{10,... | collective-permute-start | bytes 393224 | tf_op jit(solution)/shard_map/ppermute | solution.py:339
  115.2 12.1 %collective-permute-start.12 = (bf16[2,2,128,128]{3,2,1,0:T(8,128)(2,1)S(1)}, bf16[2,2,128,128]{3,2,1,0:T(8,128)(2,1)S(1)}, u32[]{:S(2)}, u32[]{:S(2)}) collective-permute-start(bf16[2,2,128,128]{3,2,1,0:T(8,128)(2,1)S(1)} %get-tuple-element.71), channel_id=1, source_target_pairs={{0,5},{1,6},{2,7},{3,0},{4,1},{5,2},{6,3},{7,4},{8,13},{9,14},{10,... | collective-permute-start | bytes 393224 | tf_op jit(solution)/shard_map/ppermute | solution.py:339
  115.5 21.2 %collective-permute-start.13 = (bf16[2,2,128,128]{3,2,1,0:T(8,128)(2,1)S(1)}, bf16[2,2,128,128]{3,2,1,0:T(8,128)(2,1)S(1)}, u32[]{:S(2)}, u32[]{:S(2)}) collective-permute-start(bf16[2,2,128,128]{3,2,1,0:T(8,128)(2,1)S(1)} %get-tuple-element.72), channel_id=1, source_target_pairs={{0,3},{1,4},{2,5},{3,6},{4,7},{5,0},{6,1},{7,2},{8,11},{9,12},{10,... | collective-permute-start | bytes 393224 | tf_op jit(solution)/shard_map/ppermute | solution.py:339
  118.5 19.0 %collective-permute-start.14 = (bf16[2,2,128,128]{3,2,1,0:T(8,128)(2,1)S(1)}, bf16[2,2,128,128]{3,2,1,0:T(8,128)(2,1)S(1)}, u32[]{:S(2)}, u32[]{:S(2)}) collective-permute-start(bf16[2,2,128,128]{3,2,1,0:T(8,128)(2,1)S(1)} %get-tuple-element.73), channel_id=1, source_target_pairs={{0,6},{1,7},{2,0},{3,1},{4,2},{5,3},{6,4},{7,5},{8,14},{9,15},{10,... | collective-permute-start | bytes 393224 | tf_op jit(solution)/shard_map/ppermute | solution.py:339
  119.5 17.9 %collective-permute-start.15 = (bf16[2,2,128,128]{3,2,1,0:T(8,128)(2,1)S(1)}, bf16[2,2,128,128]{3,2,1,0:T(8,128)(2,1)S(1)}, u32[]{:S(2)}, u32[]{:S(2)}) collective-permute-start(bf16[2,2,128,128]{3,2,1,0:T(8,128)(2,1)S(1)} %get-tuple-element.74), channel_id=1, source_target_pairs={{0,2},{1,3},{2,4},{3,5},{4,6},{5,7},{6,0},{7,1},{8,10},{9,11},{10,... | collective-permute-start | bytes 393224 | tf_op jit(solution)/shard_map/ppermute | solution.py:339
  127.3 12.5 %copy-start.10 = (bf16[2,2,128,128]{3,2,1,0:T(8,128)(2,1)}, bf16[2,2,128,128]{3,2,1,0:T(8,128)(2,1)S(1)}, u32[]{:S(2)}) copy-start(bf16[2,2,128,128]{3,2,1,0:T(8,128)(2,1)S(1)} %collective-permute-done.11.refs_1_) | copy-start | bytes 393220
  127.3 10.5 %collective-permute-start.16 = (bf16[2,2,128,128]{3,2,1,0:T(8,128)(2,1)S(1)}, bf16[2,2,128,128]{3,2,1,0:T(8,128)(2,1)S(1)}, u32[]{:S(2)}, u32[]{:S(2)}) collective-permute-start(bf16[2,2,128,128]{3,2,1,0:T(8,128)(2,1)S(1)} %get-tuple-element.75), channel_id=1, source_target_pairs={{0,7},{1,0},{2,1},{3,2},{4,3},{5,4},{6,5},{7,6},{8,15},{9,8},{10,9... | collective-permute-start | bytes 393224 | tf_op jit(solution)/shard_map/ppermute | solution.py:339
  127.3 12.5 %copy-start.11 = (bf16[2,2,128,128]{3,2,1,0:T(8,128)(2,1)}, bf16[2,2,128,128]{3,2,1,0:T(8,128)(2,1)S(1)}, u32[]{:S(2)}) copy-start(bf16[2,2,128,128]{3,2,1,0:T(8,128)(2,1)S(1)} %collective-permute-done.12.refs_2_) | copy-start | bytes 393220
  127.4 12.4 %collective-permute-start.17 = (bf16[2,2,128,128]{3,2,1,0:T(8,128)(2,1)S(1)}, bf16[2,2,128,128]{3,2,1,0:T(8,128)(2,1)S(1)}, u32[]{:S(2)}, u32[]{:S(2)}) collective-permute-start(bf16[2,2,128,128]{3,2,1,0:T(8,128)(2,1)S(1)} %get-tuple-element.76), channel_id=1, source_target_pairs={{0,1},{1,2},{2,3},{3,4},{4,5},{5,6},{6,7},{7,0},{8,9},{9,10},{10,1... | collective-permute-start | bytes 393224 | tf_op jit(solution)/shard_map/ppermute | solution.py:339
  136.7 3.1 %copy-start.12 = (bf16[2,2,128,128]{3,2,1,0:T(8,128)(2,1)}, bf16[2,2,128,128]{3,2,1,0:T(8,128)(2,1)S(1)}, u32[]{:S(2)}) copy-start(bf16[2,2,128,128]{3,2,1,0:T(8,128)(2,1)S(1)} %collective-permute-done.13.refs_3_) | copy-start | bytes 393220
  137.5 2.3 %copy-start.13 = (bf16[2,2,128,128]{3,2,1,0:T(8,128)(2,1)}, bf16[2,2,128,128]{3,2,1,0:T(8,128)(2,1)S(1)}, u32[]{:S(2)}) copy-start(bf16[2,2,128,128]{3,2,1,0:T(8,128)(2,1)S(1)} %collective-permute-done.14.refs_4_) | copy-start | bytes 393220
  137.5 2.3 %copy-start.14 = (bf16[2,2,128,128]{3,2,1,0:T(8,128)(2,1)}, bf16[2,2,128,128]{3,2,1,0:T(8,128)(2,1)S(1)}, u32[]{:S(2)}) copy-start(bf16[2,2,128,128]{3,2,1,0:T(8,128)(2,1)S(1)} %collective-permute-done.15.refs_5_) | copy-start | bytes 393220
  137.9 2.0 %copy-start.15 = (bf16[2,2,128,128]{3,2,1,0:T(8,128)(2,1)}, bf16[2,2,128,128]{3,2,1,0:T(8,128)(2,1)S(1)}, u32[]{:S(2)}) copy-start(bf16[2,2,128,128]{3,2,1,0:T(8,128)(2,1)S(1)} %collective-permute-done.16.refs_6_) | copy-start | bytes 393220
  139.8 0.7 copy-start.16

commit v4 on v3

--- a/solution.py
+++ b/solution.py
@@ -36,66 +36,89 @@
         copy.wait()
 
 
-def pack_kernel(spots, *refs):
-    sources, outs, sems = refs[:2], refs[2:-1], refs[-1]
-    n = len(outs)
+def pack_kernel(spots, n, first, second, *refs):
+    outs, (staged, sems, sent) = refs[:n], refs[n:]
     here = lax.axis_index("sp")
-    copies = []
-    for d, out in enumerate(outs):
+    turns = sorted(range(n), key=lambda d: -min(d, n - d))
+    copies = {}
+    for d in turns:
         owner = lax.rem(here + d, n)
-        for i, source in enumerate(sources):
+        copies[d] = []
+        for i, source in enumerate((first, second)):
             for h in range(spots):
                 column = pl.multiple_of((owner * spots + h) * HD, HD)
-                copies.append(
+                copies[d].append(
                     pltpu.make_async_copy(
-                        source.at[:, pl.ds(column, HD)], out.at[h, i], sems.at[d, i, h]
+                        source.at[:, pl.ds(column, HD)], staged.at[d, h, i], sems.at[d, i, h]
                     )
                 )
-    run_copies(copies)
+                copies[d][-1].start()
+    leaving = []
+    for d in turns:
+        for copy in copies[d]:
+            copy.wait()
+        leaving.append(pltpu.make_async_copy(staged.at[d], outs[d], sent.at[d]))
+        leaving[-1].start()
+    for copy in leaving:
+        copy.wait()
 
 
 def pack(first, second, spots):
     rows, width = first.shape
     n = width // (spots * HD)
     return pl.pallas_call(
-        functools.partial(pack_kernel, spots),
+        functools.partial(pack_kernel, spots, n),
         out_shape=[jax.ShapeDtypeStruct((spots, 2, rows, HD), BF16)] * n,
         in_specs=[ANY, ANY],
-        out_specs=[VMEM] * n,
-        scratch_shapes=[pltpu.SemaphoreType.DMA((n, 2, spots))],
+        out_specs=[ANY] * n,
+        scratch_shapes=[
+            pltpu.VMEM((n, spots, 2, rows, HD), BF16),
+            pltpu.SemaphoreType.DMA((n, 2, spots)),
+            pltpu.SemaphoreType.DMA((n,)),
+        ],
         name="pack",
     )(first, second)
 
 
 def unpack_kernel(spots, n, turns, *refs):
-    received, outs, sems = refs[:len(turns)], refs[-3:-1], refs[-1]
+    received, (first, second, staged, sems, sent) = refs[:len(turns)], refs[len(turns):]
     here = lax.axis_index("sp")
-    copies = []
-    for at, (turn, value) in enumerate(zip(turns, received)):
+    arriving = []
+    for at, value in enumerate(received):
+        arriving.append(pltpu.make_async_copy(value, staged.at[at], sems.at[at]))
+        arriving[-1].start()
+    leaving = []
+    for at, turn in enumerate(turns):
         source = lax.rem(here + turn, n)
-        for i, out in enumerate(outs):
+        arriving[at].wait()
+        for i, out in enumerate((first, second)):
             for h in range(spots):
                 column = pl.multiple_of((source * spots + h) * HD, HD)
-                copies.append(
+                leaving.append(
                     pltpu.make_async_copy(
-                        value.at[h, i], out.at[:, pl.ds(column, HD)], sems.at[at, i, h]
+                        staged.at[at, h, i], out.at[:, pl.ds(column, HD)], sent.at[at, i, h]
                     )
                 )
-    run_copies(copies)
-
-
-def unpack(turns, received, n, held=()):
+                leaving[-1].start()
+    for copy in leaving:
+        copy.wait()
+
+
+def unpack(turns, received, n):
     spots, _, rows, _ = received[0].shape
     count = len(turns)
     return pl.pallas_call(
         functools.partial(unpack_kernel, spots, n, turns),
         out_shape=[jax.ShapeDtypeStruct((rows, n * spots * HD), BF16)] * 2,
-        in_specs=[VMEM] * count + [ANY] * len(held),
+        in_specs=[ANY] * count,
         out_specs=[ANY] * 2,
-        input_output_aliases={count + i: i for i in range(len(held))},
-        scratch_shapes=[pltpu.SemaphoreType.DMA((count, 2, spots))],
+        scratch_shapes=[
+            pltpu.VMEM((count, spots, 2, rows, HD), BF16),
+            pltpu.SemaphoreType.DMA((count,)),
+            pltpu.SemaphoreType.DMA((count, 2, spots)),
+        ],
         name="unpack",
-    )(*received, *held)
+    )(*received)
 
 
 def join_kernel(*refs):

time: 144 us -> 143 us (level)
  Pallas kernels: 29.3 us -> 27 us
    pallas_call x1, Pallas kernels: 16.7 us -> 14.9 us  [attention(): pl.pallas_call(functools.partial(attn_kernel, spots, nb), out_shape=[jax....]
  transfers between devices with their start and end apart: 20 -> 20, of which waited for: 12 -> 11; matrix products, arithmetic and copies ran while one was open for 0% -> 0% of each run, Pallas kernels for 5% -> 5%
where the time goes in v4:
time: 143 us; the launch traced here: 141 us
  waiting for transfers between devices  62 us (43%)
  starting transfers between devices  48.9 us (34%)
  Pallas kernels  27 us (19%)
  local copies, waits for them, and re-layouts  2.3 us (2%)
    ppermute x14, starting transfers between devices, turned(): return lax.ppermute(value, 'sp', [(i, (i + steps) % n) for i in range(n)])  32.6 us
    ppermute x4, waiting for transfers between devices, swapped(): return lax.ppermute(value, 'grp', pairs + [(j, i) for i, j in pairs])  30.9 us
    ppermute x14, waiting for transfers between devices, turned(): return lax.ppermute(value, 'sp', [(i, (i + steps) % n) for i in range(n)])  22.9 us
    pallas_call x1, Pallas kernels, attention(): pl.pallas_call(functools.partial(attn_kernel, spots, nb), out_shape=[jax....  14.9 us
    all_to_all x2, starting transfers between devices, exchange(): return lax.all_to_all(value, 'sp', split_axis=0, concat_axis=0, tiled=True)  8.94 us
    all_to_all x2, waiting for transfers between devices, exchange(): return lax.all_to_all(value, 'sp', split_axis=0, concat_axis=0, tiled=True)  8.22 us
    ppermute x4, starting transfers between devices, swapped(): return lax.ppermute(value, 'grp', pairs + [(j, i) for i, j in pairs])  7.34 us
  transfers between devices with their start and end apart: 20, of which 11 were waited for; matrix products, arithmetic and copies ran while one was open for 0% of the time, Pallas kernels for 5%

profile of v4, /device:TPU:29, one launch (start us, length us, event | category | flops | bytes accessed | tf_op | source)
XLA Modules:
  0.0 141.3 jit_solution(9840876376900226265)
XLA Ops:
  0.6 2.2 %pack.1 = (bf16[2,2,128,128]{3,2,1,0:T(8,128)(2,1)}, bf16[2,2,128,128]{3,2,1,0:T(8,128)(2,1)}, bf16[2,2,128,128]{3,2,1,0:T(8,128)(2,1)}, bf16[2,2,128,128]{3,2,1...) custom-call(bf16[128,2048]{1,0:T(8,128)(2,1)} %first.1, ...), custom_call_target="tpu_custom_call" | custom-call | tf_op jit(solution)/shard_map/pack/pallas_call | solution.py:69
  2.9 7.0 %collective-permute-start = (bf16[2,2,128,128]{3,2,1,0:T(8,128)(2,1)}, bf16[2,2,128,128]{3,2,1,0:T(8,128)(2,1)S(1)}, u32[]{:S(2)}, u32[]{:S(2)}) collective-permute-start(bf16[2,2,128,128]{3,2,1,0:T(8,128)(2,1)} %get-tuple-element.46), channel_id=1, source_target_pairs={{0,4},{1,5},{2,6},{3,7},{4,0},{5,1},{6,2},{7,3},{8,12},{9,13},{10,... | collective-permute-start | bytes 393224 | tf_op jit(solution)/shard_map/ppermute | solution.py:362
  9.9 1.6 %collective-permute-start.1 = (bf16[2,2,128,128]{3,2,1,0:T(8,128)(2,1)}, bf16[2,2,128,128]{3,2,1,0:T(8,128)(2,1)S(1)}, u32[]{:S(2)}, u32[]{:S(2)}) collective-permute-start(bf16[2,2,128,128]{3,2,1,0:T(8,128)(2,1)} %get-tuple-element.47), channel_id=1, source_target_pairs={{0,3},{1,4},{2,5},{3,6},{4,7},{5,0},{6,1},{7,2},{8,11},{9,12},{10,... | collective-permute-start | bytes 393224 | tf_op jit(solution)/shard_map/ppermute | solution.py:362
  11.5 2.8 %collective-permute-start.2 = (bf16[2,2,128,128]{3,2,1,0:T(8,128)(2,1)}, bf16[2,2,128,128]{3,2,1,0:T(8,128)(2,1)S(1)}, u32[]{:S(2)}, u32[]{:S(2)}) collective-permute-start(bf16[2,2,128,128]{3,2,1,0:T(8,128)(2,1)} %get-tuple-element.48), channel_id=1, source_target_pairs={{0,5},{1,6},{2,7},{3,0},{4,1},{5,2},{6,3},{7,4},{8,13},{9,14},{10,... | collective-permute-start | bytes 393224 | tf_op jit(solution)/shard_map/ppermute | solution.py:362
  14.3 1.2 collective-permute-start.3
  15.5 2.4 %collective-permute-start.4 = (bf16[2,2,128,128]{3,2,1,0:T(8,128)(2,1)}, bf16[2,2,128,128]{3,2,1,0:T(8,128)(2,1)S(1)}, u32[]{:S(2)}, u32[]{:S(2)}) collective-permute-start(bf16[2,2,128,128]{3,2,1,0:T(8,128)(2,1)} %get-tuple-element.50), channel_id=1, source_target_pairs={{0,6},{1,7},{2,0},{3,1},{4,2},{5,3},{6,4},{7,5},{8,14},{9,15},{10,... | collective-permute-start | bytes 393224 | tf_op jit(solution)/shard_map/ppermute | solution.py:362
  17.9 0.0 collective-permute-done.refs_4_
  17.9 0.7 collective-permute-start.5
  18.6 7.8 %collective-permute-done.1.refs_3_ = bf16[2,2,128,128]{3,2,1,0:T(8,128)(2,1)S(1)} collective-permute-done((bf16[2,2,128,128]{3,2,1,0:T(8,128)(2,1)}, bf16[2,2,128,128]{3,2,1,0:T(8,128)(2,1)S(1)}, u32[]{:S(2)}, u32[]{:S(2)}) %collective-permute-start.1) | collective-permute-done | bytes 131104 | tf_op jit(solution)/shard_map/ppermute | solution.py:362
  26.5 0.0 collective-permute-start.6
  26.5 2.5 %stack.1 = bf16[8,2,2,128,128]{4,3,2,1,0:T(8,128)(2,1)} custom-call(bf16[128,2048]{1,0:T(8,128)(2,1)} %refs_0_, bf16[128,2048]{1,0:T(8,128)(2,1)} %refs_1_), custom_call_target="tpu_custom_call" | custom-call | tf_op jit(solution)/shard_map/stack/pallas_call | solution.py:162
  29.0 0.0 collective-permute-done.2.refs_5_
  29.0 0.0 copy-start.5
  29.0 0.0 collective-permute-done.3.refs_2_
  29.0 0.0 copy-start.6
  29.0 1.1 collective-permute-done.4.refs_6_
  30.1 3.2 %collective-permute-done.5.refs_1_ = bf16[2,2,128,128]{3,2,1,0:T(8,128)(2,1)S(1)} collective-permute-done((bf16[2,2,128,128]{3,2,1,0:T(8,128)(2,1)}, bf16[2,2,128,128]{3,2,1,0:T(8,128)(2,1)S(1)}, u32[]{:S(2)}, u32[]{:S(2)}) %collective-permute-start.5) | collective-permute-done | bytes 131104 | tf_op jit(solution)/shard_map/ppermute | solution.py:362
  33.3 0.7 collective-permute-done.6.refs_7_
  34.0 0.0 copy-done.3
  34.0 0.0 copy-done.4
  34.0 4.6 %all-to-all-start = ((bf16[8,2,2,128,128]{4,3,2,1,0:T(8,128)(2,1)}), bf16[8,2,2,128,128]{4,3,2,1,0:T(8,128)(2,1)S(1)}, u32[]{:S(2)}, u32[]{:S(2)}) async-start(bf16[8,2,2,128,128]{4,3,2,1,0:T(8,128)(2,1)} %stack.1), calls=%async_computation | async-start | bytes 2097152 | tf_op jit(solution)/shard_map/all_to_all | solution.py:366
  38.6 0.0 copy-done.5
  38.6 0.0 copy-done.6
  38.6 0.0 copy-done.7
  38.6 0.0 copy-done.8
  38.6 0.0 copy-done.9
  38.6 2.3 %join.1.own = bf16[8,2,2,128,128]{4,3,2,1,0:T(8,128)(2,1)} custom-call(bf16[2,2,128,128]{3,2,1,0:T(8,128)(2,1)} %get-tuple-element.45.refs_0_, bf16[2,2,128,128]{3,2,1,0:T(8,128)(2,1)} %copy-done.8, bf16[2,2,128,128]{3,2,1,0:T(8,128)(2,1)} %copy-done.6, bf16[2,2,128,128]{3,2,1,0:T(8,128)(2,1)} %copy-done.4, bf16[2,2,128,128]{3,2,1,0:T(8,128)(2,1)} %copy-done.3, ...), custom_call_target="tpu_custom_call" | custom-call | tf_op jit(solution)/shard_map/join/pallas_call | solution.py:208
  40.9 3.6 %collective-permute-start.8 = (bf16[8,2,2,128,128]{4,3,2,1,0:T(8,128)(2,1)}, bf16[8,2,2,128,128]{4,3,2,1,0:T(8,128)(2,1)S(1)}, u32[]{:S(2)}, u32[]{:S(2)}) collective-permute-start(bf16[8,2,2,128,128]{4,3,2,1,0:T(8,128)(2,1)} %join.1.own), channel_id=1, source_target_pairs={{8,16},{24,32},{40,48},{56,64},{72,80},{88,96},{104,112},{120,128}... | collective-permute-start | bytes 3145736 | tf_op jit(solution)/shard_map/ppermute | solution.py:355
  44.6 0.1 collective-permute-start.7
  44.7 14.9 %collective-permute-done.8.link = bf16[8,2,2,128,128]{4,3,2,1,0:T(8,128)(2,1)S(1)} collective-permute-done((bf16[8,2,2,128,128]{4,3,2,1,0:T(8,128)(2,1)}, bf16[8,2,2,128,128]{4,3,2,1,0:T(8,128)(2,1)S(1)}, u32[]{:S(2)}, u32[]{:S(2)}) %collective-permute-start.8) | collective-permute-done | bytes 1048608 | tf_op jit(solution)/shard_map/ppermute | solution.py:355
  59.5 0.0 collective-permute-done.7.chip
  59.5 8.2 %all-to-all-done.rows_in = bf16[8,2,2,128,128]{4,3,2,1,0:T(8,128)(2,1)S(1)} async-done(((bf16[8,2,2,128,128]{4,3,2,1,0:T(8,128)(2,1)}), bf16[8,2,2,128,128]{4,3,2,1,0:T(8,128)(2,1)S(1)}, u32[]{:S(2)}, u32[]{:S(2)}) %all-to-all-start) | async-done | bytes 1048608 | tf_op jit(solution)/shard_map/all_to_all | solution.py:366
  67.8 0.0 copy-done.17
  67.8 1.0 copy-done.2
  68.7 14.9 %attention.1 = (bf16[8,2,2,128,128]{4,3,2,1,0:T(8,128)(2,1)}, bf16[8,2,2,128,128]{4,3,2,1,0:T(8,128)(2,1)}, f32[8,2,2,128,128]{4,3,2,1,0:T(8,128)}, bf16[8,2,2,128,128]{4,3,2,1,0:T(8,128)(2,1)}) custom-call(s32[8,8]{1,0:T(8,128)} %ids.1, s32[8]{0:T(128)} %counts.1, bf16[8,2,2,128,128]{4,3,2,1,0:T(8,128)(2,1)} %collective-permute-done.7.chip, ...), custom_call_target="tpu_custom_call" | custom-call | flops 3221225472 | bytes 10485760 | tf_op jit(solution)/shard_map/attention/pallas_call | solution.py:305
  83.6 0.0 copy-start
  83.6 4.4 %all-to-all-start.1 = ((bf16[8,2,2,128,128]{4,3,2,1,0:T(8,128)(2,1)}), bf16[8,2,2,128,128]{4,3,2,1,0:T(8,128)(2,1)}, u32[]{:S(2)}, u32[]{:S(2)}) async-start(bf16[8,2,2,128,128]{4,3,2,1,0:T(8,128)(2,1)} %get-tuple-element.63), calls=%async_computation.1 | async-start | bytes 2097152 | tf_op jit(solution)/shard_map/all_to_all | solution.py:366
  88.0 1.1 collective-permute-start.9
  89.0 2.6 %collective-permute-start.10 = (bf16[8,2,2,128,128]{4,3,2,1,0:T(8,128)(2,1)}, bf16[8,2,2,128,128]{4,3,2,1,0:T(8,128)(2,1)S(1)}, u32[]{:S(2)}, u32[]{:S(2)}) collective-permute-start(bf16[8,2,2,128,128]{4,3,2,1,0:T(8,128)(2,1)} %get-tuple-element.68), channel_id=1, source_target_pairs={{8,16},{24,32},{40,48},{56,64},{72,80},{88,96},{104,112},{120,128}... | collective-permute-start | bytes 3145736 | tf_op jit(solution)/shard_map/ppermute | solution.py:355
  91.6 0.0 collective-permute-done.9.first
  91.7 16.1 %collective-permute-done.10.second = bf16[8,2,2,128,128]{4,3,2,1,0:T(8,128)(2,1)S(1)} collective-permute-done((bf16[8,2,2,128,128]{4,3,2,1,0:T(8,128)(2,1)}, bf16[8,2,2,128,128]{4,3,2,1,0:T(8,128)(2,1)S(1)}, u32[]{:S(2)}, u32[]{:S(2)}) %collective-permute-start.10) | collective-permute-done | bytes 1048608 | tf_op jit(solution)/shard_map/ppermute | solution.py:355
  107.7 0.0 copy-done
  107.7 0.3 settle.1
  108.1 0.0 copy-start.1
  108.1 0.6 copy-done.1
  108.7 5.6 %collective-permute-start.11 = (bf16[2,2,128,128]{3,2,1,0:T(8,128)(2,1)S(1)}, bf16[2,2,128,128]{3,2,1,0:T(8,128)(2,1)S(1)}, u32[]{:S(2)}, u32[]{:S(2)}) collective-permute-start(bf16[2,2,128,128]{3,2,1,0:T(8,128)(2,1)S(1)} %get-tuple-element.70), channel_id=1, source_target_pairs={{0,4},{1,5},{2,6},{3,7},{4,0},{5,1},{6,2},{7,3},{8,12},{9,13},{10,... | collective-permute-start | bytes 393224 | tf_op jit(solution)/shard_map/ppermute | solution.py:362
  114.3 0.3 collective-permute-start.12
  114.6 3.0 %collective-permute-start.13 = (bf16[2,2,128,128]{3,2,1,0:T(8,128)(2,1)S(1)}, bf16[2,2,128,128]{3,2,1,0:T(8,128)(2,1)S(1)}, u32[]{:S(2)}, u32[]{:S(2)}) collective-permute-start(bf16[2,2,128,128]{3,2,1,0:T(8,128)(2,1)S(1)} %get-tuple-element.72), channel_id=1, source_target_pairs={{0,3},{1,4},{2,5},{3,6},{4,7},{5,0},{6,1},{7,2},{8,11},{9,12},{10,... | collective-permute-start | bytes 393224 | tf_op jit(solution)/shard_map/ppermute | solution.py:362
  117.6 1.5 %collective-permute-start.14 = (bf16[2,2,128,128]{3,2,1,0:T(8,128)(2,1)S(1)}, bf16[2,2,128,128]{3,2,1,0:T(8,128)(2,1)S(1)}, u32[]{:S(2)}, u32[]{:S(2)}) collective-permute-start(bf16[2,2,128,128]{3,2,1,0:T(8,128)(2,1)S(1)} %get-tuple-element.73), channel_id=1, source_target_pairs={{0,6},{1,7},{2,0},{3,1},{4,2},{5,3},{6,4},{7,5},{8,14},{9,15},{10,... | collective-permute-start | bytes 393224 | tf_op jit(solution)/shard_map/ppermute | solution.py:362
  119.1 0.9 collective-permute-start.15
  120.0 5.0 %collective-permute-done.11.refs_1_ = bf16[2,2,128,128]{3,2,1,0:T(8,128)(2,1)S(1)} collective-permute-done((bf16[2,2,128,128]{3,2,1,0:T(8,128)(2,1)S(1)}, bf16[2,2,128,128]{3,2,1,0:T(8,128)(2,1)S(1)}, u32[]{:S(2)}, u32[]{:S(2)}) %collective-permute-start.11) | collective-permute-done | bytes 131104 | tf_op jit(solution)/shard_map/ppermute | solution.py:362
  125.0 0.0 collective-permute-start.16
  125.0 2.8 %collective-permute-done.12.refs_2_ = bf16[2,2,128,128]{3,2,1,0:T(8,128)(2,1)S(1)} collective-permute-done((bf16[2,2,128,128]{3,2,1,0:T(8,128)(2,1)S(1)}, bf16[2,2,128,128]{3,2,1,0:T(8,128)(2,1)S(1)}, u32[]{:S(2)}, u32[]{:S(2)}) %collective-permute-start.12) | collective-permute-done | bytes 131104 | tf_op jit(solution)/shard_map/ppermute | solution.py:362
  127.8 5.6 %collective-permute-start.17 = (bf16[2,2,128,128]{3,2,1,0:T(8,128)(2,1)S(1)}, bf16[2,2,128,128]{3,2,1,0:T(8,128)(2,1)S(1)}, u32[]{:S(2)}, u32[]{:S(2)}) collective-permute-start(bf16[2,2,128,128]{3,2,1,0:T(8,128)(2,1)S(1)} %get-tuple-element.76), channel_id=1, source_target_pairs={{0,1},{1,2},{2,3},{3,4},{4,5},{5,6},{6,7},{7,0},{8,9},{9,10},{10,1... | collective-permute-start | bytes 393224 | tf_op jit(solution)/shard_map/ppermute | solution.py:362
  133.4 0.0 all-to-all-done.1.value
  133.4 2.5 %unstack.1 = (bf16[128,2048]{1,0:T(8,128)(2,1)}, bf16[128,2048]{1,0:T(8,128)(2,1)}) custom-call(bf16[8,2,2,128,128]{4,3,2,1,0:T(8,128)(2,1)} %all-to-all-done.1.value), custom_call_target="tpu_custom_call" | custom-call | tf_op jit(solution)/shard_map/unstack/pallas_call | solution.py:189
  135.8 0.0 collective-permute-done.13.refs_3_
  135.9 0.0 copy-start.12
  135.9 0.0 collective-permute-done.14.refs_4_
  135.9 0.0 collective-permute-done.15.refs_5_
  135.9 0.4 collective-permute-done.16.refs_6_
  136.3 1.9 %collective-permute-done.17.refs_7_ = bf16[2,2,128,128]{3,2,1,0:T(8,128)(2,1)S(1)} collective-permute-done((bf16[2,2,128,128]{3,2,1,0:T(8,128)(2,1)S(1)}, bf16[2,2,128,128]{3,2,1,0:T(8,128)(2,1)S(1)}, u32[]{:S(2)}, u32[]{:S(2)}) %collective-permute-start.17) | collective-permute-done | bytes 131104 | tf_op jit(solution)/shard_map/ppermute | solution.py:362
  138.2 0.6 copy-done.16
  138.8 2.3 %unpack.1 = (bf16[128,2048]{1,0:T(8,128)(2,1)}, bf16[128,2048]{1,0:T(8,128)(2,1)}) custom-call(bf16[2,2,128,128]{3,2,1,0:T(8,128)(2,1)} %copy-done.1, bf16[2,2,128,128]{3,2,1,0:T(8,128)(2,1)} %copy-done.10, bf16[2,2,128,128]{3,2,1,0:T(8,128)(2,1)} %copy-done.11, bf16[2,2,128,128]{3,2,1,0:T(8,128)(2,1)} %copy-done.12, bf16[2,2,128,128]{3,2,1,0:T(8,128)(2,1)} %copy-done.13, ...), custom_call_target="tpu_custom_call" | custom-call | tf_op jit(solution)/shard_map/unpack/pallas_call | solution.py:110
  (19 shorter events, 0.0 us)
Async XLA Ops:
  2.9 15.1 %collective-permute-start = (bf16[2,2,128,128]{3,2,1,0:T(8,128)(2,1)}, bf16[2,2,128,128]{3,2,1,0:T(8,128)(2,1)S(1)}, u32[]{:S(2)}, u32[]{:S(2)}) collective-permute-start(bf16[2,2,128,128]{3,2,1,0:T(8,128)(2,1)} %get-tuple-element.46), channel_id=1, source_target_pairs={{0,4},{1,5},{2,6},{3,7},{4,0},{5,1},{6,2},{7,3},{8,12},{9,13},{10,... | collective-permute-start | bytes 393224 | tf_op jit(solution)/shard_map/ppermute | solution.py:362
  9.9 16.6 %collective-permute-start.1 = (bf16[2,2,128,128]{3,2,1,0:T(8,128)(2,1)}, bf16[2,2,128,128]{3,2,1,0:T(8,128)(2,1)S(1)}, u32[]{:S(2)}, u32[]{:S(2)}) collective-permute-start(bf16[2,2,128,128]{3,2,1,0:T(8,128)(2,1)} %get-tuple-element.47), channel_id=1, source_target_pairs={{0,3},{1,4},{2,5},{3,6},{4,7},{5,0},{6,1},{7,2},{8,11},{9,12},{10,... | collective-permute-start | bytes 393224 | tf_op jit(solution)/shard_map/ppermute | solution.py:362
  11.5 17.5 %collective-permute-start.2 = (bf16[2,2,128,128]{3,2,1,0:T(8,128)(2,1)}, bf16[2,2,128,128]{3,2,1,0:T(8,128)(2,1)S(1)}, u32[]{:S(2)}, u32[]{:S(2)}) collective-permute-start(bf16[2,2,128,128]{3,2,1,0:T(8,128)(2,1)} %get-tuple-element.48), channel_id=1, source_target_pairs={{0,5},{1,6},{2,7},{3,0},{4,1},{5,2},{6,3},{7,4},{8,13},{9,14},{10,... | collective-permute-start | bytes 393224 | tf_op jit(solution)/shard_map/ppermute | solution.py:362
  14.3 14.7 %collective-permute-start.3 = (bf16[2,2,128,128]{3,2,1,0:T(8,128)(2,1)}, bf16[2,2,128,128]{3,2,1,0:T(8,128)(2,1)S(1)}, u32[]{:S(2)}, u32[]{:S(2)}) collective-permute-start(bf16[2,2,128,128]{3,2,1,0:T(8,128)(2,1)} %get-tuple-element.49), channel_id=1, source_target_pairs={{0,2},{1,3},{2,4},{3,5},{4,6},{5,7},{6,0},{7,1},{8,10},{9,11},{10,... | collective-permute-start | bytes 393224 | tf_op jit(solution)/shard_map/ppermute | solution.py:362
  15.5 14.6 %collective-permute-start.4 = (bf16[2,2,128,128]{3,2,1,0:T(8,128)(2,1)}, bf16[2,2,128,128]{3,2,1,0:T(8,128)(2,1)S(1)}, u32[]{:S(2)}, u32[]{:S(2)}) collective-permute-start(bf16[2,2,128,128]{3,2,1,0:T(8,128)(2,1)} %get-tuple-element.50), channel_id=1, source_target_pairs={{0,6},{1,7},{2,0},{3,1},{4,2},{5,3},{6,4},{7,5},{8,14},{9,15},{10,... | collective-permute-start | bytes 393224 | tf_op jit(solution)/shard_map/ppermute | solution.py:362
  17.9 16.1 %copy-start.3 = (bf16[2,2,128,128]{3,2,1,0:T(8,128)(2,1)}, bf16[2,2,128,128]{3,2,1,0:T(8,128)(2,1)S(1)}, u32[]{:S(2)}) copy-start(bf16[2,2,128,128]{3,2,1,0:T(8,128)(2,1)S(1)} %collective-permute-done.refs_4_) | copy-start | bytes 393220
  17.9 15.4 %collective-permute-start.5 = (bf16[2,2,128,128]{3,2,1,0:T(8,128)(2,1)}, bf16[2,2,128,128]{3,2,1,0:T(8,128)(2,1)S(1)}, u32[]{:S(2)}, u32[]{:S(2)}) collective-permute-start(bf16[2,2,128,128]{3,2,1,0:T(8,128)(2,1)} %get-tuple-element.51), channel_id=1, source_target_pairs={{0,1},{1,2},{2,3},{3,4},{4,5},{5,6},{6,7},{7,0},{8,9},{9,10},{10,1... | collective-permute-start | bytes 393224 | tf_op jit(solution)/shard_map/ppermute | solution.py:362
  26.5 7.5 %copy-start.4 = (bf16[2,2,128,128]{3,2,1,0:T(8,128)(2,1)}, bf16[2,2,128,128]{3,2,1,0:T(8,128)(2,1)S(1)}, u32[]{:S(2)}) copy-start(bf16[2,2,128,128]{3,2,1,0:T(8,128)(2,1)S(1)} %collective-permute-done.1.refs_3_) | copy-start | bytes 393220
  26.5 7.5 %collective-permute-start.6 = (bf16[2,2,128,128]{3,2,1,0:T(8,128)(2,1)}, bf16[2,2,128,128]{3,2,1,0:T(8,128)(2,1)S(1)}, u32[]{:S(2)}, u32[]{:S(2)}) collective-permute-start(bf16[2,2,128,128]{3,2,1,0:T(8,128)(2,1)} %get-tuple-element.52), channel_id=1, source_target_pairs={{0,7},{1,0},{2,1},{3,2},{4,3},{5,4},{6,5},{7,6},{8,15},{9,8},{10,9... | collective-permute-start | bytes 393224 | tf_op jit(solution)/shard_map/ppermute | solution.py:362
  29.0 9.6 %copy-start.5 = (bf16[2,2,128,128]{3,2,1,0:T(8,128)(2,1)}, bf16[2,2,128,128]{3,2,1,0:T(8,128)(2,1)S(1)}, u32[]{:S(2)}) copy-start(bf16[2,2,128,128]{3,2,1,0:T(8,128)(2,1)S(1)} %collective-permute-done.2.refs_5_) | copy-start | bytes 393220
  29.0 9.5 %copy-start.6 = (bf16[2,2,128,128]{3,2,1,0:T(8,128)(2,1)}, bf16[2,2,128,128]{3,2,1,0:T(8,128)(2,1)S(1)}, u32[]{:S(2)}) copy-start(bf16[2,2,128,128]{3,2,1,0:T(8,128)(2,1)S(1)} %collective-permute-done.3.refs_2_) | copy-start | bytes 393220
  30.1 8.5 %copy-start.7 = (bf16[2,2,128,128]{3,2,1,0:T(8,128)(2,1)}, bf16[2,2,128,128]{3,2,1,0:T(8,128)(2,1)S(1)}, u32[]{:S(2)}) copy-start(bf16[2,2,128,128]{3,2,1,0:T(8,128)(2,1)S(1)} %collective-permute-done.4.refs_6_) | copy-start | bytes 393220
  33.3 5.3 %copy-start.8 = (bf16[2,2,128,128]{3,2,1,0:T(8,128)(2,1)}, bf16[2,2,128,128]{3,2,1,0:T(8,128)(2,1)S(1)}, u32[]{:S(2)}) copy-start(bf16[2,2,128,128]{3,2,1,0:T(8,128)(2,1)S(1)} %collective-permute-done.5.refs_1_) | copy-start | bytes 393220
  34.0 4.6 %copy-start.9 = (bf16[2,2,128,128]{3,2,1,0:T(8,128)(2,1)}, bf16[2,2,128,128]{3,2,1,0:T(8,128)(2,1)S(1)}, u32[]{:S(2)}) copy-start(bf16[2,2,128,128]{3,2,1,0:T(8,128)(2,1)S(1)} %collective-permute-done.6.refs_7_) | copy-start | bytes 393220
  34.0 33.8 %all-to-all-start = ((bf16[8,2,2,128,128]{4,3,2,1,0:T(8,128)(2,1)}), bf16[8,2,2,128,128]{4,3,2,1,0:T(8,128)(2,1)S(1)}, u32[]{:S(2)}, u32[]{:S(2)}) async-start(bf16[8,2,2,128,128]{4,3,2,1,0:T(8,128)(2,1)} %stack.1), calls=%async_computation | async-start | bytes 2097152 | tf_op jit(solution)/shard_map/all_to_all | solution.py:366
  40.9 18.6 %collective-permute-start.8 = (bf16[8,2,2,128,128]{4,3,2,1,0:T(8,128)(2,1)}, bf16[8,2,2,128,128]{4,3,2,1,0:T(8,128)(2,1)S(1)}, u32[]{:S(2)}, u32[]{:S(2)}) collective-permute-start(bf16[8,2,2,128,128]{4,3,2,1,0:T(8,128)(2,1)} %join.1.own), channel_id=1, source_target_pairs={{8,16},{24,32},{40,48},{56,64},{72,80},{88,96},{104,112},{120,128}... | collective-permute-start | bytes 3145736 | tf_op jit(solution)/shard_map/ppermute | solution.py:355
  44.6 15.0 %collective-permute-start.7 = (bf16[8,2,2,128,128]{4,3,2,1,0:T(8,128)(2,1)}, bf16[8,2,2,128,128]{4,3,2,1,0:T(8,128)(2,1)}, u32[]{:S(2)}, u32[]{:S(2)}) collective-permute-start(bf16[8,2,2,128,128]{4,3,2,1,0:T(8,128)(2,1)} %join.1.own), channel_id=1, source_target_pairs={{0,8},{16,24},{32,40},{48,56},{64,72},{80,88},{96,104},{112,120},{... | collective-permute-start | bytes 3145736 | tf_op jit(solution)/shard_map/ppermute | solution.py:355
  59.5 8.2 %copy-start.17 = (bf16[8,2,2,128,128]{4,3,2,1,0:T(8,128)(2,1)}, bf16[8,2,2,128,128]{4,3,2,1,0:T(8,128)(2,1)S(1)}, u32[]{:S(2)}) copy-start(bf16[8,2,2,128,128]{4,3,2,1,0:T(8,128)(2,1)S(1)} %collective-permute-done.8.link) | copy-start | bytes 3145732
  67.8 1.0 copy-start.2
  83.6 24.1 %copy-start = (f32[8,2,2,128,128]{4,3,2,1,0:T(8,128)S(1)}, f32[8,2,2,128,128]{4,3,2,1,0:T(8,128)}, u32[]{:S(2)}) copy-start(f32[8,2,2,128,128]{4,3,2,1,0:T(8,128)} %get-tuple-element.66.grad_own) | copy-start | bytes 6291460
  83.6 49.8 %all-to-all-start.1 = ((bf16[8,2,2,128,128]{4,3,2,1,0:T(8,128)(2,1)}), bf16[8,2,2,128,128]{4,3,2,1,0:T(8,128)(2,1)}, u32[]{:S(2)}, u32[]{:S(2)}) async-start(bf16[8,2,2,128,128]{4,3,2,1,0:T(8,128)(2,1)} %get-tuple-element.63), calls=%async_computation.1 | async-start | bytes 2097152 | tf_op jit(solution)/shard_map/all_to_all | solution.py:366
  88.0 3.6 %collective-permute-start.9 = (bf16[8,2,2,128,128]{4,3,2,1,0:T(8,128)(2,1)}, bf16[8,2,2,128,128]{4,3,2,1,0:T(8,128)(2,1)S(1)}, u32[]{:S(2)}, u32[]{:S(2)}) collective-permute-start(bf16[8,2,2,128,128]{4,3,2,1,0:T(8,128)(2,1)} %get-tuple-element.67), channel_id=1, source_target_pairs={{0,8},{16,24},{32,40},{48,56},{64,72},{80,88},{96,104},{112,120},{... | collective-permute-start | bytes 3145736 | tf_op jit(solution)/shard_map/ppermute | solution.py:355
  89.0 18.7 %collective-permute-start.10 = (bf16[8,2,2,128,128]{4,3,2,1,0:T(8,128)(2,1)}, bf16[8,2,2,128,128]{4,3,2,1,0:T(8,128)(2,1)S(1)}, u32[]{:S(2)}, u32[]{:S(2)}) collective-permute-start(bf16[8,2,2,128,128]{4,3,2,1,0:T(8,128)(2,1)} %get-tuple-element.68), channel_id=1, source_target_pairs={{8,16},{24,32},{40,48},{56,64},{72,80},{88,96},{104,112},{120,128}... | collective-permute-start | bytes 3145736 | tf_op jit(solution)/shard_map/ppermute | solution.py:355
  108.1 0.7 copy-start.1
  108.7 16.2 %collective-permute-start.11 = (bf16[2,2,128,128]{3,2,1,0:T(8,128)(2,1)S(1)}, bf16[2,2,128,128]{3,2,1,0:T(8,128)(2,1)S(1)}, u32[]{:S(2)}, u32[]{:S(2)}) collective-permute-start(bf16[2,2,128,128]{3,2,1,0:T(8,128)(2,1)S(1)} %get-tuple-element.70), channel_id=1, source_target_pairs={{0,4},{1,5},{2,6},{3,7},{4,0},{5,1},{6,2},{7,3},{8,12},{9,13},{10,... | collective-permute-start | bytes 393224 | tf_op jit(solution)/shard_map/ppermute | solution.py:362
  114.3 13.4 %collective-permute-start.12 = (bf16[2,2,128,128]{3,2,1,0:T(8,128)(2,1)S(1)}, bf16[2,2,128,128]{3,2,1,0:T(8,128)(2,1)S(1)}, u32[]{:S(2)}, u32[]{:S(2)}) collective-permute-start(bf16[2,2,128,128]{3,2,1,0:T(8,128)(2,1)S(1)} %get-tuple-element.71), channel_id=1, source_target_pairs={{0,5},{1,6},{2,7},{3,0},{4,1},{5,2},{6,3},{7,4},{8,13},{9,14},{10,... | collective-permute-start | bytes 393224 | tf_op jit(solution)/shard_map/ppermute | solution.py:362
  114.6 21.3 %collective-permute-start.13 = (bf16[2,2,128,128]{3,2,1,0:T(8,128)(2,1)S(1)}, bf16[2,2,128,128]{3,2,1,0:T(8,128)(2,1)S(1)}, u32[]{:S(2)}, u32[]{:S(2)}) collective-permute-start(bf16[2,2,128,128]{3,2,1,0:T(8,128)(2,1)S(1)} %get-tuple-element.72), channel_id=1, source_target_pairs={{0,3},{1,4},{2,5},{3,6},{4,7},{5,0},{6,1},{7,2},{8,11},{9,12},{10,... | collective-permute-start | bytes 393224 | tf_op jit(solution)/shard_map/ppermute | solution.py:362
  117.6 18.3 %collective-permute-start.14 = (bf16[2,2,128,128]{3,2,1,0:T(8,128)(2,1)S(1)}, bf16[2,2,128,128]{3,2,1,0:T(8,128)(2,1)S(1)}, u32[]{:S(2)}, u32[]{:S(2)}) collective-permute-start(bf16[2,2,128,128]{3,2,1,0:T(8,128)(2,1)S(1)} %get-tuple-element.73), channel_id=1, source_target_pairs={{0,6},{1,7},{2,0},{3,1},{4,2},{5,3},{6,4},{7,5},{8,14},{9,15},{10,... | collective-permute-start | bytes 393224 | tf_op jit(solution)/shard_map/ppermute | solution.py:362
  119.1 16.8 %collective-permute-start.15 = (bf16[2,2,128,128]{3,2,1,0:T(8,128)(2,1)S(1)}, bf16[2,2,128,128]{3,2,1,0:T(8,128)(2,1)S(1)}, u32[]{:S(2)}, u32[]{:S(2)}) collective-permute-start(bf16[2,2,128,128]{3,2,1,0:T(8,128)(2,1)S(1)} %get-tuple-element.74), channel_id=1, source_target_pairs={{0,2},{1,3},{2,4},{3,5},{4,6},{5,7},{6,0},{7,1},{8,10},{9,11},{10,... | collective-permute-start | bytes 393224 | tf_op jit(solution)/shard_map/ppermute | solution.py:362
  125.0 13.2 %copy-start.10 = (bf16[2,2,128,128]{3,2,1,0:T(8,128)(2,1)}, bf16[2,2,128,128]{3,2,1,0:T(8,128)(2,1)S(1)}, u32[]{:S(2)}) copy-start(bf16[2,2,128,128]{3,2,1,0:T(8,128)(2,1)S(1)} %collective-permute-done.11.refs_1_) | copy-start | bytes 393220
  125.0 11.3 %collective-permute-start.16 = (bf16[2,2,128,128]{3,2,1,0:T(8,128)(2,1)S(1)}, bf16[2,2,128,128]{3,2,1,0:T(8,128)(2,1)S(1)}, u32[]{:S(2)}, u32[]{:S(2)}) collective-permute-start(bf16[2,2,128,128]{3,2,1,0:T(8,128)(2,1)S(1)} %get-tuple-element.75), channel_id=1, source_target_pairs={{0,7},{1,0},{2,1},{3,2},{4,3},{5,4},{6,5},{7,6},{8,15},{9,8},{10,9... | collective-permute-start | bytes 393224 | tf_op jit(solution)/shard_map/ppermute | solution.py:362
  127.8 10.4 %copy-start.11 = (bf16[2,2,128,128]{3,2,1,0:T(8,128)(2,1)}, bf16[2,2,128,128]{3,2,1,0:T(8,128)(2,1)S(1)}, u32[]{:S(2)}) copy-start(bf16[2,2,128,128]{3,2,1,0:T(8,128)(2,1)S(1)} %collective-permute-done.12.refs_2_) | copy-start | bytes 393220
  127.8 10.4 %collective-permute-start.17 = (bf16[2,2,128,128]{3,2,1,0:T(8,128)(2,1)S(1)}, bf16[2,2,128,128]{3,2,1,0:T(8,128)(2,1)S(1)}, u32[]{:S(2)}, u32[]{:S(2)}) collective-permute-start(bf16[2,2,128,128]{3,2,1,0:T(8,128)(2,1)S(1)} %get-tuple-element.76), channel_id=1, source_target_pairs={{0,1},{1,2},{2,3},{3,4},{4,5},{5,6},{6,7},{7,0},{8,9},{9,10},{10,1... | collective-permute-start | bytes 393224 | tf_op jit(solution)/shard_map/ppermute | solution.py:362
  135.9 2.3 %copy-start.12 = (bf16[2,2,128,128]{3,2,1,0:T(8,128)(2,1)}, bf16[2,2,128,128]{3,2,1,0:T(8,128)(2,1)S(1)}, u32[]{:S(2)}) copy-start(bf16[2,2,128,128]{3,2,1,0:T(8,128)(2,1)S(1)} %collective-permute-done.13.refs_3_) | copy-start | bytes 393220
  135.9 2.3 %copy-start.13 = (bf16[2,2,128,128]{3,2,1,0:T(8,128)(2,1)}, bf16[2,2,128,128]{3,2,1,0:T(8,128)(2,1)S(1)}, u32[]{:S(2)}) copy-start(bf16[2,2,128,128]{3,2,1,0:T(8,128)(2,1)S(1)} %collective-permute-done.14.refs_4_) | copy-start | bytes 393220
  135.9 2.3 %copy-start.14 = (bf16[2,2,128,128]{3,2,1,0:T(8,128)(2,1)}, bf16[2,2,128,128]{3,2,1,0:T(8,128)(2,1)S(1)}, u32[]{:S(2)}) copy-start(bf16[2,2,128,128]{3,2,1,0:T(8,128)(2,1)S(1)} %collective-permute-done.15.refs_5_) | copy-start | bytes 393220
  136.3 1.9 %copy-start.15 = (bf16[2,2,128,128]{3,2,1,0:T(8,128)(2,1)}, bf16[2,2,128,128]{3,2,1,0:T(8,128)(2,1)S(1)}, u32[]{:S(2)}) copy-start(bf16[2,2,128,128]{3,2,1,0:T(8,128)(2,1)S(1)} %collective-permute-done.16.refs_6_) | copy-start | bytes 393220
  138.2 0.7 copy-start.16

commit v5 on v4

--- a/solution.py
+++ b/solution.py
@@ -239,7 +239,6 @@
             side = local_id // nb
             slots.append(side * nb + lax.rem(here - (local_id - side * nb) + nb, nb))
         heads = range(spots)
-        lane_slot = lax.broadcasted_iota(jnp.int32, (1, width * BLK), 1) // BLK
 
         def tiles(h, i):
             return jnp.concatenate([cache[s, h, i] for s in slots], axis=0)
@@ -249,7 +248,8 @@
         probs = []
         for h in heads:
             raw = dot(queries[h], tiles(h, 0), NT)
-            raw = jnp.where(lane_slot < used, raw, -1e30)
+            final = jnp.where(used == width, raw[:, -BLK:], -1e30)
+            raw = jnp.concatenate([raw[:, :-BLK], final], axis=1)
             highest = jnp.max(raw, axis=1, keepdims=True)
             raised = jnp.exp2((raw - highest) * (SCALE * LOG2E))
             probs.append(raised * (1.0 / jnp.sum(raised, axis=1, keepdims=True)))

time: 143 us -> 143 us (level)
  no operation moved by 1% of the time
where the time goes in v5:
time: 143 us; the launch traced here: 142 us
  waiting for transfers between devices  60.9 us (43%)
  starting transfers between devices  49.5 us (35%)
  Pallas kernels  27.9 us (20%)
  local copies, waits for them, and re-layouts  2.3 us (2%)
    ppermute x14, starting transfers between devices, turned(): return lax.ppermute(value, 'sp', [(i, (i + steps) % n) for i in range(n)])  33.8 us
    ppermute x4, waiting for transfers between devices, swapped(): return lax.ppermute(value, 'grp', pairs + [(j, i) for i, j in pairs])  30.6 us
    ppermute x14, waiting for transfers between devices, turned(): return lax.ppermute(value, 'sp', [(i, (i + steps) % n) for i in range(n)])  22.1 us
    pallas_call x1, Pallas kernels, attention(): pl.pallas_call(functools.partial(attn_kernel, spots, nb), out_shape=[jax....  15.8 us
    all_to_all x2, starting transfers between devices, exchange(): return lax.all_to_all(value, 'sp', split_axis=0, concat_axis=0, tiled=True)  8.94 us
    all_to_all x2, waiting for transfers between devices, exchange(): return lax.all_to_all(value, 'sp', split_axis=0, concat_axis=0, tiled=True)  8.22 us
    ppermute x4, starting transfers between devices, swapped(): return lax.ppermute(value, 'grp', pairs + [(j, i) for i, j in pairs])  6.69 us
  transfers between devices with their start and end apart: 20, of which 11 were waited for; matrix products, arithmetic and copies ran while one was open for 0% of the time, Pallas kernels for 5%

profile of v5, /device:TPU:29, one launch (start us, length us, event | category | flops | bytes accessed | tf_op | source)
XLA Modules:
  0.0 141.7 jit_solution(13397547565409399350)
XLA Ops:
  0.6 2.2 %pack.1 = (bf16[2,2,128,128]{3,2,1,0:T(8,128)(2,1)}, bf16[2,2,128,128]{3,2,1,0:T(8,128)(2,1)}, bf16[2,2,128,128]{3,2,1,0:T(8,128)(2,1)}, bf16[2,2,128,128]{3,2,1...) custom-call(bf16[128,2048]{1,0:T(8,128)(2,1)} %first.1, ...), custom_call_target="tpu_custom_call" | custom-call | tf_op jit(solution)/shard_map/pack/pallas_call | solution.py:69
  2.9 7.0 %collective-permute-start = (bf16[2,2,128,128]{3,2,1,0:T(8,128)(2,1)}, bf16[2,2,128,128]{3,2,1,0:T(8,128)(2,1)S(1)}, u32[]{:S(2)}, u32[]{:S(2)}) collective-permute-start(bf16[2,2,128,128]{3,2,1,0:T(8,128)(2,1)} %get-tuple-element.46), channel_id=1, source_target_pairs={{0,4},{1,5},{2,6},{3,7},{4,0},{5,1},{6,2},{7,3},{8,12},{9,13},{10,... | collective-permute-start | bytes 393224 | tf_op jit(solution)/shard_map/ppermute | solution.py:362
  9.9 1.6 %collective-permute-start.1 = (bf16[2,2,128,128]{3,2,1,0:T(8,128)(2,1)}, bf16[2,2,128,128]{3,2,1,0:T(8,128)(2,1)S(1)}, u32[]{:S(2)}, u32[]{:S(2)}) collective-permute-start(bf16[2,2,128,128]{3,2,1,0:T(8,128)(2,1)} %get-tuple-element.47), channel_id=1, source_target_pairs={{0,3},{1,4},{2,5},{3,6},{4,7},{5,0},{6,1},{7,2},{8,11},{9,12},{10,... | collective-permute-start | bytes 393224 | tf_op jit(solution)/shard_map/ppermute | solution.py:362
  11.5 2.8 %collective-permute-start.2 = (bf16[2,2,128,128]{3,2,1,0:T(8,128)(2,1)}, bf16[2,2,128,128]{3,2,1,0:T(8,128)(2,1)S(1)}, u32[]{:S(2)}, u32[]{:S(2)}) collective-permute-start(bf16[2,2,128,128]{3,2,1,0:T(8,128)(2,1)} %get-tuple-element.48), channel_id=1, source_target_pairs={{0,5},{1,6},{2,7},{3,0},{4,1},{5,2},{6,3},{7,4},{8,13},{9,14},{10,... | collective-permute-start | bytes 393224 | tf_op jit(solution)/shard_map/ppermute | solution.py:362
  14.3 1.2 collective-permute-start.3
  15.5 2.4 %collective-permute-start.4 = (bf16[2,2,128,128]{3,2,1,0:T(8,128)(2,1)}, bf16[2,2,128,128]{3,2,1,0:T(8,128)(2,1)S(1)}, u32[]{:S(2)}, u32[]{:S(2)}) collective-permute-start(bf16[2,2,128,128]{3,2,1,0:T(8,128)(2,1)} %get-tuple-element.50), channel_id=1, source_target_pairs={{0,6},{1,7},{2,0},{3,1},{4,2},{5,3},{6,4},{7,5},{8,14},{9,15},{10,... | collective-permute-start | bytes 393224 | tf_op jit(solution)/shard_map/ppermute | solution.py:362
  17.9 0.0 collective-permute-done.refs_4_
  17.9 0.7 collective-permute-start.5
  18.6 7.8 %collective-permute-done.1.refs_3_ = bf16[2,2,128,128]{3,2,1,0:T(8,128)(2,1)S(1)} collective-permute-done((bf16[2,2,128,128]{3,2,1,0:T(8,128)(2,1)}, bf16[2,2,128,128]{3,2,1,0:T(8,128)(2,1)S(1)}, u32[]{:S(2)}, u32[]{:S(2)}) %collective-permute-start.1) | collective-permute-done | bytes 131104 | tf_op jit(solution)/shard_map/ppermute | solution.py:362
  26.5 0.0 collective-permute-start.6
  26.5 2.5 %stack.1 = bf16[8,2,2,128,128]{4,3,2,1,0:T(8,128)(2,1)} custom-call(bf16[128,2048]{1,0:T(8,128)(2,1)} %refs_0_, bf16[128,2048]{1,0:T(8,128)(2,1)} %refs_1_), custom_call_target="tpu_custom_call" | custom-call | tf_op jit(solution)/shard_map/stack/pallas_call | solution.py:162
  29.0 0.0 collective-permute-done.2.refs_5_
  29.0 0.0 copy-start.5
  29.0 0.0 collective-permute-done.3.refs_2_
  29.0 0.0 copy-start.6
  29.0 1.1 collective-permute-done.4.refs_6_
  30.1 3.2 %collective-permute-done.5.refs_1_ = bf16[2,2,128,128]{3,2,1,0:T(8,128)(2,1)S(1)} collective-permute-done((bf16[2,2,128,128]{3,2,1,0:T(8,128)(2,1)}, bf16[2,2,128,128]{3,2,1,0:T(8,128)(2,1)S(1)}, u32[]{:S(2)}, u32[]{:S(2)}) %collective-permute-start.5) | collective-permute-done | bytes 131104 | tf_op jit(solution)/shard_map/ppermute | solution.py:362
  33.3 0.7 collective-permute-done.6.refs_7_
  34.0 0.0 copy-done.3
  34.0 0.0 copy-done.4
  34.0 4.6 %all-to-all-start = ((bf16[8,2,2,128,128]{4,3,2,1,0:T(8,128)(2,1)}), bf16[8,2,2,128,128]{4,3,2,1,0:T(8,128)(2,1)S(1)}, u32[]{:S(2)}, u32[]{:S(2)}) async-start(bf16[8,2,2,128,128]{4,3,2,1,0:T(8,128)(2,1)} %stack.1), calls=%async_computation | async-start | bytes 2097152 | tf_op jit(solution)/shard_map/all_to_all | solution.py:366
  38.6 0.0 copy-done.5
  38.6 0.0 copy-done.6
  38.6 0.0 copy-done.7
  38.6 0.0 copy-done.8
  38.6 0.0 copy-done.9
  38.6 2.3 %join.1.own = bf16[8,2,2,128,128]{4,3,2,1,0:T(8,128)(2,1)} custom-call(bf16[2,2,128,128]{3,2,1,0:T(8,128)(2,1)} %get-tuple-element.45.refs_0_, bf16[2,2,128,128]{3,2,1,0:T(8,128)(2,1)} %copy-done.8, bf16[2,2,128,128]{3,2,1,0:T(8,128)(2,1)} %copy-done.6, bf16[2,2,128,128]{3,2,1,0:T(8,128)(2,1)} %copy-done.4, bf16[2,2,128,128]{3,2,1,0:T(8,128)(2,1)} %copy-done.3, ...), custom_call_target="tpu_custom_call" | custom-call | tf_op jit(solution)/shard_map/join/pallas_call | solution.py:208
  40.9 3.6 %collective-permute-start.8 = (bf16[8,2,2,128,128]{4,3,2,1,0:T(8,128)(2,1)}, bf16[8,2,2,128,128]{4,3,2,1,0:T(8,128)(2,1)S(1)}, u32[]{:S(2)}, u32[]{:S(2)}) collective-permute-start(bf16[8,2,2,128,128]{4,3,2,1,0:T(8,128)(2,1)} %join.1.own), channel_id=1, source_target_pairs={{8,16},{24,32},{40,48},{56,64},{72,80},{88,96},{104,112},{120,128}... | collective-permute-start | bytes 3145736 | tf_op jit(solution)/shard_map/ppermute | solution.py:355
  44.6 0.1 collective-permute-start.7
  44.7 14.9 %collective-permute-done.8.link = bf16[8,2,2,128,128]{4,3,2,1,0:T(8,128)(2,1)S(1)} collective-permute-done((bf16[8,2,2,128,128]{4,3,2,1,0:T(8,128)(2,1)}, bf16[8,2,2,128,128]{4,3,2,1,0:T(8,128)(2,1)S(1)}, u32[]{:S(2)}, u32[]{:S(2)}) %collective-permute-start.8) | collective-permute-done | bytes 1048608 | tf_op jit(solution)/shard_map/ppermute | solution.py:355
  59.5 0.0 collective-permute-done.7.chip
  59.5 8.2 %all-to-all-done.rows_in = bf16[8,2,2,128,128]{4,3,2,1,0:T(8,128)(2,1)S(1)} async-done(((bf16[8,2,2,128,128]{4,3,2,1,0:T(8,128)(2,1)}), bf16[8,2,2,128,128]{4,3,2,1,0:T(8,128)(2,1)S(1)}, u32[]{:S(2)}, u32[]{:S(2)}) %all-to-all-start) | async-done | bytes 1048608 | tf_op jit(solution)/shard_map/all_to_all | solution.py:366
  67.8 1.0 copy-done.2
  68.7 15.8 %attention.1 = (bf16[8,2,2,128,128]{4,3,2,1,0:T(8,128)(2,1)}, bf16[8,2,2,128,128]{4,3,2,1,0:T(8,128)(2,1)}, f32[8,2,2,128,128]{4,3,2,1,0:T(8,128)}, bf16[8,2,2,128,128]{4,3,2,1,0:T(8,128)(2,1)}) custom-call(s32[8,8]{1,0:T(8,128)} %ids.1, s32[8]{0:T(128)} %counts.1, bf16[8,2,2,128,128]{4,3,2,1,0:T(8,128)(2,1)} %collective-permute-done.7.chip, ...), custom_call_target="tpu_custom_call" | custom-call | flops 3221225472 | bytes 10485760 | tf_op jit(solution)/shard_map/attention/pallas_call | solution.py:305
  84.5 0.0 copy-start
  84.5 4.4 %all-to-all-start.1 = ((bf16[8,2,2,128,128]{4,3,2,1,0:T(8,128)(2,1)}), bf16[8,2,2,128,128]{4,3,2,1,0:T(8,128)(2,1)}, u32[]{:S(2)}, u32[]{:S(2)}) async-start(bf16[8,2,2,128,128]{4,3,2,1,0:T(8,128)(2,1)} %get-tuple-element.63), calls=%async_computation.1 | async-start | bytes 2097152 | tf_op jit(solution)/shard_map/all_to_all | solution.py:366
  88.9 0.1 collective-permute-start.9
  89.0 2.9 %collective-permute-start.10 = (bf16[8,2,2,128,128]{4,3,2,1,0:T(8,128)(2,1)}, bf16[8,2,2,128,128]{4,3,2,1,0:T(8,128)(2,1)S(1)}, u32[]{:S(2)}, u32[]{:S(2)}) collective-permute-start(bf16[8,2,2,128,128]{4,3,2,1,0:T(8,128)(2,1)} %get-tuple-element.68), channel_id=1, source_target_pairs={{8,16},{24,32},{40,48},{56,64},{72,80},{88,96},{104,112},{120,128}... | collective-permute-start | bytes 3145736 | tf_op jit(solution)/shard_map/ppermute | solution.py:355
  91.9 0.0 collective-permute-done.9.first
  91.9 15.8 %collective-permute-done.10.second = bf16[8,2,2,128,128]{4,3,2,1,0:T(8,128)(2,1)S(1)} collective-permute-done((bf16[8,2,2,128,128]{4,3,2,1,0:T(8,128)(2,1)}, bf16[8,2,2,128,128]{4,3,2,1,0:T(8,128)(2,1)S(1)}, u32[]{:S(2)}, u32[]{:S(2)}) %collective-permute-start.10) | collective-permute-done | bytes 1048608 | tf_op jit(solution)/shard_map/ppermute | solution.py:355
  107.7 0.3 settle.1
  108.1 0.6 copy-done.1
  108.7 5.4 %collective-permute-start.11 = (bf16[2,2,128,128]{3,2,1,0:T(8,128)(2,1)S(1)}, bf16[2,2,128,128]{3,2,1,0:T(8,128)(2,1)S(1)}, u32[]{:S(2)}, u32[]{:S(2)}) collective-permute-start(bf16[2,2,128,128]{3,2,1,0:T(8,128)(2,1)S(1)} %get-tuple-element.70), channel_id=1, source_target_pairs={{0,4},{1,5},{2,6},{3,7},{4,0},{5,1},{6,2},{7,3},{8,12},{9,13},{10,... | collective-permute-start | bytes 393224 | tf_op jit(solution)/shard_map/ppermute | solution.py:362
  114.1 0.3 collective-permute-start.12
  114.4 3.0 %collective-permute-start.13 = (bf16[2,2,128,128]{3,2,1,0:T(8,128)(2,1)S(1)}, bf16[2,2,128,128]{3,2,1,0:T(8,128)(2,1)S(1)}, u32[]{:S(2)}, u32[]{:S(2)}) collective-permute-start(bf16[2,2,128,128]{3,2,1,0:T(8,128)(2,1)S(1)} %get-tuple-element.72), channel_id=1, source_target_pairs={{0,3},{1,4},{2,5},{3,6},{4,7},{5,0},{6,1},{7,2},{8,11},{9,12},{10,... | collective-permute-start | bytes 393224 | tf_op jit(solution)/shard_map/ppermute | solution.py:362
  117.4 1.5 %collective-permute-start.14 = (bf16[2,2,128,128]{3,2,1,0:T(8,128)(2,1)S(1)}, bf16[2,2,128,128]{3,2,1,0:T(8,128)(2,1)S(1)}, u32[]{:S(2)}, u32[]{:S(2)}) collective-permute-start(bf16[2,2,128,128]{3,2,1,0:T(8,128)(2,1)S(1)} %get-tuple-element.73), channel_id=1, source_target_pairs={{0,6},{1,7},{2,0},{3,1},{4,2},{5,3},{6,4},{7,5},{8,14},{9,15},{10,... | collective-permute-start | bytes 393224 | tf_op jit(solution)/shard_map/ppermute | solution.py:362
  118.9 0.9 collective-permute-start.15
  119.7 6.5 %collective-permute-done.11.refs_1_ = bf16[2,2,128,128]{3,2,1,0:T(8,128)(2,1)S(1)} collective-permute-done((bf16[2,2,128,128]{3,2,1,0:T(8,128)(2,1)S(1)}, bf16[2,2,128,128]{3,2,1,0:T(8,128)(2,1)S(1)}, u32[]{:S(2)}, u32[]{:S(2)}) %collective-permute-start.11) | collective-permute-done | bytes 131104 | tf_op jit(solution)/shard_map/ppermute | solution.py:362
  126.3 0.0 collective-permute-start.16
  126.3 0.7 collective-permute-done.12.refs_2_
  127.0 7.0 %collective-permute-start.17 = (bf16[2,2,128,128]{3,2,1,0:T(8,128)(2,1)S(1)}, bf16[2,2,128,128]{3,2,1,0:T(8,128)(2,1)S(1)}, u32[]{:S(2)}, u32[]{:S(2)}) collective-permute-start(bf16[2,2,128,128]{3,2,1,0:T(8,128)(2,1)S(1)} %get-tuple-element.76), channel_id=1, source_target_pairs={{0,1},{1,2},{2,3},{3,4},{4,5},{5,6},{6,7},{7,0},{8,9},{9,10},{10,1... | collective-permute-start | bytes 393224 | tf_op jit(solution)/shard_map/ppermute | solution.py:362
  134.0 0.0 all-to-all-done.1.value
  134.0 2.5 %unstack.1 = (bf16[128,2048]{1,0:T(8,128)(2,1)}, bf16[128,2048]{1,0:T(8,128)(2,1)}) custom-call(bf16[8,2,2,128,128]{4,3,2,1,0:T(8,128)(2,1)} %all-to-all-done.1.value), custom_call_target="tpu_custom_call" | custom-call | tf_op jit(solution)/shard_map/unstack/pallas_call | solution.py:189
  136.5 0.0 collective-permute-done.13.refs_3_
  136.5 0.0 copy-start.12
  136.5 0.0 collective-permute-done.14.refs_4_
  136.5 0.0 collective-permute-done.15.refs_5_
  136.6 0.1 collective-permute-done.16.refs_6_
  136.7 1.9 %collective-permute-done.17.refs_7_ = bf16[2,2,128,128]{3,2,1,0:T(8,128)(2,1)S(1)} collective-permute-done((bf16[2,2,128,128]{3,2,1,0:T(8,128)(2,1)S(1)}, bf16[2,2,128,128]{3,2,1,0:T(8,128)(2,1)S(1)}, u32[]{:S(2)}, u32[]{:S(2)}) %collective-permute-start.17) | collective-permute-done | bytes 131104 | tf_op jit(solution)/shard_map/ppermute | solution.py:362
  138.6 0.0 copy-done.13
  138.6 0.0 copy-done.14
  138.6 0.0 copy-done.15
  138.6 0.6 copy-done.16
  139.2 2.3 %unpack.1 = (bf16[128,2048]{1,0:T(8,128)(2,1)}, bf16[128,2048]{1,0:T(8,128)(2,1)}) custom-call(bf16[2,2,128,128]{3,2,1,0:T(8,128)(2,1)} %copy-done.1, bf16[2,2,128,128]{3,2,1,0:T(8,128)(2,1)} %copy-done.10, bf16[2,2,128,128]{3,2,1,0:T(8,128)(2,1)} %copy-done.11, bf16[2,2,128,128]{3,2,1,0:T(8,128)(2,1)} %copy-done.12, bf16[2,2,128,128]{3,2,1,0:T(8,128)(2,1)} %copy-done.13, ...), custom_call_target="tpu_custom_call" | custom-call | tf_op jit(solution)/shard_map/unpack/pallas_call | solution.py:110
  (19 shorter events, 0.0 us)
Async XLA Ops:
  2.9 15.1 %collective-permute-start = (bf16[2,2,128,128]{3,2,1,0:T(8,128)(2,1)}, bf16[2,2,128,128]{3,2,1,0:T(8,128)(2,1)S(1)}, u32[]{:S(2)}, u32[]{:S(2)}) collective-permute-start(bf16[2,2,128,128]{3,2,1,0:T(8,128)(2,1)} %get-tuple-element.46), channel_id=1, source_target_pairs={{0,4},{1,5},{2,6},{3,7},{4,0},{5,1},{6,2},{7,3},{8,12},{9,13},{10,... | collective-permute-start | bytes 393224 | tf_op jit(solution)/shard_map/ppermute | solution.py:362
  9.9 16.6 %collective-permute-start.1 = (bf16[2,2,128,128]{3,2,1,0:T(8,128)(2,1)}, bf16[2,2,128,128]{3,2,1,0:T(8,128)(2,1)S(1)}, u32[]{:S(2)}, u32[]{:S(2)}) collective-permute-start(bf16[2,2,128,128]{3,2,1,0:T(8,128)(2,1)} %get-tuple-element.47), channel_id=1, source_target_pairs={{0,3},{1,4},{2,5},{3,6},{4,7},{5,0},{6,1},{7,2},{8,11},{9,12},{10,... | collective-permute-start | bytes 393224 | tf_op jit(solution)/shard_map/ppermute | solution.py:362
  11.5 17.5 %collective-permute-start.2 = (bf16[2,2,128,128]{3,2,1,0:T(8,128)(2,1)}, bf16[2,2,128,128]{3,2,1,0:T(8,128)(2,1)S(1)}, u32[]{:S(2)}, u32[]{:S(2)}) collective-permute-start(bf16[2,2,128,128]{3,2,1,0:T(8,128)(2,1)} %get-tuple-element.48), channel_id=1, source_target_pairs={{0,5},{1,6},{2,7},{3,0},{4,1},{5,2},{6,3},{7,4},{8,13},{9,14},{10,... | collective-permute-start | bytes 393224 | tf_op jit(solution)/shard_map/ppermute | solution.py:362
  14.3 14.7 %collective-permute-start.3 = (bf16[2,2,128,128]{3,2,1,0:T(8,128)(2,1)}, bf16[2,2,128,128]{3,2,1,0:T(8,128)(2,1)S(1)}, u32[]{:S(2)}, u32[]{:S(2)}) collective-permute-start(bf16[2,2,128,128]{3,2,1,0:T(8,128)(2,1)} %get-tuple-element.49), channel_id=1, source_target_pairs={{0,2},{1,3},{2,4},{3,5},{4,6},{5,7},{6,0},{7,1},{8,10},{9,11},{10,... | collective-permute-start | bytes 393224 | tf_op jit(solution)/shard_map/ppermute | solution.py:362
  15.5 14.6 %collective-permute-start.4 = (bf16[2,2,128,128]{3,2,1,0:T(8,128)(2,1)}, bf16[2,2,128,128]{3,2,1,0:T(8,128)(2,1)S(1)}, u32[]{:S(2)}, u32[]{:S(2)}) collective-permute-start(bf16[2,2,128,128]{3,2,1,0:T(8,128)(2,1)} %get-tuple-element.50), channel_id=1, source_target_pairs={{0,6},{1,7},{2,0},{3,1},{4,2},{5,3},{6,4},{7,5},{8,14},{9,15},{10,... | collective-permute-start | bytes 393224 | tf_op jit(solution)/shard_map/ppermute | solution.py:362
  17.9 16.1 %copy-start.3 = (bf16[2,2,128,128]{3,2,1,0:T(8,128)(2,1)}, bf16[2,2,128,128]{3,2,1,0:T(8,128)(2,1)S(1)}, u32[]{:S(2)}) copy-start(bf16[2,2,128,128]{3,2,1,0:T(8,128)(2,1)S(1)} %collective-permute-done.refs_4_) | copy-start | bytes 393220
  17.9 15.4 %collective-permute-start.5 = (bf16[2,2,128,128]{3,2,1,0:T(8,128)(2,1)}, bf16[2,2,128,128]{3,2,1,0:T(8,128)(2,1)S(1)}, u32[]{:S(2)}, u32[]{:S(2)}) collective-permute-start(bf16[2,2,128,128]{3,2,1,0:T(8,128)(2,1)} %get-tuple-element.51), channel_id=1, source_target_pairs={{0,1},{1,2},{2,3},{3,4},{4,5},{5,6},{6,7},{7,0},{8,9},{9,10},{10,1... | collective-permute-start | bytes 393224 | tf_op jit(solution)/shard_map/ppermute | solution.py:362
  26.5 7.5 %copy-start.4 = (bf16[2,2,128,128]{3,2,1,0:T(8,128)(2,1)}, bf16[2,2,128,128]{3,2,1,0:T(8,128)(2,1)S(1)}, u32[]{:S(2)}) copy-start(bf16[2,2,128,128]{3,2,1,0:T(8,128)(2,1)S(1)} %collective-permute-done.1.refs_3_) | copy-start | bytes 393220
  26.5 7.5 %collective-permute-start.6 = (bf16[2,2,128,128]{3,2,1,0:T(8,128)(2,1)}, bf16[2,2,128,128]{3,2,1,0:T(8,128)(2,1)S(1)}, u32[]{:S(2)}, u32[]{:S(2)}) collective-permute-start(bf16[2,2,128,128]{3,2,1,0:T(8,128)(2,1)} %get-tuple-element.52), channel_id=1, source_target_pairs={{0,7},{1,0},{2,1},{3,2},{4,3},{5,4},{6,5},{7,6},{8,15},{9,8},{10,9... | collective-permute-start | bytes 393224 | tf_op jit(solution)/shard_map/ppermute | solution.py:362
  29.0 9.6 %copy-start.5 = (bf16[2,2,128,128]{3,2,1,0:T(8,128)(2,1)}, bf16[2,2,128,128]{3,2,1,0:T(8,128)(2,1)S(1)}, u32[]{:S(2)}) copy-start(bf16[2,2,128,128]{3,2,1,0:T(8,128)(2,1)S(1)} %collective-permute-done.2.refs_5_) | copy-start | bytes 393220
  29.0 9.5 %copy-start.6 = (bf16[2,2,128,128]{3,2,1,0:T(8,128)(2,1)}, bf16[2,2,128,128]{3,2,1,0:T(8,128)(2,1)S(1)}, u32[]{:S(2)}) copy-start(bf16[2,2,128,128]{3,2,1,0:T(8,128)(2,1)S(1)} %collective-permute-done.3.refs_2_) | copy-start | bytes 393220
  30.1 8.5 %copy-start.7 = (bf16[2,2,128,128]{3,2,1,0:T(8,128)(2,1)}, bf16[2,2,128,128]{3,2,1,0:T(8,128)(2,1)S(1)}, u32[]{:S(2)}) copy-start(bf16[2,2,128,128]{3,2,1,0:T(8,128)(2,1)S(1)} %collective-permute-done.4.refs_6_) | copy-start | bytes 393220
  33.3 5.3 %copy-start.8 = (bf16[2,2,128,128]{3,2,1,0:T(8,128)(2,1)}, bf16[2,2,128,128]{3,2,1,0:T(8,128)(2,1)S(1)}, u32[]{:S(2)}) copy-start(bf16[2,2,128,128]{3,2,1,0:T(8,128)(2,1)S(1)} %collective-permute-done.5.refs_1_) | copy-start | bytes 393220
  34.0 4.6 %copy-start.9 = (bf16[2,2,128,128]{3,2,1,0:T(8,128)(2,1)}, bf16[2,2,128,128]{3,2,1,0:T(8,128)(2,1)S(1)}, u32[]{:S(2)}) copy-start(bf16[2,2,128,128]{3,2,1,0:T(8,128)(2,1)S(1)} %collective-permute-done.6.refs_7_) | copy-start | bytes 393220
  34.0 33.8 %all-to-all-start = ((bf16[8,2,2,128,128]{4,3,2,1,0:T(8,128)(2,1)}), bf16[8,2,2,128,128]{4,3,2,1,0:T(8,128)(2,1)S(1)}, u32[]{:S(2)}, u32[]{:S(2)}) async-start(bf16[8,2,2,128,128]{4,3,2,1,0:T(8,128)(2,1)} %stack.1), calls=%async_computation | async-start | bytes 2097152 | tf_op jit(solution)/shard_map/all_to_all | solution.py:366
  40.9 18.6 %collective-permute-start.8 = (bf16[8,2,2,128,128]{4,3,2,1,0:T(8,128)(2,1)}, bf16[8,2,2,128,128]{4,3,2,1,0:T(8,128)(2,1)S(1)}, u32[]{:S(2)}, u32[]{:S(2)}) collective-permute-start(bf16[8,2,2,128,128]{4,3,2,1,0:T(8,128)(2,1)} %join.1.own), channel_id=1, source_target_pairs={{8,16},{24,32},{40,48},{56,64},{72,80},{88,96},{104,112},{120,128}... | collective-permute-start | bytes 3145736 | tf_op jit(solution)/shard_map/ppermute | solution.py:355
  44.6 15.0 %collective-permute-start.7 = (bf16[8,2,2,128,128]{4,3,2,1,0:T(8,128)(2,1)}, bf16[8,2,2,128,128]{4,3,2,1,0:T(8,128)(2,1)}, u32[]{:S(2)}, u32[]{:S(2)}) collective-permute-start(bf16[8,2,2,128,128]{4,3,2,1,0:T(8,128)(2,1)} %join.1.own), channel_id=1, source_target_pairs={{0,8},{16,24},{32,40},{48,56},{64,72},{80,88},{96,104},{112,120},{... | collective-permute-start | bytes 3145736 | tf_op jit(solution)/shard_map/ppermute | solution.py:355
  59.5 8.2 %copy-start.17 = (bf16[8,2,2,128,128]{4,3,2,1,0:T(8,128)(2,1)}, bf16[8,2,2,128,128]{4,3,2,1,0:T(8,128)(2,1)S(1)}, u32[]{:S(2)}) copy-start(bf16[8,2,2,128,128]{4,3,2,1,0:T(8,128)(2,1)S(1)} %collective-permute-done.8.link) | copy-start | bytes 3145732
  67.8 1.0 copy-start.2
  84.5 23.2 %copy-start = (f32[8,2,2,128,128]{4,3,2,1,0:T(8,128)S(1)}, f32[8,2,2,128,128]{4,3,2,1,0:T(8,128)}, u32[]{:S(2)}) copy-start(f32[8,2,2,128,128]{4,3,2,1,0:T(8,128)} %get-tuple-element.66.grad_own) | copy-start | bytes 6291460
  84.5 49.5 %all-to-all-start.1 = ((bf16[8,2,2,128,128]{4,3,2,1,0:T(8,128)(2,1)}), bf16[8,2,2,128,128]{4,3,2,1,0:T(8,128)(2,1)}, u32[]{:S(2)}, u32[]{:S(2)}) async-start(bf16[8,2,2,128,128]{4,3,2,1,0:T(8,128)(2,1)} %get-tuple-element.63), calls=%async_computation.1 | async-start | bytes 2097152 | tf_op jit(solution)/shard_map/all_to_all | solution.py:366
  88.9 3.0 %collective-permute-start.9 = (bf16[8,2,2,128,128]{4,3,2,1,0:T(8,128)(2,1)}, bf16[8,2,2,128,128]{4,3,2,1,0:T(8,128)(2,1)S(1)}, u32[]{:S(2)}, u32[]{:S(2)}) collective-permute-start(bf16[8,2,2,128,128]{4,3,2,1,0:T(8,128)(2,1)} %get-tuple-element.67), channel_id=1, source_target_pairs={{0,8},{16,24},{32,40},{48,56},{64,72},{80,88},{96,104},{112,120},{... | collective-permute-start | bytes 3145736 | tf_op jit(solution)/shard_map/ppermute | solution.py:355
  89.0 18.7 %collective-permute-start.10 = (bf16[8,2,2,128,128]{4,3,2,1,0:T(8,128)(2,1)}, bf16[8,2,2,128,128]{4,3,2,1,0:T(8,128)(2,1)S(1)}, u32[]{:S(2)}, u32[]{:S(2)}) collective-permute-start(bf16[8,2,2,128,128]{4,3,2,1,0:T(8,128)(2,1)} %get-tuple-element.68), channel_id=1, source_target_pairs={{8,16},{24,32},{40,48},{56,64},{72,80},{88,96},{104,112},{120,128}... | collective-permute-start | bytes 3145736 | tf_op jit(solution)/shard_map/ppermute | solution.py:355
  108.1 0.7 copy-start.1
  108.7 17.6 %collective-permute-start.11 = (bf16[2,2,128,128]{3,2,1,0:T(8,128)(2,1)S(1)}, bf16[2,2,128,128]{3,2,1,0:T(8,128)(2,1)S(1)}, u32[]{:S(2)}, u32[]{:S(2)}) collective-permute-start(bf16[2,2,128,128]{3,2,1,0:T(8,128)(2,1)S(1)} %get-tuple-element.70), channel_id=1, source_target_pairs={{0,4},{1,5},{2,6},{3,7},{4,0},{5,1},{6,2},{7,3},{8,12},{9,13},{10,... | collective-permute-start | bytes 393224 | tf_op jit(solution)/shard_map/ppermute | solution.py:362
  114.1 12.9 %collective-permute-start.12 = (bf16[2,2,128,128]{3,2,1,0:T(8,128)(2,1)S(1)}, bf16[2,2,128,128]{3,2,1,0:T(8,128)(2,1)S(1)}, u32[]{:S(2)}, u32[]{:S(2)}) collective-permute-start(bf16[2,2,128,128]{3,2,1,0:T(8,128)(2,1)S(1)} %get-tuple-element.71), channel_id=1, source_target_pairs={{0,5},{1,6},{2,7},{3,0},{4,1},{5,2},{6,3},{7,4},{8,13},{9,14},{10,... | collective-permute-start | bytes 393224 | tf_op jit(solution)/shard_map/ppermute | solution.py:362
  114.4 22.1 %collective-permute-start.13 = (bf16[2,2,128,128]{3,2,1,0:T(8,128)(2,1)S(1)}, bf16[2,2,128,128]{3,2,1,0:T(8,128)(2,1)S(1)}, u32[]{:S(2)}, u32[]{:S(2)}) collective-permute-start(bf16[2,2,128,128]{3,2,1,0:T(8,128)(2,1)S(1)} %get-tuple-element.72), channel_id=1, source_target_pairs={{0,3},{1,4},{2,5},{3,6},{4,7},{5,0},{6,1},{7,2},{8,11},{9,12},{10,... | collective-permute-start | bytes 393224 | tf_op jit(solution)/shard_map/ppermute | solution.py:362
  117.4 19.1 %collective-permute-start.14 = (bf16[2,2,128,128]{3,2,1,0:T(8,128)(2,1)S(1)}, bf16[2,2,128,128]{3,2,1,0:T(8,128)(2,1)S(1)}, u32[]{:S(2)}, u32[]{:S(2)}) collective-permute-start(bf16[2,2,128,128]{3,2,1,0:T(8,128)(2,1)S(1)} %get-tuple-element.73), channel_id=1, source_target_pairs={{0,6},{1,7},{2,0},{3,1},{4,2},{5,3},{6,4},{7,5},{8,14},{9,15},{10,... | collective-permute-start | bytes 393224 | tf_op jit(solution)/shard_map/ppermute | solution.py:362
  118.9 17.7 %collective-permute-start.15 = (bf16[2,2,128,128]{3,2,1,0:T(8,128)(2,1)S(1)}, bf16[2,2,128,128]{3,2,1,0:T(8,128)(2,1)S(1)}, u32[]{:S(2)}, u32[]{:S(2)}) collective-permute-start(bf16[2,2,128,128]{3,2,1,0:T(8,128)(2,1)S(1)} %get-tuple-element.74), channel_id=1, source_target_pairs={{0,2},{1,3},{2,4},{3,5},{4,6},{5,7},{6,0},{7,1},{8,10},{9,11},{10,... | collective-permute-start | bytes 393224 | tf_op jit(solution)/shard_map/ppermute | solution.py:362
  126.3 12.3 %copy-start.10 = (bf16[2,2,128,128]{3,2,1,0:T(8,128)(2,1)}, bf16[2,2,128,128]{3,2,1,0:T(8,128)(2,1)S(1)}, u32[]{:S(2)}) copy-start(bf16[2,2,128,128]{3,2,1,0:T(8,128)(2,1)S(1)} %collective-permute-done.11.refs_1_) | copy-start | bytes 393220
  126.3 10.4 %collective-permute-start.16 = (bf16[2,2,128,128]{3,2,1,0:T(8,128)(2,1)S(1)}, bf16[2,2,128,128]{3,2,1,0:T(8,128)(2,1)S(1)}, u32[]{:S(2)}, u32[]{:S(2)}) collective-permute-start(bf16[2,2,128,128]{3,2,1,0:T(8,128)(2,1)S(1)} %get-tuple-element.75), channel_id=1, source_target_pairs={{0,7},{1,0},{2,1},{3,2},{4,3},{5,4},{6,5},{7,6},{8,15},{9,8},{10,9... | collective-permute-start | bytes 393224 | tf_op jit(solution)/shard_map/ppermute | solution.py:362
  127.0 11.6 %copy-start.11 = (bf16[2,2,128,128]{3,2,1,0:T(8,128)(2,1)}, bf16[2,2,128,128]{3,2,1,0:T(8,128)(2,1)S(1)}, u32[]{:S(2)}) copy-start(bf16[2,2,128,128]{3,2,1,0:T(8,128)(2,1)S(1)} %collective-permute-done.12.refs_2_) | copy-start | bytes 393220
  127.0 11.6 %collective-permute-start.17 = (bf16[2,2,128,128]{3,2,1,0:T(8,128)(2,1)S(1)}, bf16[2,2,128,128]{3,2,1,0:T(8,128)(2,1)S(1)}, u32[]{:S(2)}, u32[]{:S(2)}) collective-permute-start(bf16[2,2,128,128]{3,2,1,0:T(8,128)(2,1)S(1)} %get-tuple-element.76), channel_id=1, source_target_pairs={{0,1},{1,2},{2,3},{3,4},{4,5},{5,6},{6,7},{7,0},{8,9},{9,10},{10,1... | collective-permute-start | bytes 393224 | tf_op jit(solution)/shard_map/ppermute | solution.py:362
  136.5 2.1 %copy-start.12 = (bf16[2,2,128,128]{3,2,1,0:T(8,128)(2,1)}, bf16[2,2,128,128]{3,2,1,0:T(8,128)(2,1)S(1)}, u32[]{:S(2)}) copy-start(bf16[2,2,128,128]{3,2,1,0:T(8,128)(2,1)S(1)} %collective-permute-done.13.refs_3_) | copy-start | bytes 393220
  136.5 2.1 %copy-start.13 = (bf16[2,2,128,128]{3,2,1,0:T(8,128)(2,1)}, bf16[2,2,128,128]{3,2,1,0:T(8,128)(2,1)S(1)}, u32[]{:S(2)}) copy-start(bf16[2,2,128,128]{3,2,1,0:T(8,128)(2,1)S(1)} %collective-permute-done.14.refs_4_) | copy-start | bytes 393220
  136.5 2.1 %copy-start.14 = (bf16[2,2,128,128]{3,2,1,0:T(8,128)(2,1)}, bf16[2,2,128,128]{3,2,1,0:T(8,128)(2,1)S(1)}, u32[]{:S(2)}) copy-start(bf16[2,2,128,128]{3,2,1,0:T(8,128)(2,1)S(1)} %collective-permute-done.15.refs_5_) | copy-start | bytes 393220
  136.7 1.9 %copy-start.15 = (bf16[2,2,128,128]{3,2,1,0:T(8,128)(2,1)}, bf16[2,2,128,128]{3,2,1,0:T(8,128)(2,1)S(1)}, u32[]{:S(2)}) copy-start(bf16[2,2,128,128]{3,2,1,0:T(8,128)(2,1)S(1)} %collective-permute-done.16.refs_6_) | copy-start | bytes 393220
  138.6 0.7 copy-start.16
